TPU v7x, 256 devices: a whole 4x4x8 slice. The times are simulated.
256 devices in a mesh: mem: 2 (over z_hi), lat: 32 (over y, x, core), lon: 4 (over z_lo).
Axes of the slice: x: 4, y: 4, z: 8 (z_hi: 2, z_lo: 4; z = z_hi * 4 + z_lo), core: 2. Of those that a mesh axis runs over, the one named last changes fastest.
Arguments:
- ensemble: bfloat16 [32, 256, 256, 128], P('mem', 'lat', 'lon'), may hold values from -6 to 6
- w_conv1: bfloat16 [3, 3, 128, 128], replicated, may hold values from -0.1875 to 0.1875
- bias1: float32 [128], replicated, may hold values from -3 to 3
- gain: float32 [128], replicated, may hold values from 0.1 to 1.9
- w_query: bfloat16 [128, 128], replicated, as said below
- w_key: bfloat16 [128, 128], replicated, may hold values from -0.5 to 0.5
- w_value: bfloat16 [128, 128], replicated, may hold values from -0.5 to 0.5
- w_out: bfloat16 [128, 128], replicated, may hold values from -0.5 to 0.5
- w_conv2: bfloat16 [3, 3, 128, 128], replicated, may hold values from -0.1875 to 0.1875
- bias2: float32 [128], replicated, may hold values from -3 to 3
Outputs:
- refined: bfloat16 [32, 256, 256, 128], P('mem', 'lat', 'lon')
Inputs may be any that keep to these rules, and one draw needn't show every extreme that they name: `w_query`: independent normal entries of mean 0 whose standard deviation lies between 128**-0.5 and 60 * 128**-0.5, so that scores may reach several hundreds.
All inputs are finite; a program needn't handle non-finite values.
Results may differ from a plain program's by a relative error of at most 0.035.
Values may be sent and summed in bfloat16 or wider, within the bound.
No kernel may reach another device: no remote copies, remote signals or barrier semaphores. Data moves between devices by JAX's collectives and lax.ppermute only.
A program may use at most 128 MiB of HBM per device.

v0:
```python
import jax
import jax.numpy as jnp
from jax import lax
from jax.sharding import PartitionSpec as P

HEADS = 8


def extended(cells, sides, width, closed):
    for axis, dim in sides:
        count = lax.axis_size(axis)
        ends = count if closed else count - 1
        head = lax.slice_in_dim(cells, 0, width, axis=dim)
        tail = lax.slice_in_dim(cells, cells.shape[dim] - width, cells.shape[dim], axis=dim)
        cells = jnp.concatenate(
            [
                lax.ppermute(tail, axis, [(i, (i + 1) % count) for i in range(ends)]),
                cells,
                lax.ppermute(head, axis, [((i + 1) % count, i) for i in range(ends)]),
            ],
            axis=dim,
        )
    return cells


def conv_taps(padded, weights):
    height = padded.shape[1] - 2
    width = padded.shape[2] - 2
    summed = None
    for row_tap in range(3):
        for col_tap in range(3):
            window = padded[:, row_tap : row_tap + height, col_tap : col_tap + width, :]
            tap_term = jnp.einsum(
                "mrlc,cd->mrld",
                window,
                weights[row_tap, col_tap],
                preferred_element_type=jnp.float32,
            )
            summed = tap_term if summed is None else summed + tap_term
    return summed


def layer_norm(hidden, gain):
    values = hidden.astype(jnp.float32)
    centre = jnp.mean(values, axis=-1, keepdims=True)
    spread = jnp.mean((values - centre) ** 2, axis=-1, keepdims=True)
    return ((values - centre) * lax.rsqrt(spread + 1e-05) * gain).astype(jnp.bfloat16)


def mix_members(normed, w_query, w_key, w_value, w_out):
    members, points, width = normed.shape
    head_dim = width // HEADS
    query = jnp.einsum("mic,cd->mid", normed, w_query, preferred_element_type=jnp.float32).astype(
        jnp.bfloat16
    )
    key_proj = jnp.einsum("mic,cd->mid", normed, w_key, preferred_element_type=jnp.float32).astype(
        jnp.bfloat16
    )
    value_proj = jnp.einsum(
        "mic,cd->mid", normed, w_value, preferred_element_type=jnp.float32
    ).astype(jnp.bfloat16)
    block_len = 1
    for guess in range(min(points, 64), 0, -1):
        block_len = guess
        break
    block_count = points // block_len
    scale = 1.0 / jnp.sqrt(jnp.float32(head_dim))

    def one_block(offset):
        q_block = lax.dynamic_slice_in_dim(query, offset, block_len, 1).reshape(
            members, block_len, HEADS, head_dim
        )
        k_block = lax.dynamic_slice_in_dim(key_proj, offset, block_len, 1).reshape(
            members, block_len, HEADS, head_dim
        )
        v_block = lax.dynamic_slice_in_dim(value_proj, offset, block_len, 1).reshape(
            members, block_len, HEADS, head_dim
        )
        scores = (
            jnp.einsum("mbhd,nbhd->bhmn", q_block, k_block, preferred_element_type=jnp.float32)
            * scale
        )
        probs = jax.nn.softmax(scores, axis=-1).astype(jnp.bfloat16)
        context = jnp.einsum(
            "bhmn,nbhd->mbhd", probs, v_block, preferred_element_type=jnp.float32
        ).astype(jnp.bfloat16)
        context = context.reshape(members, block_len, width)
        return jnp.einsum("mbc,cd->mbd", context, w_out, preferred_element_type=jnp.float32).astype(
            jnp.bfloat16
        )

    blocks = lax.map(one_block, jnp.arange(block_count, dtype=jnp.int32) * block_len)
    return jnp.moveaxis(blocks, 0, 1).reshape(members, points, width)


def attend(normed, w_query, w_key, w_value, w_out):
    members_dev, height, width, channels = normed.shape
    groups = lax.axis_size("mem")
    grouped = normed.reshape(members_dev, groups, height * width // groups, channels)
    attended = mix_members(
        lax.all_to_all(grouped, "mem", split_axis=1, concat_axis=0, tiled=True)[:, 0],
        w_query,
        w_key,
        w_value,
        w_out,
    )
    returned = lax.all_to_all(attended[:, None], "mem", split_axis=0, concat_axis=1, tiled=True)
    return returned.reshape(members_dev, height, width, channels)


def first_half(padded, w_conv1, bias1, gain, w_query, w_key, w_value, w_out):
    hidden = jax.nn.gelu(conv_taps(padded, w_conv1) + bias1, approximate=False).astype(jnp.bfloat16)
    normed = layer_norm(hidden, gain)
    attended = attend(normed, w_query, w_key, w_value, w_out)
    return (hidden.astype(jnp.float32) + attended.astype(jnp.float32)).astype(jnp.bfloat16)


def shards(ensemble, w_conv1, bias1, gain, w_query, w_key, w_value, w_out, w_conv2, bias2):
    lat_rims = extended(ensemble, (("lat", 1),), 1, False)
    padded = extended(lat_rims, (("lon", 2),), 1, True)
    centre = first_half(padded, w_conv1, bias1, gain, w_query, w_key, w_value, w_out)
    second_rims = extended(centre, (("lat", 1),), 1, False)
    spread = extended(second_rims, (("lon", 2),), 1, True)
    refined = centre.astype(jnp.float32) + conv_taps(spread, w_conv2) + bias2
    return refined.astype(jnp.bfloat16)


def solution(mesh):
    return jax.shard_map(
        shards,
        mesh=mesh,
        in_specs=(P("mem", "lat", "lon", None), P(), P(), P(), P(), P(), P(), P(), P(), P()),
        out_specs=P("mem", "lat", "lon", None),
        check_vma=False,
    )
```

profile of v0, /device:TPU:1, one launch (start us, length us, event | category | flops | bytes accessed | tf_op | source)
XLA Modules:
  0.0 327.1 jit_solution(4811767638121928229)
XLA Ops:
  1.2 4.5 %collective-permute-start = (bf16[16,1,64,128]{3,2,1,0:T(8,128)(2,1)S(1)}, bf16[16,1,64,128]{3,2,1,0:T(8,128)(2,1)S(1)}, u32[]{:S(2)}, u32[]{:S(2)}) collective-permute-start(bf16[16,1,64,128]{3,2,1,0:T(8,128)(2,1)S(1)} %get-tuple-element.90), channel_id=1, source_target_pairs={{0,4},{4,8},{8,12},{12,16},{16,20},{20,24},{24,28},{28,32},{32,36}... | collective-permute-start | bytes 786440 | tf_op jit(solution)/shard_map/ppermute | solution.py:17
  10.3 3.4 %collective-permute-done.1 = bf16[16,1,64,128]{3,2,1,0:T(8,128)(2,1)S(1)} collective-permute-done((bf16[16,1,64,128]{3,2,1,0:T(8,128)(2,1)S(1)}, bf16[16,1,64,128]{3,2,1,0:T(8,128)(2,1)S(1)}, u32[]{:S(2)}, u32[]{:S(2)}) %collective-permute-start.1) | collective-permute-done | bytes 262176 | tf_op jit(solution)/shard_map/ppermute | solution.py:19
  13.9 4.4 %collective-permute-start.3 = (bf16[16,10,1,128]{3,2,1,0:T(2,128)(2,1)S(1)}, bf16[16,10,1,128]{3,2,1,0:T(2,128)(2,1)S(1)}, u32[]{:S(2)}, u32[]{:S(2)}) collective-permute-start(bf16[16,10,1,128]{3,2,1,0:T(2,128)(2,1)S(1)} %get-tuple-element.86), channel_id=1, source_target_pairs={{1,0},{2,1},{3,2},{0,3},{5,4},{6,5},{7,6},{4,7},{9,8},{10,9},{11,1... | collective-permute-start | bytes 122888 | tf_op jit(solution)/shard_map/ppermute | solution.py:19
  23.7 2.7 fusion.46
  31.7 2.7 fusion.55
  34.4 2.7 fusion.73
  37.0 15.2 %convert_reduce_fusion = (f32[16,8,64]{2,1,0:T(8,128)S(1)}, bf16[16,8,64,128]{3,2,1,0:T(8,128)(2,1)S(1)}) fusion(f32[128]{0:T(128)S(1)} %copy-done.12, bf16[3,3,128,128]{3,2,1,0:T(8,128)(2,1)S(1)} %copy-done.7, bf16[16,10,1,128]{3,2,1,0:T(2,128)(2,1)S(1)} %collective-permute-done.3, bf16[16,10,64,128]{3,2,1,0:T(8,128)(2,1)S(1)} %constant_dynamic-update-slice_fusion, ...), kind=kOutput, calls=%fused_computation.19 | convolution fusion | flops 352313344 | bytes 38420992 | tf_op jit(solution)/shard_map/mrlc,cd->mrld/dot_general | solution.py:33
  58.7 5.6 %all-to-all-start = ((bf16[16,2,256,128]{3,2,0,1:T(8,128)(2,1)}), bf16[16,2,256,128]{3,2,0,1:T(8,128)(2,1)S(1)}, u32[]{:S(2)}, u32[]{:S(2)}) async-start(bf16[16,2,256,128]{3,2,0,1:T(8,128)(2,1)} %copy.27), calls=%async_computation | async-start | bytes 4194304 | tf_op jit(solution)/shard_map/all_to_all | solution.py:101
  64.3 44.8 %all-to-all-done = bf16[16,2,256,128]{3,2,0,1:T(8,128)(2,1)S(1)} async-done(((bf16[16,2,256,128]{3,2,0,1:T(8,128)(2,1)}), bf16[16,2,256,128]{3,2,0,1:T(8,128)(2,1)S(1)}, u32[]{:S(2)}, u32[]{:S(2)}) %all-to-all-start) | async-done | bytes 2097184 | tf_op jit(solution)/shard_map/all_to_all | solution.py:101
  115.2 104.7 %while.10 = (s32[]{:T(128)}, bf16[4,32,64,128]{3,2,0,1:T(8,128)(2,1)}, s32[4]{0:T(128)S(1)}, bf16[32,256,128]{2,1,0:T(8,128)(2,1)}, bf16[32,256,128]{2,1,0:T(8,1...) while((s32[]{:T(128)}, ...), condition=%wide.region_5.6_spmd, body=%wide.region_2.5_spmd.sunk | while | flops 103809056 | bytes 14844571 | solution.py:92
  122.6 7.1 %fusion.154 = (f32[64,8,32]{2,1,0:T(8,128)S(1)}, f32[64,8,32,32]{2,3,1,0:T(8,128)}) fusion(bf16[32,64,8,16]{0,3,2,1:T(8,128)(2,1)S(1)} %bitcast.204, bf16[32,64,8,16]{0,3,2,1:T(8,128)(2,1)} %bitcast.205), kind=kOutput, calls=%fused_computation.163.clone.1 | convolution fusion | flops 18350112 | bytes 3211264 | tf_op jit(solution)/shard_map/while/body/eval_jaxpr/sub | solution.py:83
  132.2 6.0 %fusion.155 = bf16[64,8,16,32]{3,2,1,0:T(8,128)(2,1)} fusion(bf16[32,64,8,16]{0,3,2,1:T(8,128)(2,1)S(1)} %bitcast.206, f32[64,8,32,32]{2,3,1,0:T(8,128)} %get-tuple-element.143, f32[64,8,32]{2,1,0:T(8,128)S(1)} %get-tuple-element.144), kind=kOutput, calls=%fused_computation.7.clone.1 | convolution fusion | flops 18087936 | bytes 3211264 | tf_op jit(solution)/shard_map/while/body/eval_jaxpr/bhmn,nbhd->mbhd/dot_general | solution.py:84
  148.8 7.1 %fusion.154 = (f32[64,8,32]{2,1,0:T(8,128)S(1)}, f32[64,8,32,32]{2,3,1,0:T(8,128)}) fusion(bf16[32,64,8,16]{0,3,2,1:T(8,128)(2,1)S(1)} %bitcast.204, bf16[32,64,8,16]{0,3,2,1:T(8,128)(2,1)} %bitcast.205), kind=kOutput, calls=%fused_computation.163.clone.1 | convolution fusion | flops 18350112 | bytes 3211264 | tf_op jit(solution)/shard_map/while/body/eval_jaxpr/sub | solution.py:83
  158.4 6.0 %fusion.155 = bf16[64,8,16,32]{3,2,1,0:T(8,128)(2,1)} fusion(bf16[32,64,8,16]{0,3,2,1:T(8,128)(2,1)S(1)} %bitcast.206, f32[64,8,32,32]{2,3,1,0:T(8,128)} %get-tuple-element.143, f32[64,8,32]{2,1,0:T(8,128)S(1)} %get-tuple-element.144), kind=kOutput, calls=%fused_computation.7.clone.1 | convolution fusion | flops 18087936 | bytes 3211264 | tf_op jit(solution)/shard_map/while/body/eval_jaxpr/bhmn,nbhd->mbhd/dot_general | solution.py:84
  175.0 7.1 %fusion.154 = (f32[64,8,32]{2,1,0:T(8,128)S(1)}, f32[64,8,32,32]{2,3,1,0:T(8,128)}) fusion(bf16[32,64,8,16]{0,3,2,1:T(8,128)(2,1)S(1)} %bitcast.204, bf16[32,64,8,16]{0,3,2,1:T(8,128)(2,1)} %bitcast.205), kind=kOutput, calls=%fused_computation.163.clone.1 | convolution fusion | flops 18350112 | bytes 3211264 | tf_op jit(solution)/shard_map/while/body/eval_jaxpr/sub | solution.py:83
  184.5 6.0 %fusion.155 = bf16[64,8,16,32]{3,2,1,0:T(8,128)(2,1)} fusion(bf16[32,64,8,16]{0,3,2,1:T(8,128)(2,1)S(1)} %bitcast.206, f32[64,8,32,32]{2,3,1,0:T(8,128)} %get-tuple-element.143, f32[64,8,32]{2,1,0:T(8,128)S(1)} %get-tuple-element.144), kind=kOutput, calls=%fused_computation.7.clone.1 | convolution fusion | flops 18087936 | bytes 3211264 | tf_op jit(solution)/shard_map/while/body/eval_jaxpr/bhmn,nbhd->mbhd/dot_general | solution.py:84
  201.2 7.1 %fusion.154 = (f32[64,8,32]{2,1,0:T(8,128)S(1)}, f32[64,8,32,32]{2,3,1,0:T(8,128)}) fusion(bf16[32,64,8,16]{0,3,2,1:T(8,128)(2,1)S(1)} %bitcast.204, bf16[32,64,8,16]{0,3,2,1:T(8,128)(2,1)} %bitcast.205), kind=kOutput, calls=%fused_computation.163.clone.1 | convolution fusion | flops 18350112 | bytes 3211264 | tf_op jit(solution)/shard_map/while/body/eval_jaxpr/sub | solution.py:83
  210.7 6.0 %fusion.155 = bf16[64,8,16,32]{3,2,1,0:T(8,128)(2,1)} fusion(bf16[32,64,8,16]{0,3,2,1:T(8,128)(2,1)S(1)} %bitcast.206, f32[64,8,32,32]{2,3,1,0:T(8,128)} %get-tuple-element.143, f32[64,8,32]{2,1,0:T(8,128)S(1)} %get-tuple-element.144), kind=kOutput, calls=%fused_computation.7.clone.1 | convolution fusion | flops 18087936 | bytes 3211264 | tf_op jit(solution)/shard_map/while/body/eval_jaxpr/bhmn,nbhd->mbhd/dot_general | solution.py:84
  219.9 44.0 %all_to_all.24 = bf16[32,1,256,128]{3,2,1,0:T(8,128)(2,1)S(1)} all-to-all(bf16[32,1,256,128]{3,2,1,0:T(8,128)(2,1)} %bitcast.214), channel_id=1, replica_groups=mesh['mem'=2,'lat'=32,'lon'=4] {'mem'}, dimensions={0} | all-to-all | bytes 4194304 | tf_op jit(solution)/shard_map/all_to_all | solution.py:107
  272.2 16.6 %collective-permute-done.5 = bf16[16,1,64,128]{3,2,1,0:T(8,128)(2,1)S(1)} collective-permute-done((bf16[16,1,64,128]{3,2,1,0:T(8,128)(2,1)S(1)}, bf16[16,1,64,128]{3,2,1,0:T(8,128)(2,1)S(1)}, u32[]{:S(2)}, u32[]{:S(2)}) %collective-permute-start.5) | collective-permute-done | bytes 262176 | tf_op jit(solution)/shard_map/ppermute | solution.py:19
  297.5 4.1 %pad_maximum_fusion = (bf16[16,10,65,128]{3,2,1,0:T(8,128)(2,1)S(1)}, bf16[16,10,65,128]{3,2,1,0:T(8,128)(2,1)S(1)}) fusion(bf16[16,10,1,128]{3,2,1,0:T(2,128)(2,1)S(1)} %collective-permute-done.7, bf16[16,1,64,128]{3,2,1,0:T(8,128)(2,1)S(1)} %collective-permute-done.5, bf16[16,8,64,128]{3,2,1,0:T(8,128)(2,1)S(1)} %fusion.21, ...), kind=kLoop, calls=%fused_computation.53 | loop fusion | flops 21299200 | bytes 8028160 | tf_op jit(solution)/shard_map/concatenate | solution.py:15
  301.6 2.7 fusion.61
  306.9 2.7 fusion.63
  314.9 12.1 %add_convert_fusion = bf16[16,8,64,128]{3,2,1,0:T(8,128)(2,1)} fusion(f32[16,8,64,128]{3,2,1,0:T(8,128)} %fusion.41, f32[16,8,64,128]{3,2,1,0:T(8,128)} %fusion.61, f32[16,8,64,128]{3,2,1,0:T(8,128)} %fusion.63, f32[16,8,64,128]{3,2,1,0:T(8,128)S(1)} %fusion.79, f32[16,8,64,128]{3,2,1,0:T(8,128)} %fusion.65, f32[16,8,64,128]{3,2,1,0:T(8,128)} %fusion.67, ...), kind=kOutput, calls=%fused_computation.31 | convolution fusion | flops 281018368 | bytes 39879168 | tf_op jit(solution)/shard_map/mrlc,cd->mrld/dot_general | solution.py:33
  (101 shorter events, 97.7 us)
Async XLA Ops:
  0.0 109.1 %copy-start = (bf16[128,128]{1,0:T(8,128)(2,1)S(1)}, bf16[128,128]{1,0:T(8,128)(2,1)}, u32[]{:S(2)}) copy-start(bf16[128,128]{1,0:T(8,128)(2,1)} %param.17) | copy-start | bytes 98308
  0.0 10.0 %copy-start.2 = (bf16[16,8,64,128]{3,2,1,0:T(8,128)(2,1)S(1)}, bf16[16,8,64,128]{3,2,1,0:T(8,128)(2,1)}, u32[]{:S(2)}) copy-start(bf16[16,8,64,128]{3,2,1,0:T(8,128)(2,1)} %param.12) | copy-start | bytes 6291460
  1.2 8.8 %collective-permute-start = (bf16[16,1,64,128]{3,2,1,0:T(8,128)(2,1)S(1)}, bf16[16,1,64,128]{3,2,1,0:T(8,128)(2,1)S(1)}, u32[]{:S(2)}, u32[]{:S(2)}) collective-permute-start(bf16[16,1,64,128]{3,2,1,0:T(8,128)(2,1)S(1)} %get-tuple-element.90), channel_id=1, source_target_pairs={{0,4},{4,8},{8,12},{12,16},{16,20},{20,24},{24,28},{28,32},{32,36}... | collective-permute-start | bytes 786440 | tf_op jit(solution)/shard_map/ppermute | solution.py:17
  5.7 8.0 %collective-permute-start.1 = (bf16[16,1,64,128]{3,2,1,0:T(8,128)(2,1)S(1)}, bf16[16,1,64,128]{3,2,1,0:T(8,128)(2,1)S(1)}, u32[]{:S(2)}, u32[]{:S(2)}) collective-permute-start(bf16[16,1,64,128]{3,2,1,0:T(8,128)(2,1)S(1)} %get-tuple-element.91), channel_id=1, source_target_pairs={{4,0},{8,4},{12,8},{16,12},{20,16},{24,20},{28,24},{32,28},{36,32}... | collective-permute-start | bytes 786440 | tf_op jit(solution)/shard_map/ppermute | solution.py:19
  10.0 8.4 %copy-start.7 = (bf16[3,3,128,128]{3,2,1,0:T(8,128)(2,1)S(1)}, bf16[3,3,128,128]{3,2,1,0:T(8,128)(2,1)}, u32[]{:S(2)}) copy-start(bf16[3,3,128,128]{3,2,1,0:T(8,128)(2,1)} %param.13) | copy-start | bytes 884740
  13.9 9.7 %collective-permute-start.3 = (bf16[16,10,1,128]{3,2,1,0:T(2,128)(2,1)S(1)}, bf16[16,10,1,128]{3,2,1,0:T(2,128)(2,1)S(1)}, u32[]{:S(2)}, u32[]{:S(2)}) collective-permute-start(bf16[16,10,1,128]{3,2,1,0:T(2,128)(2,1)S(1)} %get-tuple-element.86), channel_id=1, source_target_pairs={{1,0},{2,1},{3,2},{0,3},{5,4},{6,5},{7,6},{4,7},{9,8},{10,9},{11,1... | collective-permute-start | bytes 122888 | tf_op jit(solution)/shard_map/ppermute | solution.py:19
  18.3 10.7 %collective-permute-start.2 = (bf16[16,10,1,128]{3,2,1,0:T(2,128)(2,1)S(1)}, bf16[16,10,1,128]{3,2,1,0:T(2,128)(2,1)S(1)}, u32[]{:S(2)}, u32[]{:S(2)}) collective-permute-start(bf16[16,10,1,128]{3,2,1,0:T(2,128)(2,1)S(1)} %get-tuple-element.87), channel_id=1, source_target_pairs={{0,1},{1,2},{2,3},{3,0},{4,5},{5,6},{6,7},{7,4},{8,9},{9,10},{10,1... | collective-permute-start | bytes 122888 | tf_op jit(solution)/shard_map/ppermute | solution.py:17
  34.4 2.7 copy-start.12
  37.0 17.7 %copy-start.10 = (f32[128]{0:T(128)S(1)}, f32[128]{0:T(128)}, u32[]{:S(2)}) copy-start(f32[128]{0:T(128)} %param.15) | copy-start | bytes 1540
  52.3 2.4 copy-start.3
  58.7 52.4 %copy-start.8 = (bf16[128,128]{1,0:T(8,128)(2,1)S(1)}, bf16[128,128]{1,0:T(8,128)(2,1)}, u32[]{:S(2)}) copy-start(bf16[128,128]{1,0:T(8,128)(2,1)} %param.16) | copy-start | bytes 98308
  58.7 50.4 %all-to-all-start = ((bf16[16,2,256,128]{3,2,0,1:T(8,128)(2,1)}), bf16[16,2,256,128]{3,2,0,1:T(8,128)(2,1)S(1)}, u32[]{:S(2)}, u32[]{:S(2)}) async-start(bf16[16,2,256,128]{3,2,0,1:T(8,128)(2,1)} %copy.27), calls=%async_computation | async-start | bytes 4194304 | tf_op jit(solution)/shard_map/all_to_all | solution.py:101
  109.1 4.0 %copy-start.9 = (bf16[128,128]{1,0:T(8,128)(2,1)S(1)}, bf16[128,128]{1,0:T(8,128)(2,1)}, u32[]{:S(2)}) copy-start(bf16[128,128]{1,0:T(8,128)(2,1)} %param.18) | copy-start | bytes 98308
  111.1 4.1 %copy-start.5 = (bf16[128,128]{1,0:T(8,128)(2,1)S(1)}, bf16[128,128]{1,0:T(8,128)(2,1)}, u32[]{:S(2)}) copy-start(bf16[128,128]{1,0:T(8,128)(2,1)} %param.19) | copy-start | bytes 98308
  264.4 1.6 copy-start.4
  266.0 5.3 %copy-start.6 = (bf16[3,3,128,128]{3,2,1,0:T(8,128)(2,1)S(1)}, bf16[3,3,128,128]{3,2,1,0:T(8,128)(2,1)}, u32[]{:S(2)}) copy-start(bf16[3,3,128,128]{3,2,1,0:T(8,128)(2,1)} %param.20) | copy-start | bytes 884740
  266.9 5.2 %collective-permute-start.4 = (bf16[16,1,64,128]{3,2,1,0:T(8,128)(2,1)S(1)}, bf16[16,1,64,128]{3,2,1,0:T(8,128)(2,1)S(1)}, u32[]{:S(2)}, u32[]{:S(2)}) collective-permute-start(bf16[16,1,64,128]{3,2,1,0:T(8,128)(2,1)S(1)} %get-tuple-element.88), channel_id=1, source_target_pairs={{0,4},{4,8},{8,12},{12,16},{16,20},{20,24},{24,28},{28,32},{32,36}... | collective-permute-start | bytes 786440 | tf_op jit(solution)/shard_map/ppermute | solution.py:17
  268.9 19.9 %collective-permute-start.5 = (bf16[16,1,64,128]{3,2,1,0:T(8,128)(2,1)S(1)}, bf16[16,1,64,128]{3,2,1,0:T(8,128)(2,1)S(1)}, u32[]{:S(2)}, u32[]{:S(2)}) collective-permute-start(bf16[16,1,64,128]{3,2,1,0:T(8,128)(2,1)S(1)} %get-tuple-element.89), channel_id=1, source_target_pairs={{4,0},{8,4},{12,8},{16,12},{20,16},{24,20},{28,24},{32,28},{36,32}... | collective-permute-start | bytes 786440 | tf_op jit(solution)/shard_map/ppermute | solution.py:19
  288.9 8.7 %collective-permute-start.6 = (bf16[16,10,1,128]{3,2,1,0:T(2,128)(2,1)S(1)}, bf16[16,10,1,128]{3,2,1,0:T(2,128)(2,1)S(1)}, u32[]{:S(2)}, u32[]{:S(2)}) collective-permute-start(bf16[16,10,1,128]{3,2,1,0:T(2,128)(2,1)S(1)} %get-tuple-element.85), channel_id=1, source_target_pairs={{0,1},{1,2},{2,3},{3,0},{4,5},{5,6},{6,7},{7,4},{8,9},{9,10},{10,1... | collective-permute-start | bytes 122888 | tf_op jit(solution)/shard_map/ppermute | solution.py:17
  290.8 6.7 %collective-permute-start.7 = (bf16[16,10,1,128]{3,2,1,0:T(2,128)(2,1)S(1)}, bf16[16,10,1,128]{3,2,1,0:T(2,128)(2,1)S(1)}, u32[]{:S(2)}, u32[]{:S(2)}) collective-permute-start(bf16[16,10,1,128]{3,2,1,0:T(2,128)(2,1)S(1)} %get-tuple-element.84), channel_id=1, source_target_pairs={{1,0},{2,1},{3,2},{0,3},{5,4},{6,5},{7,6},{4,7},{9,8},{10,9},{11,1... | collective-permute-start | bytes 122888 | tf_op jit(solution)/shard_map/ppermute | solution.py:19
  312.3 2.7 copy-start.11
  314.9 12.1 %copy-start.1 = (bf16[128,128]{1,0:T(8,128)(2,1)S(1)}, bf16[128,128]{1,0:T(8,128)(2,1)}, u32[]{:S(2)}) copy-start(bf16[128,128]{1,0:T(8,128)(2,1)} %param.17) | copy-start | bytes 98308
where the time goes:
time: 331 us; the launch traced here: 327 us
  matrix products  130 us (39%)
  waiting for transfers between devices  64.9 us (20%)
  local copies, waits for them, and re-layouts  44.4 us (13%)
  blocking collectives  44 us (13%)
  starting transfers between devices  24.2 us (7%)
  other arithmetic  10.4 us (3%)
  loops' own time  8.45 us (3%)
    dot_general x18, matrix products, conv_taps(): jnp.einsum('mrlc,cd->mrld', window, weights[row_tap, col_tap], preferred_...  67.7 us
    all_to_all x1, waiting for transfers between devices, attend(): lax.all_to_all(grouped, 'mem', split_axis=1, concat_axis=0, tiled=True)  44.8 us
    all_to_all x1, blocking collectives, attend(): lax.all_to_all(attended[:, None], 'mem', split_axis=0, concat_axis=1, til...  44 us
    sub x4, matrix products, one_block(): probs = jax.nn.softmax(scores, axis=-1).astype(jnp.bfloat16)  28.6 us
    dot_general x4, matrix products, one_block(): jnp.einsum('bhmn,nbhd->mbhd', probs, v_block, preferred_element_type=jnp....  23.8 us
    ppermute x4, waiting for transfers between devices, extended(): lax.ppermute(head, axis, [((i + 1) % count, i) for i in range(ends)])  20 us
    dynamic_slice x8, local copies, waits for them, and re-layouts, one_block(): lax.dynamic_slice_in_dim(key_proj, offset, block_len, 1)  14.1 us
    ppermute x4, starting transfers between devices, extended(): lax.ppermute(head, axis, [((i + 1) % count, i) for i in range(ends)])  10.2 us
  transfers between devices with their start and end apart: 9, of which 4 were waited for; matrix products, arithmetic and copies ran while one was open for 6% of the time, Pallas kernels for 0%

commit v1 on v0

v1 whole, which is shorter than its diff:
```python
import functools

import jax
import jax.numpy as jnp
from jax import lax
from jax.experimental import pallas as pl
from jax.experimental.pallas import tpu as pltpu
from jax.sharding import PartitionSpec as P

HEADS = 8
CH = 128
HEAD_DIM = CH // HEADS
MEM = 16
ROWS = 8
COLS = 64
EDGE = 4
MID = COLS - 2 * EDGE
BF = jnp.bfloat16
F32 = jnp.float32
WEIGHT = 0.35
VMEM_LIMIT = 56 * 1024 * 1024


def call(body, out_shape, scratch, micros, name, aliases=None, in_specs=None, out_specs=None, grid=()):
    return pl.pallas_call(
        body,
        out_shape=out_shape,
        scratch_shapes=scratch,
        in_specs=in_specs,
        out_specs=out_specs,
        grid=grid,
        input_output_aliases=aliases or {},
        compiler_params=pltpu.CompilerParams(vmem_limit_bytes=VMEM_LIMIT),
        cost_estimate=pl.CostEstimate(
            flops=int(micros * WEIGHT * 1e9), bytes_accessed=1024, transcendentals=0
        ),
        name=name,
    )


def bf(*shape):
    return jax.ShapeDtypeStruct(shape, BF)


VM = pl.BlockSpec(memory_space=pltpu.VMEM)


def pair_weights(w_ref, wide):
    zero = jnp.zeros((3 * CH, CH), BF)
    wide[0 : 9 * CH, 0:CH] = w_ref[...]
    wide[9 * CH : 12 * CH, 0:CH] = zero
    wide[0 : 3 * CH, CH : 2 * CH] = zero
    wide[3 * CH : 12 * CH, CH : 2 * CH] = w_ref[...]


def taps(load, rows, first, width):
    return jnp.concatenate(
        [load(r, first + j, width).reshape(width * MEM, CH) for r in rows for j in range(3)],
        axis=-1,
    )


def head_of(summed, bias, gain):
    values = summed + bias
    hidden = (values * 0.5 * (1.0 + lax.erf(values * 0.7071067811865476))).astype(BF)
    wide = hidden.astype(F32)
    centre = jnp.mean(wide, axis=-1, keepdims=True)
    moved = wide - centre
    spread = jnp.mean(moved * moved, axis=-1, keepdims=True)
    normed = (moved * lax.rsqrt(spread + 1e-05) * gain).astype(BF)
    return hidden, normed


def finish(acc, count, lane, bias, gain, hid_ref, norm_ref, start):
    part = count // 2

    def body(t, _):
        rows = pl.ds(pl.multiple_of(t * part * MEM, 128), part * MEM)
        hidden, normed = head_of(acc[rows, lane : lane + CH], bias, gain)
        hid_ref[pl.ds(start + t * part, part)] = hidden.reshape(part, MEM, CH)
        norm_ref[pl.ds(start + t * part, part)] = normed.reshape(part, MEM, CH)
        return 0

    lax.fori_loop(0, 2, body, 0)


def turn(ens_ref, row, out_ref):
    out_ref[row] = jnp.swapaxes(ens_ref[:, row], 0, 1)


def first_body(ens_ref, w_ref, bias_ref, gain_ref, x_ref, hid_ref, norm_ref, wide, acc):
    pair_weights(w_ref, wide)
    for row in range(4):
        turn(ens_ref, row, x_ref)
    load = lambda r, c, n: x_ref[r, c : c + n]
    acc[...] = jnp.dot(taps(load, range(4), EDGE - 1, MID), wide[...], preferred_element_type=F32)
    bias, gain = bias_ref[...], gain_ref[...]
    for k in range(2):
        finish(acc, MID, k * CH, bias, gain, hid_ref, norm_ref, k * MID)


def second_body(
    x0_ref, x1_ref, w_ref, bias_ref, gain_ref, hid3, norm3, hid4, norm4, hid56, norm56, wide, acc
):
    pair_weights(w_ref, wide)
    load = lambda r, c, n: x0_ref[r, c : c + n] if r < 4 else x1_ref[r - 4, c : c + n]
    bias, gain = bias_ref[...], gain_ref[...]
    for top, outs in ((3, ((hid3, norm3, 0), (hid4, norm4, 0))), (5, ((hid56, norm56, 0), (hid56, norm56, MID)))):
        acc[...] = jnp.dot(
            taps(load, range(top - 1, top + 3), EDGE - 1, MID), wide[...], preferred_element_type=F32
        )
        for k, (hid, norm, start) in enumerate(outs):
            finish(acc, MID, k * CH, bias, gain, hid, norm, start)


def fill(pad, top, bottom, left, right):
    pad[0, 1 : COLS + 1] = top[...]
    pad[ROWS + 1, 1 : COLS + 1] = bottom[...]
    pad[:, 0] = left[...]
    pad[:, COLS + 1] = right[...]


def edge_body(
    ens_ref, x0_ref, top, bottom, left, right, w_ref, bias_ref, gain_ref,
    x1_ref, hid, norm, wide, acc, pad,
):
    pair_weights(w_ref, wide)
    flip = lambda ref: jnp.swapaxes(ref[...], 0, 1)
    pad[0, 1 : COLS + 1] = flip(top)
    pad[ROWS + 1, 1 : COLS + 1] = flip(bottom)
    pad[:, 0] = flip(left)
    pad[:, COLS + 1] = flip(right)
    for r in range(4):
        turn(ens_ref, r, x1_ref)
        pad[r + 1, 1 : COLS + 1] = x0_ref[r]
        pad[r + 5, 1 : COLS + 1] = x1_ref[r]
    load = lambda r, c, n: pad[r, c : c + n]
    bias, gain = bias_ref[...], gain_ref[...]
    for k, row in enumerate((0, 7)):
        acc[...] = jnp.dot(
            taps(load, range(row, row + 3), 0, COLS), w_ref[...], preferred_element_type=F32
        )
        finish(acc, COLS, 0, bias, gain, hid, norm, k * COLS)
    sides = [
        taps(load, range(row, row + 4), first, EDGE)
        for row in (1, 3, 5)
        for first in (0, COLS - EDGE)
    ]
    both = jnp.dot(jnp.concatenate(sides, axis=0), wide[...], preferred_element_type=F32)
    count = 3 * 2 * EDGE * MEM
    acc[0:count] = both[:, 0:CH]
    acc[count : 2 * count] = both[:, CH : 2 * CH]
    finish(acc, 2 * 3 * 2 * EDGE, 0, bias, gain, hid, norm, 2 * COLS)


def mix(
    count, own_ref, far_ref, hid_ref, wq_ref, wk_ref, wv_ref, wo_ref, upd_ref,
    q_scr, k_scr, v_scr, ctx, s_scr, p_scr,
):
    own = own_ref[...].reshape(count * MEM, CH)
    far = far_ref[...].reshape(count * MEM, CH)
    dot = functools.partial(jnp.dot, preferred_element_type=F32)
    points = lambda cells: cells.astype(BF).reshape(count, MEM, CH)
    both = jnp.concatenate([wk_ref[...], wv_ref[...]], axis=1)
    near = dot(own, jnp.concatenate([both, wq_ref[...]], axis=1))
    k_scr[:, 0:MEM] = points(near[:, 0:CH])
    v_scr[:, 0:MEM] = points(near[:, CH : 2 * CH])
    q_scr[...] = points(near[:, 2 * CH :])
    other = dot(far, both)
    k_scr[:, MEM:] = points(other[:, 0:CH])
    v_scr[:, MEM:] = points(other[:, CH:])

    rows = lax.broadcasted_iota(jnp.int32, (CH, CH), 0) // HEAD_DIM
    lanes = lax.broadcasted_iota(jnp.int32, (CH, CH), 1) // HEAD_DIM
    own_head = jnp.where(rows == lanes, 1.0, 0.0).astype(BF)
    lane16 = lax.broadcasted_iota(jnp.int32, (MEM, CH), 1) // HEAD_DIM
    factor = 1.4426950408889634 / HEAD_DIM**0.5
    group = group_of(count)
    steps = count // group
    blank = jnp.zeros((2 * MEM, CH), BF)

    def score(t):
        for u in range(group):
            p = t * group + u
            heads = jnp.concatenate([q_scr[p]] * HEADS, axis=0) * own_head
            s_scr[t % 2, u] = lax.dot_general(
                k_scr[p], heads, (((1,), (1,)), ((), ())), preferred_element_type=F32
            )

    def weigh(t):
        for g in range(group // 4):
            probs = []
            for v in range(4):
                scores = s_scr[t % 2, g * 4 + v]
                top = jnp.max(scores, axis=0, keepdims=True)
                grown = jnp.exp2((scores - top) * factor)
                total = jnp.sum(grown, axis=0, keepdims=True)
                probs.append(grown * (1.0 / total))
            p_scr[t % 2, g] = jnp.concatenate(probs, axis=0).T.astype(BF)

    def gather(t):
        for g in range(group // 4):
            first = t * group + g * 4
            values = [
                jnp.concatenate([v_scr[first + v] if w == v else blank for w in range(4)], axis=1)
                for v in range(4)
            ]
            mixed = dot(p_scr[t % 2, g], jnp.concatenate(values, axis=0))
            for v in range(4):
                out = mixed[0:MEM, v * CH : (v + 1) * CH]
                for h in range(1, HEADS):
                    out = jnp.where(
                        lane16 == h, mixed[h * MEM : (h + 1) * MEM, v * CH : (v + 1) * CH], out
                    )
                ctx[first + v] = out.astype(BF)

    score(0)
    score(1)
    weigh(0)

    def body(t, _):
        gather(t - 2)
        weigh(t - 1)
        score(t)
        return 0

    lax.fori_loop(2, steps, body, 0)
    weigh(steps - 1)
    gather(steps - 2)
    gather(steps - 1)
    attended = dot(ctx[...].reshape(count * MEM, CH), wo_ref[...]).astype(BF)
    upd_ref[...] = (
        hid_ref[...].astype(F32) + attended.astype(F32).reshape(count, MEM, CH)
    ).astype(BF)


def group_of(count):
    return 16 if count % 16 == 0 else 8


def mix_scratch(count):
    group = group_of(count)
    return [
        pltpu.VMEM((count, MEM, CH), BF),
        pltpu.VMEM((count, 2 * MEM, CH), BF),
        pltpu.VMEM((count, 2 * MEM, CH), BF),
        pltpu.VMEM((count, MEM, CH), BF),
        pltpu.VMEM((2, group, 2 * MEM, CH), F32),
        pltpu.VMEM((2, group // 4, CH, CH), BF),
    ]


def put_edge(pad, edge):
    pad[1, 1 : COLS + 1] = edge[0:COLS]
    pad[ROWS, 1 : COLS + 1] = edge[COLS : 2 * COLS]
    half = 3 * 2 * EDGE
    for k in range(2):
        for i, row in enumerate((1, 3, 5)):
            base = 2 * COLS + k * half + i * 2 * EDGE
            pad[row + k + 1, 1 : EDGE + 1] = edge[base : base + EDGE]
            pad[row + k + 1, COLS - EDGE + 1 : COLS + 1] = edge[base + EDGE : base + 2 * EDGE]


def second_conv(pad, row, w, bias, out_ref):
    load = lambda r, c, n: pad[r, c : c + n]
    both = jnp.dot(taps(load, range(row, row + 4), 0, COLS), w, preferred_element_type=F32)
    for k in range(2):
        own = pad[row + k + 1, 1 : COLS + 1].reshape(COLS * MEM, CH).astype(F32)
        cells = (own + both[:, k * CH : (k + 1) * CH] + bias).astype(BF)
        out_ref[:, k] = jnp.swapaxes(cells.reshape(COLS, MEM, CH), 0, 1)


def outer_body(
    edge, upd12, upd56, top, bottom, left, right, w_ref, bias_ref, out_ref, wide, pad
):
    step = pl.program_id(0)

    @pl.when(step == 0)
    def _():
        pair_weights(w_ref, wide)
        fill(pad, top, bottom, left, right)
        put_edge(pad, edge)
        for k in range(2):
            pad[2 + k, EDGE + 1 : EDGE + 1 + MID] = upd12[k * MID : (k + 1) * MID]
            pad[6 + k, EDGE + 1 : EDGE + 1 + MID] = upd56[k * MID : (k + 1) * MID]
        second_conv(pad, 0, wide[...], bias_ref[...], out_ref)

    @pl.when(step == 1)
    def _():
        second_conv(pad, 6, wide[...], bias_ref[...], out_ref)


def last_body(
    own_ref, far_ref, hid_ref, wq_ref, wk_ref, wv_ref, wo_ref,
    edge, upd12, upd56, upd3, left, right, w_ref, bias_ref, _, out_ref,
    q_scr, k_scr, v_scr, ctx, s_scr, p_scr, upd4, wide, pad,
):
    step = pl.program_id(0)

    @pl.when(step == 0)
    def _():
        mix(
            MID, own_ref, far_ref, hid_ref, wq_ref, wk_ref, wv_ref, wo_ref, upd4,
            q_scr, k_scr, v_scr, ctx, s_scr, p_scr,
        )
        pair_weights(w_ref, wide)
        pad[:, 0] = left[...]
        pad[:, COLS + 1] = right[...]
        put_edge(pad, edge)
        mid = slice(EDGE + 1, EDGE + 1 + MID)
        pad[4, mid] = upd3[...]
        pad[5, mid] = upd4[...]
        for k in range(2):
            pad[2 + k, mid] = upd12[k * MID : (k + 1) * MID]
            pad[6 + k, mid] = upd56[k * MID : (k + 1) * MID]
        second_conv(pad, 2, wide[...], bias_ref[...], out_ref)

    @pl.when(step == 1)
    def _():
        second_conv(pad, 4, wide[...], bias_ref[...], out_ref)


WIDE = pltpu.VMEM((12 * CH, 2 * CH), BF)
PAD = pltpu.VMEM((ROWS + 2, COLS + 2, MEM, CH), BF)
ACC_MID = pltpu.VMEM((MID * MEM, 2 * CH), F32)
ACC1 = pltpu.VMEM((COLS * MEM, CH), F32)
EDGES = 2 * COLS + 6 * 2 * EDGE


def half_rows(which):
    return pl.BlockSpec((MEM, 4, COLS, CH), lambda i: (0, which, 0, 0))


def run_first(ens, w, bias, gain):
    return call(
        first_body,
        (bf(4, COLS, MEM, CH), bf(2 * MID, MEM, CH), bf(2 * MID, MEM, CH)),
        [WIDE, ACC_MID],
        0.1,
        "conv_rows12",
        in_specs=[half_rows(0), VM, VM, VM],
        out_specs=[VM] * 3,
        grid=(1,),
    )(ens, w, bias, gain)


def run_edge(ens, x0, rim, w, bias, gain):
    return call(
        edge_body,
        (bf(4, COLS, MEM, CH),) + (bf(EDGES, MEM, CH),) * 2,
        [WIDE, ACC1, PAD],
        0.1,
        "conv_edges",
        in_specs=[half_rows(1)] + [VM] * 8,
        out_specs=[VM] * 3,
        grid=(1,),
    )(ens, x0, *rim, w, bias, gain)


def run_second(x0, x1, w, bias, gain):
    return call(
        second_body,
        (bf(MID, MEM, CH),) * 4 + (bf(2 * MID, MEM, CH),) * 2,
        [WIDE, ACC_MID],
        10,
        "conv_rows3456",
        in_specs=[VM] * 5,
        out_specs=[VM] * 6,
    )(x0, x1, w, bias, gain)


def run_mix(count, micros, own, far, hid, mats):
    return call(
        functools.partial(mix, count),
        bf(count, MEM, CH),
        mix_scratch(count),
        micros,
        f"mix{count}",
        in_specs=[VM] * 7,
        out_specs=VM,
    )(own, far, hid, *mats)


def mix_edges(
    own_ref, far_ref, hid_ref, wq_ref, wk_ref, wv_ref, wo_ref,
    upd_ref, top, bottom, left, right, *scratch,
):
    mix(EDGES, own_ref, far_ref, hid_ref, wq_ref, wk_ref, wv_ref, wo_ref, upd_ref, *scratch)
    top[...] = upd_ref[0:COLS]
    bottom[...] = upd_ref[COLS : 2 * COLS]
    half = 3 * 2 * EDGE
    for col, at, row_at in ((left, 0, 0), (right, 2 * EDGE - 1, COLS - 1)):
        col[0] = upd_ref[row_at]
        col[ROWS - 1] = upd_ref[COLS + row_at]
        for k in range(2):
            for i, row in enumerate((1, 3, 5)):
                col[row + k] = upd_ref[2 * COLS + k * half + i * 2 * EDGE + at]


def run_mix_edges(own, far, hid, mats):
    return call(
        mix_edges,
        (bf(EDGES, MEM, CH),) + (bf(COLS, MEM, CH),) * 2 + (bf(ROWS, MEM, CH),) * 2,
        mix_scratch(EDGES),
        0.1,
        "mix_edges",
        in_specs=[VM] * 7,
        out_specs=[VM] * 5,
    )(own, far, hid, *mats)


def row_pair(index):
    return pl.BlockSpec((MEM, 2, COLS, CH), index)


def run_outer(edge, upd12, upd56, rim, w, bias):
    return call(
        outer_body,
        bf(MEM, ROWS, COLS, CH),
        [WIDE, PAD],
        0.1,
        "conv2_outer",
        in_specs=[VM] * 9,
        out_specs=row_pair(lambda i: (0, 3 * i, 0, 0)),
        grid=(2,),
    )(edge, upd12, upd56, *rim, w, bias)


def run_last(own, far, hid, mats, edge, upd12, upd56, upd3, left, right, w, bias, partial):
    return call(
        last_body,
        bf(MEM, ROWS, COLS, CH),
        mix_scratch(MID) + [pltpu.VMEM((MID, MEM, CH), BF), WIDE, PAD],
        7.3,
        "mix_conv2_inner",
        aliases={15: 0},
        in_specs=[VM] * 15 + [pl.BlockSpec(memory_space=pl.ANY)],
        out_specs=row_pair(lambda i: (0, i + 1, 0, 0)),
        grid=(2,),
    )(own, far, hid, *mats, edge, upd12, upd56, upd3, left, right, w, bias, partial)


def swap(cells):
    return lax.ppermute(cells, "mem", [(0, 1), (1, 0)])


def lat_rims(top_row, bottom_row):
    count = lax.axis_size("lat")
    above = lax.ppermute(bottom_row, "lat", [(i, i + 1) for i in range(count - 1)])
    below = lax.ppermute(top_row, "lat", [(i + 1, i) for i in range(count - 1)])
    return above, below


def lon_rims(left_col, right_col):
    count = lax.axis_size("lon")
    left = lax.ppermute(right_col, "lon", [(i, (i + 1) % count) for i in range(count)])
    right = lax.ppermute(left_col, "lon", [((i + 1) % count, i) for i in range(count)])
    return left, right


def after(value, *others):
    return lax.optimization_barrier((value, *others))[0]


def shards(ensemble, w_conv1, bias1, gain, w_query, w_key, w_value, w_out, w_conv2, bias2):
    w1 = w_conv1.reshape(9 * CH, CH)
    w2 = w_conv2.reshape(9 * CH, CH)
    b1, g1, b2 = bias1.reshape(1, CH), gain.reshape(1, CH), bias2.reshape(1, CH)
    mats = (w_query, w_key, w_value, w_out)

    x0, hid12, norm12 = run_first(ensemble, w1, b1, g1)
    far12 = swap(norm12)
    above, below = lat_rims(after(ensemble[:, 0], x0), after(ensemble[:, ROWS - 1], x0))
    column = lambda c: jnp.concatenate(
        [above[:, c : c + 1], ensemble[:, :, c], below[:, c : c + 1]], axis=1
    )
    left, right = lon_rims(column(0), column(COLS - 1))
    x1, hid_e, norm_e = run_edge(ensemble, x0, (above, below, left, right), w1, b1, g1)
    far_e = swap(norm_e)
    upd12 = run_mix(2 * MID, 10, after(norm12, norm_e), far12, hid12, mats)
    hid3, norm3, hid4, norm4, hid56, norm56 = run_second(after(x0, upd12), x1, w1, b1, g1)
    far3 = swap(norm3)
    far56 = swap(norm56)
    far4 = swap(after(norm4, far_e))
    upd_e, row0, row7, col0, col63 = run_mix_edges(after(norm_e, norm3), far_e, hid_e, mats)
    above2, below2 = lat_rims(row0, row7)
    side = lambda col, c: jnp.concatenate([above2[c : c + 1], col, below2[c : c + 1]], axis=0)
    left2, right2 = lon_rims(side(col0, 0), side(col63, COLS - 1))
    upd3 = run_mix(MID, 10, after(norm3, upd_e), far3, hid3, mats)
    upd56 = run_mix(2 * MID, 7, after(norm56, upd3), far56, hid56, mats)
    partial = run_outer(upd_e, upd12, upd56, (above2, below2, left2, right2), w2, b2)
    return run_last(
        norm4, far4, hid4, mats, upd_e, upd12, upd56, upd3, left2, right2, w2, b2, partial
    )


def solution(mesh):
    return jax.shard_map(
        shards,
        mesh=mesh,
        in_specs=(P("mem", "lat", "lon", None), P(), P(), P(), P(), P(), P(), P(), P(), P()),
        out_specs=P("mem", "lat", "lon", None),
        check_vma=False,
    )
```

time: 331 us -> 151 us (0.46)
  matrix products: 130 us -> 0 us
  Pallas kernels: 0 us -> 59.9 us
  blocking collectives: 44 us -> 0 us
  waiting for transfers between devices: 64.9 us -> 27 us
  local copies, waits for them, and re-layouts: 44.4 us -> 7.32 us
  starting transfers between devices: 24.2 us -> 54.5 us
  other arithmetic: 10.4 us -> 0.09 us
  loops' own time: 8.45 us -> 0 us
    dot_general x29 -> x0, matrix products: 102 us -> none  [the longest x18 67.7 us: conv_taps(): jnp.einsum('mrlc,cd->mrld', window, weights[row_tap, col_tap], preferred_...]
    pallas_call x0 -> x9, Pallas kernels: none -> 59.9 us  [the longest x3 17.9 us: run_mix(): call(functools.partial(mix, count), bf(count, MEM, CH), mix_scratch(count...]
    all_to_all x1 -> x0, waiting for transfers between devices: 44.8 us -> none  [attend(): lax.all_to_all(grouped, 'mem', split_axis=1, concat_axis=0, tiled=True)]
    all_to_all x1 -> x0, blocking collectives: 44 us -> none  [attend(): lax.all_to_all(attended[:, None], 'mem', split_axis=0, concat_axis=1, til...]
    ppermute x8 -> x13, starting transfers between devices: 18.6 us -> 54.5 us  [the longest x2 27 us: lon_rims(): lax.ppermute(right_col, 'lon', [(i, (i + 1) % count) for i in range(count)])]
    dynamic_slice x24 -> x0, local copies, waits for them, and re-layouts: 30.7 us -> none  [the longest x8 14.1 us: one_block(): lax.dynamic_slice_in_dim(key_proj, offset, block_len, 1)]
    sub x4 -> x0, matrix products: 28.6 us -> none  [one_block(): probs = jax.nn.softmax(scores, axis=-1).astype(jnp.bfloat16)]
    reshape x5 -> x0, local copies, waits for them, and re-layouts: 10.3 us -> none  [the longest x4 8.81 us: one_block(): context = context.reshape(members, block_len, width)]
  transfers between devices with their start and end apart: 9 -> 13, of which waited for: 4 -> 4; matrix products, arithmetic and copies ran while one was open for 6% -> 1% of each run, Pallas kernels for 0% -> 32%
where the time goes in v1:
time: 151 us; the launch traced here: 149 us
  Pallas kernels  59.9 us (40%)
  starting transfers between devices  54.5 us (36%)
  waiting for transfers between devices  27 us (18%)
  local copies, waits for them, and re-layouts  7.32 us (5%)
    ppermute x2, starting transfers between devices, lon_rims(): lax.ppermute(right_col, 'lon', [(i, (i + 1) % count) for i in range(count)])  27 us
    pallas_call x3, Pallas kernels, run_mix(): call(functools.partial(mix, count), bf(count, MEM, CH), mix_scratch(count...  17.9 us
    ppermute x2, waiting for transfers between devices, lon_rims(): lax.ppermute(right_col, 'lon', [(i, (i + 1) % count) for i in range(count)])  17 us
    ppermute x5, starting transfers between devices, swap(): return lax.ppermute(cells, 'mem', [(0, 1), (1, 0)])  12.5 us
    pallas_call x1, Pallas kernels, run_mix_edges(): call(mix_edges, (bf(EDGES, MEM, CH),) + (bf(COLS, MEM, CH),) * 2 + (bf(RO...  9.67 us
    ppermute x5, waiting for transfers between devices, swap(): return lax.ppermute(cells, 'mem', [(0, 1), (1, 0)])  8.84 us
    ppermute x2, starting transfers between devices, lat_rims(): lax.ppermute(bottom_row, 'lat', [(i, i + 1) for i in range(count - 1)])  8.14 us
    pallas_call x1, Pallas kernels, run_edge(): call(edge_body, (bf(4, COLS, MEM, CH),) + (bf(EDGES, MEM, CH),) * 2, [WID...  8.06 us
  transfers between devices with their start and end apart: 13, of which 4 were waited for; matrix products, arithmetic and copies ran while one was open for 1% of the time, Pallas kernels for 32%

profile of v1, /device:TPU:1, one launch (start us, length us, event | category | flops | bytes accessed | tf_op | source)
XLA Modules:
  0.0 149.0 jit_solution(5891274803341406739)
XLA Ops:
  0.0 1.1 slice_bitcast_fusion
  1.1 4.3 %conv_rows12.1 = (bf16[4,64,16,128]{3,2,1,0:T(8,128)(2,1)}, bf16[112,16,128]{2,1,0:T(8,128)(2,1)}, bf16[112,16,128]{2,1,0:T(8,128)(2,1)}) custom-call(bf16[16,8,64,128]{3,2,1,0:T(8,128)(2,1)} %ens_ref.3, bf16[1152,128]{1,0:T(8,128)(2,1)} %bitcast.19, f32[1,128]{1,0:T(1,128)} %bitcast.26, f32[1,128]{1,0:T(1,128)} %bitcast.29), custom_call_target="tpu_custom_call" | custom-call | flops 35000000 | bytes 1024 | tf_op jit(solution)/shard_map/conv_rows12/pallas_call | solution.py:335
  5.4 4.5 %collective-permute-start = (bf16[16,64,128]{2,1,0:T(8,128)(2,1)S(1)}, bf16[16,64,128]{2,1,0:T(8,128)(2,1)S(1)}, u32[]{:S(2)}, u32[]{:S(2)}) collective-permute-start(bf16[16,64,128]{2,1,0:T(8,128)(2,1)S(1)} %get-tuple-element.32), channel_id=1, source_target_pairs={{0,4},{4,8},{8,12},{12,16},{16,20},{20,24},{24,28},{28,32},{32,36}... | collective-permute-start | bytes 786440 | tf_op jit(solution)/shard_map/ppermute | solution.py:449
  9.9 1.9 %collective-permute-start.1 = (bf16[16,64,128]{2,1,0:T(8,128)(2,1)S(1)}, bf16[16,64,128]{2,1,0:T(8,128)(2,1)S(1)}, u32[]{:S(2)}, u32[]{:S(2)}) collective-permute-start(bf16[16,64,128]{2,1,0:T(8,128)(2,1)S(1)} %get-tuple-element.33), channel_id=1, source_target_pairs={{4,0},{8,4},{12,8},{16,12},{20,16},{24,20},{28,24},{32,28},{36,32}... | collective-permute-start | bytes 786440 | tf_op jit(solution)/shard_map/ppermute | solution.py:450
  11.8 7.0 %collective-permute-start.4 = (bf16[112,16,128]{2,1,0:T(8,128)(2,1)}, bf16[112,16,128]{2,1,0:T(8,128)(2,1)S(1)}, u32[]{:S(2)}, u32[]{:S(2)}) collective-permute-start(bf16[112,16,128]{2,1,0:T(8,128)(2,1)} %get-tuple-element.35.own_ref), channel_id=1, source_target_pairs={{0,128},{128,0},{1,129},{129,1},{2,130},{130,2},{3,131},{131,3},{4... | collective-permute-start | bytes 1376264 | tf_op jit(solution)/shard_map/ppermute | solution.py:444
  18.8 1.1 fusion
  21.0 2.6 %collective-permute-start.3 = (bf16[16,10,128]{2,1,0:T(8,128)(2,1)S(1)}, bf16[16,10,128]{2,1,0:T(8,128)(2,1)S(1)}, u32[]{:S(2)}, u32[]{:S(2)}) collective-permute-start(bf16[16,10,128]{2,1,0:T(8,128)(2,1)S(1)} %pad_maximum_fusion.1), channel_id=1, source_target_pairs={{1,0},{2,1},{3,2},{0,3},{5,4},{6,5},{7,6},{4,7},{9,8},{10,9},{11,1... | collective-permute-start | bytes 122888 | tf_op jit(solution)/shard_map/ppermute | solution.py:457
  23.6 17.0 %collective-permute-done.2.left = bf16[16,10,128]{2,1,0:T(8,128)(2,1)S(1)} collective-permute-done((bf16[16,10,128]{2,1,0:T(8,128)(2,1)S(1)}, bf16[16,10,128]{2,1,0:T(8,128)(2,1)S(1)}, u32[]{:S(2)}, u32[]{:S(2)}) %collective-permute-start.2) | collective-permute-done | bytes 40992 | tf_op jit(solution)/shard_map/ppermute | solution.py:456
  40.5 1.2 collective-permute-done.3.right
  42.4 8.1 %conv_edges.1 = (bf16[4,64,16,128]{3,2,1,0:T(8,128)(2,1)}, bf16[176,16,128]{2,1,0:T(8,128)(2,1)}, bf16[176,16,128]{2,1,0:T(8,128)(2,1)}) custom-call(bf16[16,8,64,128]{3,2,1,0:T(8,128)(2,1)} %ens_ref.3, bf16[4,64,16,128]{3,2,1,0:T(8,128)(2,1)} %get-tuple-element.37.x0_ref, bf16[16,64,128]{2,1,0:T(8,128)(2,1)} %copy-done.1, bf16[16,64,128]{2,1,0:T(8,128)(2,1)} %copy-done.2, ...), custom_call_target="tpu_custom_call" | custom-call | flops 35000000 | bytes 1024 | tf_op jit(solution)/shard_map/conv_edges/pallas_call | solution.py:348
  51.4 6.6 %mix112.2.upd12 = bf16[112,16,128]{2,1,0:T(8,128)(2,1)} custom-call(bf16[112,16,128]{2,1,0:T(8,128)(2,1)} %get-tuple-element.35.own_ref, bf16[112,16,128]{2,1,0:T(8,128)(2,1)} %copy-done.12, bf16[112,16,128]{2,1,0:T(8,128)(2,1)} %get-tuple-element.36.hid_ref, bf16[128,128]{1,0:T(8,128)(2,1)} %wq_ref.9, bf16[128,128]{1,0:T(8,128)(2,1)} %wk_ref.9, ...), custom_call_target="tpu_custom_call" | custom-call | flops 3500000000 | bytes 1024 | tf_op jit(solution)/shard_map/mix112/pallas_call | solution.py:373
  58.0 7.8 %conv_rows3456.1 = (bf16[56,16,128]{2,1,0:T(8,128)(2,1)}, bf16[56,16,128]{2,1,0:T(8,128)(2,1)}, bf16[56,16,128]{2,1,0:T(8,128)(2,1)}, bf16[56,16,128]{2,1,0:T(8,...) custom-call(bf16[4,64,16,128]{3,2,1,0:T(8,128)(2,1)} %get-tuple-element.37.x0_ref, ...), custom_call_target="tpu_custom_call" | custom-call | flops 3500000000 | bytes 1024 | tf_op jit(solution)/shard_map/conv_rows3456/pallas_call | solution.py:361
  65.8 5.2 %collective-permute-start.7 = (bf16[56,16,128]{2,1,0:T(8,128)(2,1)}, bf16[56,16,128]{2,1,0:T(8,128)(2,1)S(1)}, u32[]{:S(2)}, u32[]{:S(2)}) collective-permute-start(bf16[56,16,128]{2,1,0:T(8,128)(2,1)} %get-tuple-element.47.own_ref), channel_id=1, source_target_pairs={{0,128},{128,0},{1,129},{129,1},{2,130},{130,2},{3,131},{131,3},{4... | collective-permute-start | bytes 688136 | tf_op jit(solution)/shard_map/ppermute | solution.py:444
  71.2 7.6 %collective-permute-done.5.far_ref = bf16[176,16,128]{2,1,0:T(8,128)(2,1)S(1)} collective-permute-done((bf16[176,16,128]{2,1,0:T(8,128)(2,1)}, bf16[176,16,128]{2,1,0:T(8,128)(2,1)S(1)}, u32[]{:S(2)}, u32[]{:S(2)}) %collective-permute-start.5) | collective-permute-done | bytes 720928 | tf_op jit(solution)/shard_map/ppermute | solution.py:444
  78.8 0.9 copy-done
  79.6 9.7 %mix_edges.1 = (bf16[176,16,128]{2,1,0:T(8,128)(2,1)}, bf16[64,16,128]{2,1,0:T(8,128)(2,1)}, bf16[64,16,128]{2,1,0:T(8,128)(2,1)}, bf16[8,16,128]{2,1,0:T(8,128)(2,1)}, bf16[8,16,128]{2,1,0:T(8,128)(2,1)}) custom-call(bf16[176,16,128]{2,1,0:T(8,128)(2,1)} %get-tuple-element.43.own_ref, bf16[176,16,128]{2,1,0:T(8,128)(2,1)} %copy-done, ...), custom_call_target="tpu_custom_call" | custom-call | flops 35000000 | bytes 1024 | tf_op jit(solution)/shard_map/mix_edges/pallas_call | solution.py:401
  89.3 3.6 %collective-permute-start.9 = (bf16[64,16,128]{2,1,0:T(8,128)(2,1)}, bf16[64,16,128]{2,1,0:T(8,128)(2,1)S(1)}, u32[]{:S(2)}, u32[]{:S(2)}) collective-permute-start(bf16[64,16,128]{2,1,0:T(8,128)(2,1)} %get-tuple-element.51), channel_id=1, source_target_pairs={{0,4},{4,8},{8,12},{12,16},{16,20},{20,24},{24,28},{28,32},{32,36}... | collective-permute-start | bytes 786440 | tf_op jit(solution)/shard_map/ppermute | solution.py:449
  92.9 1.9 %collective-permute-start.10 = (bf16[64,16,128]{2,1,0:T(8,128)(2,1)}, bf16[64,16,128]{2,1,0:T(8,128)(2,1)S(1)}, u32[]{:S(2)}, u32[]{:S(2)}) collective-permute-start(bf16[64,16,128]{2,1,0:T(8,128)(2,1)} %get-tuple-element.53), channel_id=1, source_target_pairs={{4,0},{8,4},{12,8},{16,12},{20,16},{24,20},{28,24},{32,28},{36,32}... | collective-permute-start | bytes 786440 | tf_op jit(solution)/shard_map/ppermute | solution.py:450
  94.9 1.3 collective-permute-done.7.far_ref
  96.8 4.7 %mix56.1.upd3 = bf16[56,16,128]{2,1,0:T(8,128)(2,1)} custom-call(bf16[56,16,128]{2,1,0:T(8,128)(2,1)} %get-tuple-element.47.own_ref, bf16[56,16,128]{2,1,0:T(8,128)(2,1)} %copy-done.15, bf16[56,16,128]{2,1,0:T(8,128)(2,1)} %get-tuple-element.48.hid_ref, bf16[128,128]{1,0:T(8,128)(2,1)} %wq_ref.9, bf16[128,128]{1,0:T(8,128)(2,1)} %wk_ref.9, ...), custom_call_target="tpu_custom_call" | custom-call | flops 3500000000 | bytes 1024 | tf_op jit(solution)/shard_map/mix56/pallas_call | solution.py:373
  101.6 26.2 %collective-permute-start.11 = (bf16[10,16,128]{2,1,0:T(8,128)(2,1)S(1)}, bf16[10,16,128]{2,1,0:T(8,128)(2,1)S(1)}, u32[]{:S(2)}, u32[]{:S(2)}) collective-permute-start(bf16[10,16,128]{2,1,0:T(8,128)(2,1)S(1)} %pad_maximum_fusion.2), channel_id=1, source_target_pairs={{0,1},{1,2},{2,3},{3,0},{4,5},{5,6},{6,7},{7,4},{8,9},{9,10},{10,1... | collective-permute-start | bytes 122888 | tf_op jit(solution)/shard_map/ppermute | solution.py:456
  128.9 6.6 %mix112.3.upd56 = bf16[112,16,128]{2,1,0:T(8,128)(2,1)} custom-call(bf16[112,16,128]{2,1,0:T(8,128)(2,1)} %get-tuple-element.49.own_ref, bf16[112,16,128]{2,1,0:T(8,128)(2,1)} %copy-done.11, bf16[112,16,128]{2,1,0:T(8,128)(2,1)} %get-tuple-element.50.hid_ref, bf16[128,128]{1,0:T(8,128)(2,1)} %wq_ref.9, bf16[128,128]{1,0:T(8,128)(2,1)} %wk_ref.9, ...), custom_call_target="tpu_custom_call" | custom-call | flops 2449999872 | bytes 1024 | tf_op jit(solution)/shard_map/mix112/pallas_call | solution.py:373
  136.2 4.7 %conv2_outer.1._ = bf16[16,8,64,128]{3,2,1,0:T(8,128)(2,1)} custom-call(bf16[176,16,128]{2,1,0:T(8,128)(2,1)} %get-tuple-element.45.edge, bf16[112,16,128]{2,1,0:T(8,128)(2,1)} %mix112.2.upd12, bf16[112,16,128]{2,1,0:T(8,128)(2,1)} %mix112.3.upd56, bf16[64,16,128]{2,1,0:T(8,128)(2,1)} %copy-done.3, bf16[64,16,128]{2,1,0:T(8,128)(2,1)} %copy-done.4, ...), custom_call_target="tpu_custom_call" | custom-call | flops 35000000 | bytes 1024 | tf_op jit(solution)/shard_map/conv2_outer/pallas_call | solution.py:417
  141.6 7.4 %mix_conv2_inner.1 = bf16[16,8,64,128]{3,2,1,0:T(8,128)(2,1)} custom-call(bf16[56,16,128]{2,1,0:T(8,128)(2,1)} %get-tuple-element.40.own_ref, bf16[56,16,128]{2,1,0:T(8,128)(2,1)} %copy-done.14, bf16[56,16,128]{2,1,0:T(8,128)(2,1)} %get-tuple-element.41.hid_ref, bf16[128,128]{1,0:T(8,128)(2,1)} %wq_ref.9, ...), custom_call_target="tpu_custom_call", output_to_operand_aliasing={{}: (15, {})} | custom-call | flops 2555000064 | bytes 1024 | tf_op jit(solution)/shard_map/mix_conv2_inner/pallas_call | solution.py:430
  (55 shorter events, 5.8 us)
Async XLA Ops:
  5.4 14.6 %collective-permute-start = (bf16[16,64,128]{2,1,0:T(8,128)(2,1)S(1)}, bf16[16,64,128]{2,1,0:T(8,128)(2,1)S(1)}, u32[]{:S(2)}, u32[]{:S(2)}) collective-permute-start(bf16[16,64,128]{2,1,0:T(8,128)(2,1)S(1)} %get-tuple-element.32), channel_id=1, source_target_pairs={{0,4},{4,8},{8,12},{12,16},{16,20},{20,24},{24,28},{28,32},{32,36}... | collective-permute-start | bytes 786440 | tf_op jit(solution)/shard_map/ppermute | solution.py:449
  9.9 10.1 %collective-permute-start.1 = (bf16[16,64,128]{2,1,0:T(8,128)(2,1)S(1)}, bf16[16,64,128]{2,1,0:T(8,128)(2,1)S(1)}, u32[]{:S(2)}, u32[]{:S(2)}) collective-permute-start(bf16[16,64,128]{2,1,0:T(8,128)(2,1)S(1)} %get-tuple-element.33), channel_id=1, source_target_pairs={{4,0},{8,4},{12,8},{16,12},{20,16},{24,20},{28,24},{32,28},{36,32}... | collective-permute-start | bytes 786440 | tf_op jit(solution)/shard_map/ppermute | solution.py:450
  11.8 38.8 %collective-permute-start.4 = (bf16[112,16,128]{2,1,0:T(8,128)(2,1)}, bf16[112,16,128]{2,1,0:T(8,128)(2,1)S(1)}, u32[]{:S(2)}, u32[]{:S(2)}) collective-permute-start(bf16[112,16,128]{2,1,0:T(8,128)(2,1)} %get-tuple-element.35.own_ref), channel_id=1, source_target_pairs={{0,128},{128,0},{1,129},{129,1},{2,130},{130,2},{3,131},{131,3},{4... | collective-permute-start | bytes 1376264 | tf_op jit(solution)/shard_map/ppermute | solution.py:444
  20.0 21.8 %copy-start.1 = (bf16[16,64,128]{2,1,0:T(8,128)(2,1)}, bf16[16,64,128]{2,1,0:T(8,128)(2,1)S(1)}, u32[]{:S(2)}) copy-start(bf16[16,64,128]{2,1,0:T(8,128)(2,1)S(1)} %collective-permute-done.top) | copy-start | bytes 786436
  20.0 21.7 %copy-start.2 = (bf16[16,64,128]{2,1,0:T(8,128)(2,1)}, bf16[16,64,128]{2,1,0:T(8,128)(2,1)S(1)}, u32[]{:S(2)}) copy-start(bf16[16,64,128]{2,1,0:T(8,128)(2,1)S(1)} %collective-permute-done.1.bottom) | copy-start | bytes 786436
  20.1 20.4 %collective-permute-start.2 = (bf16[16,10,128]{2,1,0:T(8,128)(2,1)S(1)}, bf16[16,10,128]{2,1,0:T(8,128)(2,1)S(1)}, u32[]{:S(2)}, u32[]{:S(2)}) collective-permute-start(bf16[16,10,128]{2,1,0:T(8,128)(2,1)S(1)} %pad_maximum_fusion), channel_id=1, source_target_pairs={{0,1},{1,2},{2,3},{3,0},{4,5},{5,6},{6,7},{7,4},{8,9},{9,10},{10,1... | collective-permute-start | bytes 122888 | tf_op jit(solution)/shard_map/ppermute | solution.py:456
  21.0 20.8 %collective-permute-start.3 = (bf16[16,10,128]{2,1,0:T(8,128)(2,1)S(1)}, bf16[16,10,128]{2,1,0:T(8,128)(2,1)S(1)}, u32[]{:S(2)}, u32[]{:S(2)}) collective-permute-start(bf16[16,10,128]{2,1,0:T(8,128)(2,1)S(1)} %pad_maximum_fusion.1), channel_id=1, source_target_pairs={{1,0},{2,1},{3,2},{0,3},{5,4},{6,5},{7,6},{4,7},{9,8},{10,9},{11,1... | collective-permute-start | bytes 122888 | tf_op jit(solution)/shard_map/ppermute | solution.py:457
  40.5 1.2 copy-start.5
  50.5 28.3 %collective-permute-start.5 = (bf16[176,16,128]{2,1,0:T(8,128)(2,1)}, bf16[176,16,128]{2,1,0:T(8,128)(2,1)S(1)}, u32[]{:S(2)}, u32[]{:S(2)}) collective-permute-start(bf16[176,16,128]{2,1,0:T(8,128)(2,1)} %get-tuple-element.43.own_ref), channel_id=1, source_target_pairs={{0,128},{128,0},{1,129},{129,1},{2,130},{130,2},{3,131},{131,3},{4... | collective-permute-start | bytes 2162696 | tf_op jit(solution)/shard_map/ppermute | solution.py:444
  50.6 0.8 copy-start.12
  65.8 30.3 %collective-permute-start.7 = (bf16[56,16,128]{2,1,0:T(8,128)(2,1)}, bf16[56,16,128]{2,1,0:T(8,128)(2,1)S(1)}, u32[]{:S(2)}, u32[]{:S(2)}) collective-permute-start(bf16[56,16,128]{2,1,0:T(8,128)(2,1)} %get-tuple-element.47.own_ref), channel_id=1, source_target_pairs={{0,128},{128,0},{1,129},{129,1},{2,130},{130,2},{3,131},{131,3},{4... | collective-permute-start | bytes 688136 | tf_op jit(solution)/shard_map/ppermute | solution.py:444
  71.0 57.1 %collective-permute-start.8 = (bf16[112,16,128]{2,1,0:T(8,128)(2,1)}, bf16[112,16,128]{2,1,0:T(8,128)(2,1)S(1)}, u32[]{:S(2)}, u32[]{:S(2)}) collective-permute-start(bf16[112,16,128]{2,1,0:T(8,128)(2,1)} %get-tuple-element.49.own_ref), channel_id=1, source_target_pairs={{0,128},{128,0},{1,129},{129,1},{2,130},{130,2},{3,131},{131,3},{4... | collective-permute-start | bytes 1376264 | tf_op jit(solution)/shard_map/ppermute | solution.py:444
  78.8 0.9 copy-start
  89.3 12.2 %collective-permute-start.9 = (bf16[64,16,128]{2,1,0:T(8,128)(2,1)}, bf16[64,16,128]{2,1,0:T(8,128)(2,1)S(1)}, u32[]{:S(2)}, u32[]{:S(2)}) collective-permute-start(bf16[64,16,128]{2,1,0:T(8,128)(2,1)} %get-tuple-element.51), channel_id=1, source_target_pairs={{0,4},{4,8},{8,12},{12,16},{16,20},{20,24},{24,28},{28,32},{32,36}... | collective-permute-start | bytes 786440 | tf_op jit(solution)/shard_map/ppermute | solution.py:449
  92.9 8.6 %collective-permute-start.10 = (bf16[64,16,128]{2,1,0:T(8,128)(2,1)}, bf16[64,16,128]{2,1,0:T(8,128)(2,1)S(1)}, u32[]{:S(2)}, u32[]{:S(2)}) collective-permute-start(bf16[64,16,128]{2,1,0:T(8,128)(2,1)} %get-tuple-element.53), channel_id=1, source_target_pairs={{4,0},{8,4},{12,8},{16,12},{20,16},{24,20},{28,24},{32,28},{36,32}... | collective-permute-start | bytes 786440 | tf_op jit(solution)/shard_map/ppermute | solution.py:450
  96.8 4.7 %copy-start.13 = (bf16[56,16,128]{2,1,0:T(8,128)(2,1)S(1)}, bf16[56,16,128]{2,1,0:T(8,128)(2,1)}, u32[]{:S(2)}) copy-start(bf16[56,16,128]{2,1,0:T(8,128)(2,1)} %get-tuple-element.40.own_ref) | copy-start | bytes 688132
  96.8 4.7 %copy-start.10 = (bf16[8,16,128]{2,1,0:T(8,128)(2,1)S(1)}, bf16[8,16,128]{2,1,0:T(8,128)(2,1)}, u32[]{:S(2)}) copy-start(bf16[8,16,128]{2,1,0:T(8,128)(2,1)} %get-tuple-element.52) | copy-start | bytes 98308
  96.8 31.0 %copy-start.9 = (bf16[8,16,128]{2,1,0:T(8,128)(2,1)S(1)}, bf16[8,16,128]{2,1,0:T(8,128)(2,1)}, u32[]{:S(2)}) copy-start(bf16[8,16,128]{2,1,0:T(8,128)(2,1)} %get-tuple-element.54) | copy-start | bytes 98308
  101.5 39.4 %collective-permute-start.6 = (bf16[56,16,128]{2,1,0:T(8,128)(2,1)S(1)}, bf16[56,16,128]{2,1,0:T(8,128)(2,1)S(1)}, u32[]{:S(2)}, u32[]{:S(2)}) collective-permute-start(bf16[56,16,128]{2,1,0:T(8,128)(2,1)S(1)} %copy-done.13), channel_id=1, source_target_pairs={{0,128},{128,0},{1,129},{129,1},{2,130},{130,2},{3,131},{131,3},{4... | collective-permute-start | bytes 688136 | tf_op jit(solution)/shard_map/ppermute | solution.py:444
  101.5 34.1 %copy-start.3 = (bf16[64,16,128]{2,1,0:T(8,128)(2,1)}, bf16[64,16,128]{2,1,0:T(8,128)(2,1)S(1)}, u32[]{:S(2)}) copy-start(bf16[64,16,128]{2,1,0:T(8,128)(2,1)S(1)} %collective-permute-done.9.top) | copy-start | bytes 786436
  101.5 34.0 %copy-start.4 = (bf16[64,16,128]{2,1,0:T(8,128)(2,1)}, bf16[64,16,128]{2,1,0:T(8,128)(2,1)S(1)}, u32[]{:S(2)}) copy-start(bf16[64,16,128]{2,1,0:T(8,128)(2,1)S(1)} %collective-permute-done.10.bottom) | copy-start | bytes 786436
  101.6 34.0 %collective-permute-start.11 = (bf16[10,16,128]{2,1,0:T(8,128)(2,1)S(1)}, bf16[10,16,128]{2,1,0:T(8,128)(2,1)S(1)}, u32[]{:S(2)}, u32[]{:S(2)}) collective-permute-start(bf16[10,16,128]{2,1,0:T(8,128)(2,1)S(1)} %pad_maximum_fusion.2), channel_id=1, source_target_pairs={{0,1},{1,2},{2,3},{3,0},{4,5},{5,6},{6,7},{7,4},{8,9},{9,10},{10,1... | collective-permute-start | bytes 122888 | tf_op jit(solution)/shard_map/ppermute | solution.py:456
  127.8 7.7 %collective-permute-start.12 = (bf16[10,16,128]{2,1,0:T(8,128)(2,1)S(1)}, bf16[10,16,128]{2,1,0:T(8,128)(2,1)S(1)}, u32[]{:S(2)}, u32[]{:S(2)}) collective-permute-start(bf16[10,16,128]{2,1,0:T(8,128)(2,1)S(1)} %pad_maximum_fusion.3), channel_id=1, source_target_pairs={{1,0},{2,1},{3,2},{0,3},{5,4},{6,5},{7,6},{4,7},{9,8},{10,9},{11,1... | collective-permute-start | bytes 122888 | tf_op jit(solution)/shard_map/ppermute | solution.py:457
  128.1 0.8 copy-start.11
  (5 other events, 3.3 us)

commit v2 on v1

v2 whole, which is shorter than its diff:
```python
import functools

import jax
import jax.numpy as jnp
from jax import lax
from jax.experimental import pallas as pl
from jax.experimental.pallas import tpu as pltpu
from jax.sharding import PartitionSpec as P

HEADS = 8
CH = 128
HEAD_DIM = CH // HEADS
MEM = 16
ROWS = 8
COLS = 64
EDGE = 4
MID = COLS - 2 * EDGE
WIDTH = COLS + 2
SIDE = EDGE + 1
BF = jnp.bfloat16
F32 = jnp.float32
WEIGHT = 0.35
COST_SECOND, COST_MIX12, COST_MIX56, COST_OUTER = 10, 10, 1, 10
VMEM_LIMIT = 24 * 1024 * 1024
FIRST_VMEM = 59 * 1024 * 1024


def call(body, out_shape, scratch, micros, name, vmem=VMEM_LIMIT, aliases=None, in_specs=None, out_specs=None, grid=()):
    return pl.pallas_call(
        body,
        out_shape=out_shape,
        scratch_shapes=scratch,
        in_specs=in_specs,
        out_specs=out_specs,
        grid=grid,
        input_output_aliases=aliases or {},
        compiler_params=pltpu.CompilerParams(vmem_limit_bytes=vmem),
        cost_estimate=pl.CostEstimate(
            flops=int(micros * WEIGHT * 1e9), bytes_accessed=1024, transcendentals=0
        ),
        name=name,
    )


def bf(*shape):
    return jax.ShapeDtypeStruct(shape, BF)


VM = pl.BlockSpec(memory_space=pltpu.VMEM)


def pair_weights(w_ref, wide):
    zero = jnp.zeros((3 * CH, CH), BF)
    wide[0 : 9 * CH, 0:CH] = w_ref[...]
    wide[9 * CH : 12 * CH, 0:CH] = zero
    wide[0 : 3 * CH, CH : 2 * CH] = zero
    wide[3 * CH : 12 * CH, CH : 2 * CH] = w_ref[...]


def taps(load, rows, first, width):
    return jnp.concatenate(
        [load(r, first + j, width).reshape(width * MEM, CH) for r in rows for j in range(3)],
        axis=-1,
    )


def head_of(summed, bias, gain):
    values = summed + bias
    hidden = (values * 0.5 * (1.0 + lax.erf(values * 0.7071067811865476))).astype(BF)
    wide = hidden.astype(F32)
    centre = jnp.mean(wide, axis=-1, keepdims=True)
    moved = wide - centre
    spread = jnp.mean(moved * moved, axis=-1, keepdims=True)
    normed = (moved * lax.rsqrt(spread + 1e-05) * gain).astype(BF)
    return hidden, normed


def finish(acc, count, lane, bias, gain, hid_ref, norm_ref, start):
    part = count // 2

    def body(t, _):
        rows = pl.ds(pl.multiple_of(t * part * MEM, MEM), part * MEM)
        hidden, normed = head_of(acc[rows, lane : lane + CH], bias, gain)
        hid_ref[pl.ds(start + t * part, part)] = hidden.reshape(part, MEM, CH)
        norm_ref[pl.ds(start + t * part, part)] = normed.reshape(part, MEM, CH)
        return 0

    lax.fori_loop(0, 2, body, 0)


def first_body(
    ens_ref, w_ref, bias_ref, gain_ref, x_ref, col0, col63, hid12, norm12,
    wide, acc, held, turned, weights, bias, gain, in_sems, out_sems,
):
    rows = [
        pltpu.make_async_copy(ens_ref.at[:, row], held.at[row], in_sems.at[row])
        for row in range(ROWS)
    ]
    others = [
        pltpu.make_async_copy(src, dst, in_sems.at[ROWS + k])
        for k, (src, dst) in enumerate(((w_ref, weights), (bias_ref, bias), (gain_ref, gain)))
    ]
    for copy in rows[:4] + others + rows[4:]:
        copy.start()
    outs = []
    for row in range(ROWS):
        rows[row].wait()
        turned[row] = jnp.swapaxes(held[row], 0, 1)
        outs.append(pltpu.make_async_copy(turned.at[row], x_ref.at[row], out_sems.at[row]))
        outs[row].start()
    for copy in others:
        copy.wait()
    pair_weights(weights, wide)
    col0[...] = turned[:, 0:2]
    col63[...] = turned[:, COLS - 2 : COLS]
    load = lambda r, c, n: turned[r, c : c + n]
    middle(load, 1, ((hid12, norm12, 0), (hid12, norm12, MID)), wide, acc, bias[...], gain[...])
    for copy in outs:
        copy.wait()


def middle(load, top, outs, wide, acc, bias, gain):
    acc[...] = jnp.dot(
        taps(load, range(top - 1, top + 3), EDGE - 1, MID), wide[...], preferred_element_type=F32
    )
    for k, (hid, norm, start) in enumerate(outs):
        finish(acc, MID, k * CH, bias, gain, hid, norm, start)


def second_body(x_ref, w_ref, bias_ref, gain_ref, hid34, norm34, hid56, norm56, wide, acc):
    pair_weights(w_ref, wide)
    load = lambda r, c, n: x_ref[r, c : c + n]
    bias, gain = bias_ref[...], gain_ref[...]
    for top, hid, norm in ((3, hid34, norm34), (5, hid56, norm56)):
        middle(load, top, ((hid, norm, 0), (hid, norm, MID)), wide, acc, bias, gain)


def edge_body(
    x_ref, above, below, left, right, w_ref, bias_ref, gain_ref, hid, norm, wide, acc, pad
):
    pair_weights(w_ref, wide)
    pad[0] = above[...]
    pad[ROWS + 1] = below[...]
    pad[1 : ROWS + 1, 0:2] = left[...]
    pad[1 : ROWS + 1, COLS + 2 :] = right[...]
    pad[1 : ROWS + 1, 2 : COLS + 2] = x_ref[...]
    load = lambda r, c, n: pad[r, c : c + n]
    bias, gain = bias_ref[...], gain_ref[...]
    for k, row in enumerate((0, 7)):
        acc[...] = jnp.dot(
            taps(load, range(row, row + 3), 0, WIDTH), w_ref[...], preferred_element_type=F32
        )
        finish(acc, WIDTH, 0, bias, gain, hid, norm, k * WIDTH)
    sides = [
        taps(load, range(row, row + 4), first, SIDE)
        for row in (1, 3, 5)
        for first in (0, WIDTH - SIDE)
    ]
    both = jnp.dot(jnp.concatenate(sides, axis=0), wide[...], preferred_element_type=F32)
    count = 3 * 2 * SIDE * MEM
    acc[0:count] = both[:, 0:CH]
    acc[count : 2 * count] = both[:, CH : 2 * CH]
    finish(acc, 2 * 3 * 2 * SIDE, 0, bias, gain, hid, norm, 2 * WIDTH)


def mix(
    count, start, own_ref, far_ref, hid_ref, wq_ref, wk_ref, wv_ref, wo_ref, upd_ref,
    q_scr, k_scr, v_scr, ctx, s_scr, p_scr,
):
    own = own_ref[start : start + count].reshape(count * MEM, CH)
    far = far_ref[start : start + count].reshape(count * MEM, CH)
    dot = functools.partial(jnp.dot, preferred_element_type=F32)
    points = lambda cells: cells.astype(BF).reshape(count, MEM, CH)
    both = jnp.concatenate([wk_ref[...], wv_ref[...]], axis=1)
    near = dot(own, jnp.concatenate([both, wq_ref[...]], axis=1))
    k_scr[:, 0:MEM] = points(near[:, 0:CH])
    v_scr[:, 0:MEM] = points(near[:, CH : 2 * CH])
    q_scr[...] = points(near[:, 2 * CH :])
    other = dot(far, both)
    k_scr[:, MEM:] = points(other[:, 0:CH])
    v_scr[:, MEM:] = points(other[:, CH:])

    rows = lax.broadcasted_iota(jnp.int32, (CH, CH), 0) // HEAD_DIM
    lanes = lax.broadcasted_iota(jnp.int32, (CH, CH), 1) // HEAD_DIM
    own_head = jnp.where(rows == lanes, 1.0, 0.0).astype(BF)
    lane16 = lax.broadcasted_iota(jnp.int32, (MEM, CH), 1) // HEAD_DIM
    factor = 1.4426950408889634 / HEAD_DIM**0.5
    group = group_of(count)
    steps = count // group
    blank = jnp.zeros((2 * MEM, CH), BF)

    def score(t):
        for u in range(group):
            p = t * group + u
            heads = jnp.concatenate([q_scr[p]] * HEADS, axis=0) * own_head
            s_scr[t % 2, u] = lax.dot_general(
                k_scr[p], heads, (((1,), (1,)), ((), ())), preferred_element_type=F32
            )

    def weigh(t):
        for g in range(group // 4):
            probs = []
            for v in range(4):
                scores = s_scr[t % 2, g * 4 + v]
                top = jnp.max(scores, axis=0, keepdims=True)
                grown = jnp.exp2((scores - top) * factor)
                total = jnp.sum(grown, axis=0, keepdims=True)
                probs.append(grown * (1.0 / total))
            p_scr[t % 2, g] = jnp.concatenate(probs, axis=0).T.astype(BF)

    def gather(t):
        for g in range(group // 4):
            first = t * group + g * 4
            values = [
                jnp.concatenate([v_scr[first + v] if w == v else blank for w in range(4)], axis=1)
                for v in range(4)
            ]
            mixed = dot(p_scr[t % 2, g], jnp.concatenate(values, axis=0))
            for v in range(4):
                out = mixed[0:MEM, v * CH : (v + 1) * CH]
                for h in range(1, HEADS):
                    out = jnp.where(
                        lane16 == h, mixed[h * MEM : (h + 1) * MEM, v * CH : (v + 1) * CH], out
                    )
                ctx[first + v] = out.astype(BF)

    score(0)
    score(1)
    weigh(0)

    def body(t, _):
        gather(t - 2)
        weigh(t - 1)
        score(t)
        return 0

    lax.fori_loop(2, steps, body, 0)
    weigh(steps - 1)
    gather(steps - 2)
    gather(steps - 1)
    attended = dot(ctx[...].reshape(count * MEM, CH), wo_ref[...]).astype(BF)
    upd_ref[...] = (
        hid_ref[start : start + count].astype(F32) + attended.astype(F32).reshape(count, MEM, CH)
    ).astype(BF)


def group_of(count):
    return 16 if count % 16 == 0 else 8


def mix_scratch(count):
    group = group_of(count)
    return [
        pltpu.VMEM((count, MEM, CH), BF),
        pltpu.VMEM((count, 2 * MEM, CH), BF),
        pltpu.VMEM((count, 2 * MEM, CH), BF),
        pltpu.VMEM((count, MEM, CH), BF),
        pltpu.VMEM((2, group, 2 * MEM, CH), F32),
        pltpu.VMEM((2, group // 4, CH, CH), BF),
    ]


def put_edge(pad, edge):
    pad[1] = edge[0:WIDTH]
    pad[ROWS] = edge[WIDTH : 2 * WIDTH]
    half = 3 * 2 * SIDE
    for k in range(2):
        for i, row in enumerate((1, 3, 5)):
            base = 2 * WIDTH + k * half + i * 2 * SIDE
            pad[row + k + 1, 0:SIDE] = edge[base : base + SIDE]
            pad[row + k + 1, WIDTH - SIDE : WIDTH] = edge[base + SIDE : base + 2 * SIDE]


def second_conv(pad, row, w, bias, out_ref):
    load = lambda r, c, n: pad[r, c : c + n]
    both = jnp.dot(taps(load, range(row, row + 4), 0, COLS), w, preferred_element_type=F32)
    for k in range(2):
        own = pad[row + k + 1, 1 : COLS + 1].reshape(COLS * MEM, CH).astype(F32)
        cells = (own + both[:, k * CH : (k + 1) * CH] + bias).astype(BF)
        out_ref[:, k] = jnp.swapaxes(cells.reshape(COLS, MEM, CH), 0, 1)


def outer_body(
    edge, upd12, upd56, top, bottom, w_ref, bias_ref, out_ref, wide, pad
):
    step = pl.program_id(0)

    @pl.when(step == 0)
    def _():
        pair_weights(w_ref, wide)
        pad[0] = top[...]
        pad[ROWS + 1] = bottom[...]
        put_edge(pad, edge)
        for k in range(2):
            pad[2 + k, EDGE + 1 : EDGE + 1 + MID] = upd12[k * MID : (k + 1) * MID]
            pad[6 + k, EDGE + 1 : EDGE + 1 + MID] = upd56[k * MID : (k + 1) * MID]
        second_conv(pad, 0, wide[...], bias_ref[...], out_ref)

    @pl.when(step == 1)
    def _():
        second_conv(pad, 6, wide[...], bias_ref[...], out_ref)


def last_body(
    own_ref, far_ref, hid_ref, wq_ref, wk_ref, wv_ref, wo_ref,
    edge, upd12, upd56, w_ref, bias_ref, _, out_ref,
    q_scr, k_scr, v_scr, ctx, s_scr, p_scr, upd34, wide, pad,
):
    step = pl.program_id(0)

    @pl.when(step == 0)
    def _():
        mix(
            2 * MID, 0, own_ref, far_ref, hid_ref, wq_ref, wk_ref, wv_ref, wo_ref, upd34,
            q_scr, k_scr, v_scr, ctx, s_scr, p_scr,
        )
        pair_weights(w_ref, wide)
        put_edge(pad, edge)
        mid = slice(EDGE + 1, EDGE + 1 + MID)
        for k in range(2):
            pad[2 + k, mid] = upd12[k * MID : (k + 1) * MID]
            pad[4 + k, mid] = upd34[k * MID : (k + 1) * MID]
            pad[6 + k, mid] = upd56[k * MID : (k + 1) * MID]
        second_conv(pad, 2, wide[...], bias_ref[...], out_ref)

    @pl.when(step == 1)
    def _():
        second_conv(pad, 4, wide[...], bias_ref[...], out_ref)


WIDE = pltpu.VMEM((12 * CH, 2 * CH), BF)
PAD = pltpu.VMEM((ROWS + 2, COLS + 2, MEM, CH), BF)
ACC_MID = pltpu.VMEM((MID * MEM, 2 * CH), F32)
ACC1 = pltpu.VMEM((WIDTH * MEM, CH), F32)
PAD1 = pltpu.VMEM((ROWS + 2, COLS + 4, MEM, CH), BF)
EDGES = 2 * WIDTH + 6 * 2 * SIDE


def half_rows(which):
    return pl.BlockSpec((MEM, 4, COLS, CH), lambda i: (0, which, 0, 0))


def run_first(ens, w, bias, gain):
    hbm = pl.BlockSpec(memory_space=pltpu.HBM)
    return call(
        first_body,
        (bf(ROWS, COLS, MEM, CH),) + (bf(ROWS, 2, MEM, CH),) * 2 + (bf(2 * MID, MEM, CH),) * 2,
        [
            WIDE,
            ACC_MID,
            pltpu.VMEM((ROWS, MEM, COLS, CH), BF),
            pltpu.VMEM((ROWS, COLS, MEM, CH), BF),
            pltpu.VMEM((9 * CH, CH), BF),
            pltpu.VMEM((1, CH), F32),
            pltpu.VMEM((1, CH), F32),
            pltpu.SemaphoreType.DMA((ROWS + 3,)),
            pltpu.SemaphoreType.DMA((ROWS,)),
        ],
        0.1,
        "conv_rows12",
        vmem=FIRST_VMEM,
        in_specs=[hbm] * 4,
        out_specs=[hbm] + [VM] * 4,
    )(ens, w, bias, gain)


def run_edge(x, rim, w, bias, gain):
    return call(
        edge_body,
        (bf(EDGES, MEM, CH),) * 2,
        [WIDE, ACC1, PAD1],
        0.1,
        "conv_edges",
        in_specs=[VM] * 8,
        out_specs=[VM] * 2,
    )(x, *rim, w, bias, gain)


def run_second(x, w, bias, gain):
    return call(
        second_body,
        (bf(2 * MID, MEM, CH),) * 4,
        [WIDE, ACC_MID],
        COST_SECOND,
        "conv_rows3456",
        in_specs=[VM] * 4,
        out_specs=[VM] * 4,
    )(x, w, bias, gain)


def run_mix(count, start, micros, own, far, hid, mats):
    return call(
        functools.partial(mix, count, start),
        bf(count, MEM, CH),
        mix_scratch(count),
        micros,
        f"mix{count}",
        in_specs=[VM] * 7,
        out_specs=VM,
    )(own, far, hid, *mats)


def mix_edges(
    own_ref, far_ref, hid_ref, wq_ref, wk_ref, wv_ref, wo_ref, upd_ref, top, bottom, *scratch
):
    mix(EDGES, 0, own_ref, far_ref, hid_ref, wq_ref, wk_ref, wv_ref, wo_ref, upd_ref, *scratch)
    top[...] = upd_ref[0:WIDTH]
    bottom[...] = upd_ref[WIDTH : 2 * WIDTH]


def run_mix_edges(own, far, hid, mats):
    return call(
        mix_edges,
        (bf(EDGES, MEM, CH),) + (bf(WIDTH, MEM, CH),) * 2,
        mix_scratch(EDGES),
        0.1,
        "mix_edges",
        in_specs=[VM] * 7,
        out_specs=[VM] * 3,
    )(own, far, hid, *mats)


def row_pair(index):
    return pl.BlockSpec((MEM, 2, COLS, CH), index)


def run_outer(edge, upd12, upd56, rim, w, bias):
    return call(
        outer_body,
        bf(MEM, ROWS, COLS, CH),
        [WIDE, PAD],
        COST_OUTER,
        "conv2_outer",
        in_specs=[VM] * 7,
        out_specs=row_pair(lambda i: (0, 3 * i, 0, 0)),
        grid=(2,),
    )(edge, upd12, upd56, *rim, w, bias)


def run_last(own, far, hid, mats, edge, upd12, upd56, w, bias, partial):
    return call(
        last_body,
        bf(MEM, ROWS, COLS, CH),
        mix_scratch(2 * MID) + [pltpu.VMEM((2 * MID, MEM, CH), BF), WIDE, PAD],
        7.3,
        "mix_conv2_inner",
        aliases={12: 0},
        in_specs=[VM] * 12 + [pl.BlockSpec(memory_space=pl.ANY)],
        out_specs=row_pair(lambda i: (0, i + 1, 0, 0)),
        grid=(2,),
    )(own, far, hid, *mats, edge, upd12, upd56, w, bias, partial)


def swap(cells):
    return lax.ppermute(cells, "mem", [(0, 1), (1, 0)])


def lat_rims(top_row, bottom_row):
    count = lax.axis_size("lat")
    above = lax.ppermute(bottom_row, "lat", [(i, i + 1) for i in range(count - 1)])
    below = lax.ppermute(top_row, "lat", [(i + 1, i) for i in range(count - 1)])
    return above, below


def lon_rims(left_col, right_col):
    count = lax.axis_size("lon")
    left = lax.ppermute(right_col, "lon", [(i, (i + 1) % count) for i in range(count)])
    right = lax.ppermute(left_col, "lon", [((i + 1) % count, i) for i in range(count)])
    return left, right


def after(value, *others):
    return lax.optimization_barrier((value, *others))[0]


def shards(ensemble, w_conv1, bias1, gain, w_query, w_key, w_value, w_out, w_conv2, bias2):
    w1 = w_conv1.reshape(9 * CH, CH)
    w2 = w_conv2.reshape(9 * CH, CH)
    b1, g1, b2 = bias1.reshape(1, CH), gain.reshape(1, CH), bias2.reshape(1, CH)
    mats = (w_query, w_key, w_value, w_out)

    x, col0, col63, hid12, norm12 = run_first(ensemble, w1, b1, g1)
    left, right = lon_rims(col0, col63)
    far12 = swap(norm12)
    row = lambda r: jnp.concatenate([left[r], x[r], right[r]], axis=0)
    above, below = lat_rims(row(0), row(ROWS - 1))
    hid34, norm34, hid56, norm56 = run_second(after(x, row(0)), w1, b1, g1)
    hid_e, norm_e = run_edge(after(x, norm56), (above, below, left, right), w1, b1, g1)
    far_e = swap(norm_e)
    upd12 = run_mix(2 * MID, 0, COST_MIX12, after(norm12, norm_e), far12, hid12, mats)
    far56 = swap(after(norm56, norm_e))
    upd_e, row0, row7 = run_mix_edges(after(norm_e, upd12), far_e, hid_e, mats)
    above2, below2 = lat_rims(row0, row7)
    upd56 = run_mix(2 * MID, 0, COST_MIX56, after(norm56, upd_e), far56, hid56, mats)
    far34 = swap(after(norm34, far_e))
    partial = run_outer(upd_e, upd12, upd56, (above2, below2), w2, b2)
    return run_last(norm34, far34, hid34, mats, upd_e, upd12, upd56, w2, b2, partial)


def solution(mesh):
    return jax.shard_map(
        shards,
        mesh=mesh,
        in_specs=(P("mem", "lat", "lon", None), P(), P(), P(), P(), P(), P(), P(), P(), P()),
        out_specs=P("mem", "lat", "lon", None),
        check_vma=False,
    )
```

time: 151 us -> 124 us (0.82); the launches traced: 149 us -> 124 us
  starting transfers between devices: 54.5 us -> 31.4 us
  waiting for transfers between devices: 27 us -> 48.9 us
  Pallas kernels: 59.9 us -> 42.3 us
  local copies, waits for them, and re-layouts: 7.32 us -> 1.13 us
    ppermute x5 -> x4, waiting for transfers between devices: 8.84 us -> 48.9 us  [swap(): return lax.ppermute(cells, 'mem', [(0, 1), (1, 0)])]
    ppermute x2 -> x1, starting transfers between devices: 27 us -> 2.54 us  [lon_rims(): lax.ppermute(right_col, 'lon', [(i, (i + 1) % count) for i in range(count)])]
    pallas_call x9 -> x8, Pallas kernels: 59.9 us -> 42.3 us  [the longest x2 8.96 us: run_mix(): call(functools.partial(mix, count, start), bf(count, MEM, CH), mix_scratc...]
    ppermute x2 -> x1, waiting for transfers between devices: 17 us -> 0.01 us  [lon_rims(): lax.ppermute(right_col, 'lon', [(i, (i + 1) % count) for i in range(count)])]
    unnamed x34 -> x24, local copies, waits for them, and re-layouts: 5.07 us -> 0.06 us
    ppermute x5 -> x4, starting transfers between devices: 12.5 us -> 14.2 us  [swap(): return lax.ppermute(cells, 'mem', [(0, 1), (1, 0)])]
    ppermute x2, starting transfers between devices: 8.14 us -> 6.49 us  [lat_rims(): lax.ppermute(bottom_row, 'lat', [(i, i + 1) for i in range(count - 1)])]
  transfers between devices with their start and end apart: 13 -> 10, of which waited for: 4 -> 2; matrix products, arithmetic and copies ran while one was open for 1% -> 1% of each run, Pallas kernels for 32% -> 24%
where the time goes in v2:
time: 124 us
  waiting for transfers between devices  48.9 us (39%)
  Pallas kernels  42.3 us (34%)
  starting transfers between devices  31.4 us (25%)
    ppermute x4, waiting for transfers between devices, swap(): return lax.ppermute(cells, 'mem', [(0, 1), (1, 0)])  48.9 us
    ppermute x4, starting transfers between devices, swap(): return lax.ppermute(cells, 'mem', [(0, 1), (1, 0)])  14.2 us
    pallas_call x2, Pallas kernels, run_mix(): call(functools.partial(mix, count, start), bf(count, MEM, CH), mix_scratc...  8.96 us
    pallas_call x1, Pallas kernels, run_mix_edges(): call(mix_edges, (bf(EDGES, MEM, CH),) + (bf(WIDTH, MEM, CH),) * 2, mix_sc...  7.7 us
    pallas_call x1, Pallas kernels, run_last(): call(last_body, bf(MEM, ROWS, COLS, CH), mix_scratch(2 * MID) + [pltpu.VM...  7.41 us
    ppermute x2, starting transfers between devices, lat_rims(): lax.ppermute(bottom_row, 'lat', [(i, i + 1) for i in range(count - 1)])  6.49 us
    ppermute x2, starting transfers between devices, lat_rims(): below = lax.ppermute(top_row, 'lat', [(i + 1, i) for i in range(count - 1)])  5.35 us
    pallas_call x1, Pallas kernels, run_first(): call(first_body, (bf(ROWS, COLS, MEM, CH),) + (bf(ROWS, 2, MEM, CH),) * 2...  5.2 us
  transfers between devices with their start and end apart: 10, of which 2 were waited for; matrix products, arithmetic and copies ran while one was open for 1% of the time, Pallas kernels for 24%

profile of v2, /device:TPU:1, one launch (start us, length us, event | category | flops | bytes accessed | tf_op | source)
XLA Modules:
  0.0 124.2 jit_solution(4383789692902955087)
XLA Ops:
  0.0 5.2 %conv_rows12.1 = (bf16[8,64,16,128]{3,2,1,0:T(8,128)(2,1)}, bf16[8,2,16,128]{3,2,1,0:T(8,128)(2,1)}, bf16[8,2,16,128]{3,2,1,0:T(8,128)(2,1)}, bf16[112,16,128]{2,1,0:T(8,128)(2,1)}, bf16[112,16,128]{2,1,0:T(8,128)(2,1)}) custom-call(bf16[16,8,64,128]{3,2,1,0:T(8,128)(2,1)} %ens_ref.1, bf16[1152,128]{1,0:T(8,128)(2,1)} %bitcast.17, f32[1,128]{1,0:T(1,128)} %bitcast.20, ...), custom_call_target="tpu_custom_call" | custom-call | flops 35000000 | bytes 1024 | tf_op jit(solution)/shard_map/conv_rows12/pallas_call | solution.py:345
  5.2 0.0 copy-start
  5.2 2.5 %collective-permute-start = (bf16[8,2,16,128]{3,2,1,0:T(8,128)(2,1)}, bf16[8,2,16,128]{3,2,1,0:T(8,128)(2,1)S(1)}, u32[]{:S(2)}, u32[]{:S(2)}) collective-permute-start(bf16[8,2,16,128]{3,2,1,0:T(8,128)(2,1)} %get-tuple-element.27), channel_id=1, source_target_pairs={{0,1},{1,2},{2,3},{3,0},{4,5},{5,6},{6,7},{7,4},{8,9},{9,10},{10,1... | collective-permute-start | bytes 196616 | tf_op jit(solution)/shard_map/ppermute | solution.py:467
  7.8 2.8 %collective-permute-start.1 = (bf16[8,2,16,128]{3,2,1,0:T(8,128)(2,1)}, bf16[8,2,16,128]{3,2,1,0:T(8,128)(2,1)S(1)}, u32[]{:S(2)}, u32[]{:S(2)}) collective-permute-start(bf16[8,2,16,128]{3,2,1,0:T(8,128)(2,1)} %get-tuple-element.28), channel_id=1, source_target_pairs={{1,0},{2,1},{3,2},{0,3},{5,4},{6,5},{7,6},{4,7},{9,8},{10,9},{11,1... | collective-permute-start | bytes 196616 | tf_op jit(solution)/shard_map/ppermute | solution.py:468
  10.6 5.7 %collective-permute-start.6 = (bf16[112,16,128]{2,1,0:T(8,128)(2,1)}, bf16[112,16,128]{2,1,0:T(8,128)(2,1)S(1)}, u32[]{:S(2)}, u32[]{:S(2)}) collective-permute-start(bf16[112,16,128]{2,1,0:T(8,128)(2,1)} %get-tuple-element.37.own_ref), channel_id=1, source_target_pairs={{0,128},{128,0},{1,129},{129,1},{2,130},{130,2},{3,131},{131,3},{4... | collective-permute-start | bytes 1376264 | tf_op jit(solution)/shard_map/ppermute | solution.py:455
  16.3 1.1 slice_bitcast_fusion
  17.5 3.4 %collective-permute-start.3 = (bf16[68,16,128]{2,1,0:T(8,128)(2,1)S(1)}, bf16[68,16,128]{2,1,0:T(8,128)(2,1)S(1)}, u32[]{:S(2)}, u32[]{:S(2)}) collective-permute-start(bf16[68,16,128]{2,1,0:T(8,128)(2,1)S(1)} %pad_maximum_fusion), channel_id=1, source_target_pairs={{4,0},{8,4},{12,8},{16,12},{20,16},{24,20},{28,24},{32,28},{36,32}... | collective-permute-start | bytes 835592 | tf_op jit(solution)/shard_map/ppermute | solution.py:461
  20.9 3.0 %collective-permute-start.2 = (bf16[68,16,128]{2,1,0:T(8,128)(2,1)S(1)}, bf16[68,16,128]{2,1,0:T(8,128)(2,1)S(1)}, u32[]{:S(2)}, u32[]{:S(2)}) collective-permute-start(bf16[68,16,128]{2,1,0:T(8,128)(2,1)S(1)} %pad_maximum_fusion.1), channel_id=1, source_target_pairs={{0,4},{4,8},{8,12},{12,16},{16,20},{20,24},{24,28},{28,32},{32,36}... | collective-permute-start | bytes 835592 | tf_op jit(solution)/shard_map/ppermute | solution.py:460
  24.0 5.1 %conv_rows3456.1 = (bf16[112,16,128]{2,1,0:T(8,128)(2,1)S(1)}, bf16[112,16,128]{2,1,0:T(8,128)(2,1)S(1)}, bf16[112,16,128]{2,1,0:T(8,128)(2,1)S(1)}, bf16[112,16,128]{2,1,0:T(8,128)(2,1)S(1)}) custom-call(bf16[8,64,16,128]{3,2,1,0:T(8,128)(2,1)S(1)} %copy-done, bf16[1152,128]{1,0:T(8,128)(2,1)S(1)} %bitcast.18, f32[1,128]{1,0:T(1,128)S(1)} %bitcast.21, ...), custom_call_target="tpu_custom_call" | custom-call | flops 3500000000 | bytes 1024 | tf_op jit(solution)/shard_map/conv_rows3456/pallas_call | solution.py:380
  29.1 0.0 copy-start.2
  29.2 0.0 copy-start.3
  29.2 4.9 %conv_edges.1 = (bf16[192,16,128]{2,1,0:T(8,128)(2,1)S(1)}, bf16[192,16,128]{2,1,0:T(8,128)(2,1)S(1)}) custom-call(bf16[8,64,16,128]{3,2,1,0:T(8,128)(2,1)S(1)} %copy-done, bf16[68,16,128]{2,1,0:T(8,128)(2,1)S(1)} %collective-permute-done.2.above, bf16[68,16,128]{2,1,0:T(8,128)(2,1)S(1)} %collective-permute-done.3.below, ...), custom_call_target="tpu_custom_call" | custom-call | flops 35000000 | bytes 1024 | tf_op jit(solution)/shard_map/conv_edges/pallas_call | solution.py:368
  34.1 4.2 %collective-permute-start.4 = (bf16[192,16,128]{2,1,0:T(8,128)(2,1)S(1)}, bf16[192,16,128]{2,1,0:T(8,128)(2,1)S(1)}, u32[]{:S(2)}, u32[]{:S(2)}) collective-permute-start(bf16[192,16,128]{2,1,0:T(8,128)(2,1)S(1)} %get-tuple-element.39.own_ref), channel_id=1, source_target_pairs={{0,128},{128,0},{1,129},{129,1},{2,130},{130,2},{3,131},{131,3},{4... | collective-permute-start | bytes 2359304 | tf_op jit(solution)/shard_map/ppermute | solution.py:455
  38.3 1.3 %collective-permute-start.7 = (bf16[112,16,128]{2,1,0:T(8,128)(2,1)S(1)}, bf16[112,16,128]{2,1,0:T(8,128)(2,1)S(1)}, u32[]{:S(2)}, u32[]{:S(2)}) collective-permute-start(bf16[112,16,128]{2,1,0:T(8,128)(2,1)S(1)} %get-tuple-element.43.own_ref), channel_id=1, source_target_pairs={{0,128},{128,0},{1,129},{129,1},{2,130},{130,2},{3,131},{131,3},{4... | collective-permute-start | bytes 1376264 | tf_op jit(solution)/shard_map/ppermute | solution.py:455
  39.6 4.5 %mix112.2.upd12 = bf16[112,16,128]{2,1,0:T(8,128)(2,1)S(1)} custom-call(bf16[112,16,128]{2,1,0:T(8,128)(2,1)S(1)} %copy-done.9, bf16[112,16,128]{2,1,0:T(8,128)(2,1)S(1)} %collective-permute-done.6.far_ref, bf16[112,16,128]{2,1,0:T(8,128)(2,1)S(1)} %copy-done.8, bf16[128,128]{1,0:T(8,128)(2,1)S(1)} %copy-done.2, bf16[128,128]{1,0:T(8,128)(2,1)S(1)} %copy-done.3, ...), custom_call_target="tpu_custom_call" | custom-call | flops 3500000000 | bytes 1024 | tf_op jit(solution)/shard_map/mix112/pallas_call | solution.py:392
  44.1 40.6 %collective-permute-done.4.far_ref = bf16[192,16,128]{2,1,0:T(8,128)(2,1)S(1)} collective-permute-done((bf16[192,16,128]{2,1,0:T(8,128)(2,1)S(1)}, bf16[192,16,128]{2,1,0:T(8,128)(2,1)S(1)}, u32[]{:S(2)}, u32[]{:S(2)}) %collective-permute-start.4) | collective-permute-done | bytes 786464 | tf_op jit(solution)/shard_map/ppermute | solution.py:455
  84.7 7.7 %mix_edges.1 = (bf16[192,16,128]{2,1,0:T(8,128)(2,1)S(1)}, bf16[66,16,128]{2,1,0:T(8,128)(2,1)S(1)}, bf16[66,16,128]{2,1,0:T(8,128)(2,1)S(1)}) custom-call(bf16[192,16,128]{2,1,0:T(8,128)(2,1)S(1)} %get-tuple-element.39.own_ref, bf16[192,16,128]{2,1,0:T(8,128)(2,1)S(1)} %collective-permute-done.4.far_ref, ...), custom_call_target="tpu_custom_call" | custom-call | flops 35000000 | bytes 1024 | tf_op jit(solution)/shard_map/mix_edges/pallas_call | solution.py:412
  92.4 3.5 %collective-permute-start.8 = (bf16[66,16,128]{2,1,0:T(8,128)(2,1)S(1)}, bf16[66,16,128]{2,1,0:T(8,128)(2,1)S(1)}, u32[]{:S(2)}, u32[]{:S(2)}) collective-permute-start(bf16[66,16,128]{2,1,0:T(8,128)(2,1)S(1)} %get-tuple-element.45), channel_id=1, source_target_pairs={{0,4},{4,8},{8,12},{12,16},{16,20},{20,24},{24,28},{28,32},{32,36}... | collective-permute-start | bytes 811016 | tf_op jit(solution)/shard_map/ppermute | solution.py:460
  95.9 1.9 %collective-permute-start.9 = (bf16[66,16,128]{2,1,0:T(8,128)(2,1)S(1)}, bf16[66,16,128]{2,1,0:T(8,128)(2,1)S(1)}, u32[]{:S(2)}, u32[]{:S(2)}) collective-permute-start(bf16[66,16,128]{2,1,0:T(8,128)(2,1)S(1)} %get-tuple-element.46), channel_id=1, source_target_pairs={{4,0},{8,4},{12,8},{16,12},{20,16},{24,20},{28,24},{32,28},{36,32}... | collective-permute-start | bytes 811016 | tf_op jit(solution)/shard_map/ppermute | solution.py:461
  97.8 3.0 %collective-permute-start.5 = (bf16[112,16,128]{2,1,0:T(8,128)(2,1)S(1)}, bf16[112,16,128]{2,1,0:T(8,128)(2,1)S(1)}, u32[]{:S(2)}, u32[]{:S(2)}) collective-permute-start(bf16[112,16,128]{2,1,0:T(8,128)(2,1)S(1)} %get-tuple-element.34.own_ref), channel_id=1, source_target_pairs={{0,128},{128,0},{1,129},{129,1},{2,130},{130,2},{3,131},{131,3},{4... | collective-permute-start | bytes 1376264 | tf_op jit(solution)/shard_map/ppermute | solution.py:455
  100.9 4.5 %mix112.3.upd56 = bf16[112,16,128]{2,1,0:T(8,128)(2,1)S(1)} custom-call(bf16[112,16,128]{2,1,0:T(8,128)(2,1)S(1)} %get-tuple-element.43.own_ref, bf16[112,16,128]{2,1,0:T(8,128)(2,1)S(1)} %collective-permute-done.7.far_ref, bf16[112,16,128]{2,1,0:T(8,128)(2,1)S(1)} %get-tuple-element.44.hid_ref, bf16[128,128]{1,0:T(8,128)(2,1)S(1)} %copy-done.2, ...), custom_call_target="tpu_custom_call" | custom-call | flops 350000000 | bytes 1024 | tf_op jit(solution)/shard_map/mix112/pallas_call | solution.py:392
  105.4 3.1 %conv2_outer.1._ = bf16[16,8,64,128]{3,2,1,0:T(8,128)(2,1)} custom-call(bf16[192,16,128]{2,1,0:T(8,128)(2,1)S(1)} %get-tuple-element.41.edge, bf16[112,16,128]{2,1,0:T(8,128)(2,1)S(1)} %mix112.2.upd12, bf16[112,16,128]{2,1,0:T(8,128)(2,1)S(1)} %mix112.3.upd56, bf16[66,16,128]{2,1,0:T(8,128)(2,1)S(1)} %collective-permute-done.8.top, ...), custom_call_target="tpu_custom_call" | custom-call | flops 3500000000 | bytes 1024 | tf_op jit(solution)/shard_map/conv2_outer/pallas_call | solution.py:428
  108.5 8.2 %collective-permute-done.5.far_ref = bf16[112,16,128]{2,1,0:T(8,128)(2,1)S(1)} collective-permute-done((bf16[112,16,128]{2,1,0:T(8,128)(2,1)S(1)}, bf16[112,16,128]{2,1,0:T(8,128)(2,1)S(1)}, u32[]{:S(2)}, u32[]{:S(2)}) %collective-permute-start.5) | collective-permute-done | bytes 458784 | tf_op jit(solution)/shard_map/ppermute | solution.py:455
  116.7 7.4 %mix_conv2_inner.1 = bf16[16,8,64,128]{3,2,1,0:T(8,128)(2,1)} custom-call(bf16[112,16,128]{2,1,0:T(8,128)(2,1)S(1)} %get-tuple-element.34.own_ref, bf16[112,16,128]{2,1,0:T(8,128)(2,1)S(1)} %collective-permute-done.5.far_ref, bf16[112,16,128]{2,1,0:T(8,128)(2,1)S(1)} %get-tuple-element.35.hid_ref, ...), custom_call_target="tpu_custom_call", output_to_operand_aliasing={{}: (12, {})} | custom-call | flops 2555000064 | bytes 1024 | tf_op jit(solution)/shard_map/mix_conv2_inner/pallas_call | solution.py:441
  (33 shorter events, 0.2 us)
Async XLA Ops:
  0.0 24.0 %copy-start.1 = (bf16[3,3,128,128]{3,2,1,0:T(8,128)(2,1)S(1)}, bf16[3,3,128,128]{3,2,1,0:T(8,128)(2,1)}, u32[]{:S(2)}) copy-start(bf16[3,3,128,128]{3,2,1,0:T(8,128)(2,1)} %param.11) | copy-start | bytes 884740
  0.0 24.0 %copy-start.6 = (f32[128]{0:T(128)S(1)}, f32[128]{0:T(128)}, u32[]{:S(2)}) copy-start(f32[128]{0:T(128)} %param.12) | copy-start | bytes 1540
  0.0 24.0 %copy-start.7 = (f32[128]{0:T(128)S(1)}, f32[128]{0:T(128)}, u32[]{:S(2)}) copy-start(f32[128]{0:T(128)} %param.13) | copy-start | bytes 1540
  5.2 18.8 %copy-start = (bf16[8,64,16,128]{3,2,1,0:T(8,128)(2,1)S(1)}, bf16[8,64,16,128]{3,2,1,0:T(8,128)(2,1)}, u32[]{:S(2)}) copy-start(bf16[8,64,16,128]{3,2,1,0:T(8,128)(2,1)} %get-tuple-element.32.x_ref) | copy-start | bytes 6291460
  5.2 12.2 %collective-permute-start = (bf16[8,2,16,128]{3,2,1,0:T(8,128)(2,1)}, bf16[8,2,16,128]{3,2,1,0:T(8,128)(2,1)S(1)}, u32[]{:S(2)}, u32[]{:S(2)}) collective-permute-start(bf16[8,2,16,128]{3,2,1,0:T(8,128)(2,1)} %get-tuple-element.27), channel_id=1, source_target_pairs={{0,1},{1,2},{2,3},{3,0},{4,5},{5,6},{6,7},{7,4},{8,9},{9,10},{10,1... | collective-permute-start | bytes 196616 | tf_op jit(solution)/shard_map/ppermute | solution.py:467
  7.8 9.6 %collective-permute-start.1 = (bf16[8,2,16,128]{3,2,1,0:T(8,128)(2,1)}, bf16[8,2,16,128]{3,2,1,0:T(8,128)(2,1)S(1)}, u32[]{:S(2)}, u32[]{:S(2)}) collective-permute-start(bf16[8,2,16,128]{3,2,1,0:T(8,128)(2,1)} %get-tuple-element.28), channel_id=1, source_target_pairs={{1,0},{2,1},{3,2},{0,3},{5,4},{6,5},{7,6},{4,7},{9,8},{10,9},{11,1... | collective-permute-start | bytes 196616 | tf_op jit(solution)/shard_map/ppermute | solution.py:468
  10.6 29.0 %collective-permute-start.6 = (bf16[112,16,128]{2,1,0:T(8,128)(2,1)}, bf16[112,16,128]{2,1,0:T(8,128)(2,1)S(1)}, u32[]{:S(2)}, u32[]{:S(2)}) collective-permute-start(bf16[112,16,128]{2,1,0:T(8,128)(2,1)} %get-tuple-element.37.own_ref), channel_id=1, source_target_pairs={{0,128},{128,0},{1,129},{129,1},{2,130},{130,2},{3,131},{131,3},{4... | collective-permute-start | bytes 1376264 | tf_op jit(solution)/shard_map/ppermute | solution.py:455
  17.5 11.7 %collective-permute-start.3 = (bf16[68,16,128]{2,1,0:T(8,128)(2,1)S(1)}, bf16[68,16,128]{2,1,0:T(8,128)(2,1)S(1)}, u32[]{:S(2)}, u32[]{:S(2)}) collective-permute-start(bf16[68,16,128]{2,1,0:T(8,128)(2,1)S(1)} %pad_maximum_fusion), channel_id=1, source_target_pairs={{4,0},{8,4},{12,8},{16,12},{20,16},{24,20},{28,24},{32,28},{36,32}... | collective-permute-start | bytes 835592 | tf_op jit(solution)/shard_map/ppermute | solution.py:461
  20.9 8.3 %collective-permute-start.2 = (bf16[68,16,128]{2,1,0:T(8,128)(2,1)S(1)}, bf16[68,16,128]{2,1,0:T(8,128)(2,1)S(1)}, u32[]{:S(2)}, u32[]{:S(2)}) collective-permute-start(bf16[68,16,128]{2,1,0:T(8,128)(2,1)S(1)} %pad_maximum_fusion.1), channel_id=1, source_target_pairs={{0,4},{4,8},{8,12},{12,16},{16,20},{20,24},{24,28},{28,32},{32,36}... | collective-permute-start | bytes 835592 | tf_op jit(solution)/shard_map/ppermute | solution.py:460
  29.1 10.4 %copy-start.2 = (bf16[128,128]{1,0:T(8,128)(2,1)S(1)}, bf16[128,128]{1,0:T(8,128)(2,1)}, u32[]{:S(2)}) copy-start(bf16[128,128]{1,0:T(8,128)(2,1)} %wq_ref.7) | copy-start | bytes 98308
  29.2 10.4 %copy-start.3 = (bf16[128,128]{1,0:T(8,128)(2,1)S(1)}, bf16[128,128]{1,0:T(8,128)(2,1)}, u32[]{:S(2)}) copy-start(bf16[128,128]{1,0:T(8,128)(2,1)} %wk_ref.7) | copy-start | bytes 98308
  29.2 10.4 %copy-start.4 = (bf16[128,128]{1,0:T(8,128)(2,1)S(1)}, bf16[128,128]{1,0:T(8,128)(2,1)}, u32[]{:S(2)}) copy-start(bf16[128,128]{1,0:T(8,128)(2,1)} %wv_ref.7) | copy-start | bytes 98308
  29.2 10.4 %copy-start.5 = (bf16[128,128]{1,0:T(8,128)(2,1)S(1)}, bf16[128,128]{1,0:T(8,128)(2,1)}, u32[]{:S(2)}) copy-start(bf16[128,128]{1,0:T(8,128)(2,1)} %wo_ref.7) | copy-start | bytes 98308
  29.2 10.4 %copy-start.8 = (bf16[112,16,128]{2,1,0:T(8,128)(2,1)S(1)}, bf16[112,16,128]{2,1,0:T(8,128)(2,1)}, u32[]{:S(2)}) copy-start(bf16[112,16,128]{2,1,0:T(8,128)(2,1)} %get-tuple-element.38.hid_ref) | copy-start | bytes 1376260
  29.2 10.4 %copy-start.9 = (bf16[112,16,128]{2,1,0:T(8,128)(2,1)S(1)}, bf16[112,16,128]{2,1,0:T(8,128)(2,1)}, u32[]{:S(2)}) copy-start(bf16[112,16,128]{2,1,0:T(8,128)(2,1)} %get-tuple-element.37.own_ref) | copy-start | bytes 1376260
  34.1 50.6 %collective-permute-start.4 = (bf16[192,16,128]{2,1,0:T(8,128)(2,1)S(1)}, bf16[192,16,128]{2,1,0:T(8,128)(2,1)S(1)}, u32[]{:S(2)}, u32[]{:S(2)}) collective-permute-start(bf16[192,16,128]{2,1,0:T(8,128)(2,1)S(1)} %get-tuple-element.39.own_ref), channel_id=1, source_target_pairs={{0,128},{128,0},{1,129},{129,1},{2,130},{130,2},{3,131},{131,3},{4... | collective-permute-start | bytes 2359304 | tf_op jit(solution)/shard_map/ppermute | solution.py:455
  38.3 62.6 %collective-permute-start.7 = (bf16[112,16,128]{2,1,0:T(8,128)(2,1)S(1)}, bf16[112,16,128]{2,1,0:T(8,128)(2,1)S(1)}, u32[]{:S(2)}, u32[]{:S(2)}) collective-permute-start(bf16[112,16,128]{2,1,0:T(8,128)(2,1)S(1)} %get-tuple-element.43.own_ref), channel_id=1, source_target_pairs={{0,128},{128,0},{1,129},{129,1},{2,130},{130,2},{3,131},{131,3},{4... | collective-permute-start | bytes 1376264 | tf_op jit(solution)/shard_map/ppermute | solution.py:455
  84.7 20.7 %copy-start.10 = (bf16[3,3,128,128]{3,2,1,0:T(8,128)(2,1)S(1)}, bf16[3,3,128,128]{3,2,1,0:T(8,128)(2,1)}, u32[]{:S(2)}) copy-start(bf16[3,3,128,128]{3,2,1,0:T(8,128)(2,1)} %param.18) | copy-start | bytes 884740
  84.7 20.7 %copy-start.11 = (f32[128]{0:T(128)S(1)}, f32[128]{0:T(128)}, u32[]{:S(2)}) copy-start(f32[128]{0:T(128)} %param.19) | copy-start | bytes 1540
  92.4 12.9 %collective-permute-start.8 = (bf16[66,16,128]{2,1,0:T(8,128)(2,1)S(1)}, bf16[66,16,128]{2,1,0:T(8,128)(2,1)S(1)}, u32[]{:S(2)}, u32[]{:S(2)}) collective-permute-start(bf16[66,16,128]{2,1,0:T(8,128)(2,1)S(1)} %get-tuple-element.45), channel_id=1, source_target_pairs={{0,4},{4,8},{8,12},{12,16},{16,20},{20,24},{24,28},{28,32},{32,36}... | collective-permute-start | bytes 811016 | tf_op jit(solution)/shard_map/ppermute | solution.py:460
  95.9 9.5 %collective-permute-start.9 = (bf16[66,16,128]{2,1,0:T(8,128)(2,1)S(1)}, bf16[66,16,128]{2,1,0:T(8,128)(2,1)S(1)}, u32[]{:S(2)}, u32[]{:S(2)}) collective-permute-start(bf16[66,16,128]{2,1,0:T(8,128)(2,1)S(1)} %get-tuple-element.46), channel_id=1, source_target_pairs={{4,0},{8,4},{12,8},{16,12},{20,16},{24,20},{28,24},{32,28},{36,32}... | collective-permute-start | bytes 811016 | tf_op jit(solution)/shard_map/ppermute | solution.py:461
  97.8 18.9 %collective-permute-start.5 = (bf16[112,16,128]{2,1,0:T(8,128)(2,1)S(1)}, bf16[112,16,128]{2,1,0:T(8,128)(2,1)S(1)}, u32[]{:S(2)}, u32[]{:S(2)}) collective-permute-start(bf16[112,16,128]{2,1,0:T(8,128)(2,1)S(1)} %get-tuple-element.34.own_ref), channel_id=1, source_target_pairs={{0,128},{128,0},{1,129},{129,1},{2,130},{130,2},{3,131},{131,3},{4... | collective-permute-start | bytes 1376264 | tf_op jit(solution)/shard_map/ppermute | solution.py:455

commit v3 on v2

--- a/solution.py
+++ b/solution.py
@@ -20,7 +20,7 @@
 BF = jnp.bfloat16
 F32 = jnp.float32
 WEIGHT = 0.35
-COST_SECOND, COST_MIX12, COST_MIX56, COST_OUTER = 10, 10, 1, 10
+COST_SECOND, COST_MIX12, COST_ROWS, COST_INNER, COST_UPPER = 10, 12, 7, 10, 0.1
 VMEM_LIMIT = 24 * 1024 * 1024
 FIRST_VMEM = 59 * 1024 * 1024
 
@@ -136,7 +136,8 @@
 
 
 def edge_body(
-    x_ref, above, below, left, right, w_ref, bias_ref, gain_ref, hid, norm, wide, acc, pad
+    x_ref, above, below, left, right, hid34, norm34, w_ref, bias_ref, gain_ref,
+    hid_rows, norm_rows, hid, norm, wide, acc, pad,
 ):
     pair_weights(w_ref, wide)
     pad[0] = above[...]
@@ -150,7 +151,7 @@
         acc[...] = jnp.dot(
             taps(load, range(row, row + 3), 0, WIDTH), w_ref[...], preferred_element_type=F32
         )
-        finish(acc, WIDTH, 0, bias, gain, hid, norm, k * WIDTH)
+        finish(acc, WIDTH, 0, bias, gain, hid_rows, norm_rows, k * WIDTH)
     sides = [
         taps(load, range(row, row + 4), first, SIDE)
         for row in (1, 3, 5)
@@ -160,15 +161,17 @@
     count = 3 * 2 * SIDE * MEM
     acc[0:count] = both[:, 0:CH]
     acc[count : 2 * count] = both[:, CH : 2 * CH]
-    finish(acc, 2 * 3 * 2 * SIDE, 0, bias, gain, hid, norm, 2 * WIDTH)
+    hid[0 : 2 * MID] = hid34[...]
+    norm[0 : 2 * MID] = norm34[...]
+    finish(acc, SIDES, 0, bias, gain, hid, norm, 2 * MID)
 
 
 def mix(
-    count, start, own_ref, far_ref, hid_ref, wq_ref, wk_ref, wv_ref, wo_ref, upd_ref,
+    count, own_ref, far_ref, hid_ref, wq_ref, wk_ref, wv_ref, wo_ref, upd_ref,
     q_scr, k_scr, v_scr, ctx, s_scr, p_scr,
 ):
-    own = own_ref[start : start + count].reshape(count * MEM, CH)
-    far = far_ref[start : start + count].reshape(count * MEM, CH)
+    own = own_ref[...].reshape(count * MEM, CH)
+    far = far_ref[...].reshape(count * MEM, CH)
     dot = functools.partial(jnp.dot, preferred_element_type=F32)
     points = lambda cells: cells.astype(BF).reshape(count, MEM, CH)
     both = jnp.concatenate([wk_ref[...], wv_ref[...]], axis=1)
@@ -186,12 +189,14 @@
     lane16 = lax.broadcasted_iota(jnp.int32, (MEM, CH), 1) // HEAD_DIM
     factor = 1.4426950408889634 / HEAD_DIM**0.5
     group = group_of(count)
-    steps = count // group
+    steps = -(-count // group)
+    last = count - group
+    first_of = lambda t: min(t * group, last) if isinstance(t, int) else jnp.minimum(t * group, last)
     blank = jnp.zeros((2 * MEM, CH), BF)
 
     def score(t):
         for u in range(group):
-            p = t * group + u
+            p = first_of(t) + u
             heads = jnp.concatenate([q_scr[p]] * HEADS, axis=0) * own_head
             s_scr[t % 2, u] = lax.dot_general(
                 k_scr[p], heads, (((1,), (1,)), ((), ())), preferred_element_type=F32
@@ -210,7 +215,7 @@
 
     def gather(t):
         for g in range(group // 4):
-            first = t * group + g * 4
+            first = first_of(t) + g * 4
             values = [
                 jnp.concatenate([v_scr[first + v] if w == v else blank for w in range(4)], axis=1)
                 for v in range(4)
@@ -240,12 +245,12 @@
     gather(steps - 1)
     attended = dot(ctx[...].reshape(count * MEM, CH), wo_ref[...]).astype(BF)
     upd_ref[...] = (
-        hid_ref[start : start + count].astype(F32) + attended.astype(F32).reshape(count, MEM, CH)
+        hid_ref[...].astype(F32) + attended.astype(F32).reshape(count, MEM, CH)
     ).astype(BF)
 
 
 def group_of(count):
-    return 16 if count % 16 == 0 else 8
+    return min((16, 12, 8), key=lambda group: -(-count // group) * group - count)
 
 
 def mix_scratch(count):
@@ -260,15 +265,14 @@
     ]
 
 
-def put_edge(pad, edge):
-    pad[1] = edge[0:WIDTH]
-    pad[ROWS] = edge[WIDTH : 2 * WIDTH]
-    half = 3 * 2 * SIDE
+def put_edge(pad, rows, inner):
+    pad[1] = rows[0:WIDTH]
+    pad[ROWS] = rows[WIDTH : 2 * WIDTH]
     for k in range(2):
         for i, row in enumerate((1, 3, 5)):
-            base = 2 * WIDTH + k * half + i * 2 * SIDE
-            pad[row + k + 1, 0:SIDE] = edge[base : base + SIDE]
-            pad[row + k + 1, WIDTH - SIDE : WIDTH] = edge[base + SIDE : base + 2 * SIDE]
+            base = 2 * MID + k * (SIDES // 2) + i * 2 * SIDE
+            pad[row + k + 1, 0:SIDE] = inner[base : base + SIDE]
+            pad[row + k + 1, WIDTH - SIDE : WIDTH] = inner[base + SIDE : base + 2 * SIDE]
 
 
 def second_conv(pad, row, w, bias, out_ref):
@@ -280,52 +284,51 @@
         out_ref[:, k] = jnp.swapaxes(cells.reshape(COLS, MEM, CH), 0, 1)
 
 
-def outer_body(
-    edge, upd12, upd56, top, bottom, w_ref, bias_ref, out_ref, wide, pad
-):
+def put_pair(pad, row, upd):
+    for k in range(2):
+        pad[row + k + 1, EDGE + 1 : EDGE + 1 + MID] = upd[k * MID : (k + 1) * MID]
+
+
+def upper_body(rows, upd12, upd34, above, w_ref, bias_ref, out_ref, wide, pad):
     step = pl.program_id(0)
 
     @pl.when(step == 0)
     def _():
         pair_weights(w_ref, wide)
-        pad[0] = top[...]
-        pad[ROWS + 1] = bottom[...]
-        put_edge(pad, edge)
-        for k in range(2):
-            pad[2 + k, EDGE + 1 : EDGE + 1 + MID] = upd12[k * MID : (k + 1) * MID]
-            pad[6 + k, EDGE + 1 : EDGE + 1 + MID] = upd56[k * MID : (k + 1) * MID]
+        pad[0] = above[...]
+        put_edge(pad, rows, upd34)
+        put_pair(pad, 1, upd12)
+        put_pair(pad, 3, upd34)
         second_conv(pad, 0, wide[...], bias_ref[...], out_ref)
+
+    @pl.when(step == 1)
+    def _():
+        second_conv(pad, 2, wide[...], bias_ref[...], out_ref)
+
+
+def last_body(
+    own_ref, far_ref, hid_ref, wq_ref, wk_ref, wv_ref, wo_ref,
+    rows, upd34, below, w_ref, bias_ref, _, out_ref,
+    q_scr, k_scr, v_scr, ctx, s_scr, p_scr, upd56, wide, pad,
+):
+    step = pl.program_id(0)
+
+    @pl.when(step == 0)
+    def _():
+        mix(
+            2 * MID, own_ref, far_ref, hid_ref, wq_ref, wk_ref, wv_ref, wo_ref, upd56,
+            q_scr, k_scr, v_scr, ctx, s_scr, p_scr,
+        )
+        pair_weights(w_ref, wide)
+        pad[ROWS + 1] = below[...]
+        put_edge(pad, rows, upd34)
+        put_pair(pad, 3, upd34)
+        put_pair(pad, 5, upd56)
+        second_conv(pad, 4, wide[...], bias_ref[...], out_ref)
 
     @pl.when(step == 1)
     def _():
         second_conv(pad, 6, wide[...], bias_ref[...], out_ref)
-
-
-def last_body(
-    own_ref, far_ref, hid_ref, wq_ref, wk_ref, wv_ref, wo_ref,
-    edge, upd12, upd56, w_ref, bias_ref, _, out_ref,
-    q_scr, k_scr, v_scr, ctx, s_scr, p_scr, upd34, wide, pad,
-):
-    step = pl.program_id(0)
-
-    @pl.when(step == 0)
-    def _():
-        mix(
-            2 * MID, 0, own_ref, far_ref, hid_ref, wq_ref, wk_ref, wv_ref, wo_ref, upd34,
-            q_scr, k_scr, v_scr, ctx, s_scr, p_scr,
-        )
-        pair_weights(w_ref, wide)
-        put_edge(pad, edge)
-        mid = slice(EDGE + 1, EDGE + 1 + MID)
-        for k in range(2):
-            pad[2 + k, mid] = upd12[k * MID : (k + 1) * MID]
-            pad[4 + k, mid] = upd34[k * MID : (k + 1) * MID]
-            pad[6 + k, mid] = upd56[k * MID : (k + 1) * MID]
-        second_conv(pad, 2, wide[...], bias_ref[...], out_ref)
-
-    @pl.when(step == 1)
-    def _():
-        second_conv(pad, 4, wide[...], bias_ref[...], out_ref)
 
 
 WIDE = pltpu.VMEM((12 * CH, 2 * CH), BF)
@@ -333,7 +336,8 @@
 ACC_MID = pltpu.VMEM((MID * MEM, 2 * CH), F32)
 ACC1 = pltpu.VMEM((WIDTH * MEM, CH), F32)
 PAD1 = pltpu.VMEM((ROWS + 2, COLS + 4, MEM, CH), BF)
-EDGES = 2 * WIDTH + 6 * 2 * SIDE
+SIDES = 6 * 2 * SIDE
+INNER = 2 * MID + SIDES
 
 
 def half_rows(which):
@@ -364,16 +368,16 @@
     )(ens, w, bias, gain)
 
 
-def run_edge(x, rim, w, bias, gain):
+def run_edge(x, rim, hid34, norm34, w, bias, gain):
     return call(
         edge_body,
-        (bf(EDGES, MEM, CH),) * 2,
+        (bf(2 * WIDTH, MEM, CH),) * 2 + (bf(INNER, MEM, CH),) * 2,
         [WIDE, ACC1, PAD1],
         0.1,
         "conv_edges",
-        in_specs=[VM] * 8,
-        out_specs=[VM] * 2,
-    )(x, *rim, w, bias, gain)
+        in_specs=[VM] * 10,
+        out_specs=[VM] * 4,
+    )(x, *rim, hid34, norm34, w, bias, gain)
 
 
 def run_second(x, w, bias, gain):
@@ -388,67 +392,85 @@
     )(x, w, bias, gain)
 
 
-def run_mix(count, start, micros, own, far, hid, mats):
-    return call(
-        functools.partial(mix, count, start),
+def run_mix(count, micros, own, far, hid, mats, mark=None):
+    body = functools.partial(mix, count)
+    marks = () if mark is None else (mark,)
+    return call(
+        body if mark is None else lambda _, *refs: body(*refs),
         bf(count, MEM, CH),
         mix_scratch(count),
         micros,
         f"mix{count}",
-        in_specs=[VM] * 7,
+        in_specs=[pl.BlockSpec(memory_space=pl.ANY)] * len(marks) + [VM] * 7,
         out_specs=VM,
-    )(own, far, hid, *mats)
+    )(*marks, own, far, hid, *mats)
 
 
 def mix_edges(
-    own_ref, far_ref, hid_ref, wq_ref, wk_ref, wv_ref, wo_ref, upd_ref, top, bottom, *scratch
+    _, own_ref, far_ref, hid_ref, wq_ref, wk_ref, wv_ref, wo_ref, upd_ref, top, bottom, *scratch
 ):
-    mix(EDGES, 0, own_ref, far_ref, hid_ref, wq_ref, wk_ref, wv_ref, wo_ref, upd_ref, *scratch)
+    mix(2 * WIDTH, own_ref, far_ref, hid_ref, wq_ref, wk_ref, wv_ref, wo_ref, upd_ref, *scratch)
     top[...] = upd_ref[0:WIDTH]
     bottom[...] = upd_ref[WIDTH : 2 * WIDTH]
 
 
-def run_mix_edges(own, far, hid, mats):
+def run_mix_edges(own, far, hid, mats, mark):
     return call(
         mix_edges,
-        (bf(EDGES, MEM, CH),) + (bf(WIDTH, MEM, CH),) * 2,
-        mix_scratch(EDGES),
+        (bf(2 * WIDTH, MEM, CH),) + (bf(WIDTH, MEM, CH),) * 2,
+        mix_scratch(2 * WIDTH),
+        COST_ROWS,
+        "mix_edges",
+        in_specs=[pl.BlockSpec(memory_space=pl.ANY)] + [VM] * 7,
+        out_specs=[VM] * 3,
+    )(mark, own, far, hid, *mats)
+
+
+def pass_body(cells_ref, *refs):
+    refs[-1][...] = cells_ref[...]
+
+
+def run_pass(cells, *others):
+    return call(
+        pass_body,
+        bf(*cells.shape),
+        [],
         0.1,
-        "mix_edges",
-        in_specs=[VM] * 7,
-        out_specs=[VM] * 3,
-    )(own, far, hid, *mats)
+        "pass_on",
+        in_specs=[VM] + [pl.BlockSpec(memory_space=pl.ANY)] * len(others),
+        out_specs=VM,
+    )(cells, *others)
 
 
 def row_pair(index):
     return pl.BlockSpec((MEM, 2, COLS, CH), index)
 
 
-def run_outer(edge, upd12, upd56, rim, w, bias):
-    return call(
-        outer_body,
+def run_upper(rows, upd12, upd34, above, w, bias):
+    return call(
+        upper_body,
         bf(MEM, ROWS, COLS, CH),
         [WIDE, PAD],
-        COST_OUTER,
-        "conv2_outer",
-        in_specs=[VM] * 7,
-        out_specs=row_pair(lambda i: (0, 3 * i, 0, 0)),
+        COST_UPPER,
+        "conv2_upper",
+        in_specs=[VM] * 6,
+        out_specs=row_pair(lambda i: (0, i, 0, 0)),
         grid=(2,),
-    )(edge, upd12, upd56, *rim, w, bias)
-
-
-def run_last(own, far, hid, mats, edge, upd12, upd56, w, bias, partial):
+    )(rows, upd12, upd34, above, w, bias)
+
+
+def run_last(own, far, hid, mats, rows, upd34, below, w, bias, partial):
     return call(
         last_body,
         bf(MEM, ROWS, COLS, CH),
         mix_scratch(2 * MID) + [pltpu.VMEM((2 * MID, MEM, CH), BF), WIDE, PAD],
-        7.3,
-        "mix_conv2_inner",
+        0.1,
+        "mix_conv2_lower",
         aliases={12: 0},
         in_specs=[VM] * 12 + [pl.BlockSpec(memory_space=pl.ANY)],
-        out_specs=row_pair(lambda i: (0, i + 1, 0, 0)),
+        out_specs=row_pair(lambda i: (0, i + 2, 0, 0)),
         grid=(2,),
-    )(own, far, hid, *mats, edge, upd12, upd56, w, bias, partial)
+    )(own, far, hid, *mats, rows, upd34, below, w, bias, partial)
 
 
 def swap(cells):
@@ -485,16 +507,19 @@
     row = lambda r: jnp.concatenate([left[r], x[r], right[r]], axis=0)
     above, below = lat_rims(row(0), row(ROWS - 1))
     hid34, norm34, hid56, norm56 = run_second(after(x, row(0)), w1, b1, g1)
-    hid_e, norm_e = run_edge(after(x, norm56), (above, below, left, right), w1, b1, g1)
-    far_e = swap(norm_e)
-    upd12 = run_mix(2 * MID, 0, COST_MIX12, after(norm12, norm_e), far12, hid12, mats)
-    far56 = swap(after(norm56, norm_e))
-    upd_e, row0, row7 = run_mix_edges(after(norm_e, upd12), far_e, hid_e, mats)
+    hid_r, norm_r, hid_i, norm_i = run_edge(
+        x, (above, below, left, right), hid34, norm34, w1, b1, g1
+    )
+    far_r = swap(norm_r)
+    upd12 = run_mix(2 * MID, COST_MIX12, norm12, far12, hid12, mats, norm_r)
+    sent_i = run_pass(norm_i, far_r, upd12)
+    far_i = swap(sent_i)
+    far56 = swap(run_pass(norm56, sent_i))
+    upd_r, row0, row7 = run_mix_edges(norm_r, far_r, hid_r, mats, upd12)
     above2, below2 = lat_rims(row0, row7)
-    upd56 = run_mix(2 * MID, 0, COST_MIX56, after(norm56, upd_e), far56, hid56, mats)
-    far34 = swap(after(norm34, far_e))
-    partial = run_outer(upd_e, upd12, upd56, (above2, below2), w2, b2)
-    return run_last(norm34, far34, hid34, mats, upd_e, upd12, upd56, w2, b2, partial)
+    upd_i = run_mix(INNER, COST_INNER, norm_i, far_i, hid_i, mats, upd_r)
+    partial = run_upper(upd_r, upd12, upd_i, above2, w2, b2)
+    return run_last(norm56, far56, hid56, mats, upd_r, upd_i, below2, w2, b2, partial)
 
 
 def solution(mesh):

time: 124 us -> 125 us (level)
  waiting for transfers between devices: 48.9 us -> 46.4 us
  starting transfers between devices: 31.4 us -> 33.7 us
    ppermute x4, waiting for transfers between devices: 48.9 us -> 46.4 us  [swap(): return lax.ppermute(cells, 'mem', [(0, 1), (1, 0)])]
    ppermute x4, starting transfers between devices: 14.2 us -> 15.7 us  [swap(): return lax.ppermute(cells, 'mem', [(0, 1), (1, 0)])]
    pallas_call x5 -> x7, Pallas kernels: 24.6 us -> 25.1 us  [the longest x2 11.5 us: run_mix(): call(body if mark is None else lambda _, *refs: body(*refs), bf(count, ME...]
where the time goes in v3:
time: 125 us; the launch traced here: 124 us
  waiting for transfers between devices  46.4 us (37%)
  Pallas kernels  42.9 us (34%)
  starting transfers between devices  33.7 us (27%)
    ppermute x4, waiting for transfers between devices, swap(): return lax.ppermute(cells, 'mem', [(0, 1), (1, 0)])  46.4 us
    ppermute x4, starting transfers between devices, swap(): return lax.ppermute(cells, 'mem', [(0, 1), (1, 0)])  15.7 us
    pallas_call x2, Pallas kernels, run_mix(): call(body if mark is None else lambda _, *refs: body(*refs), bf(count, ME...  11.5 us
    pallas_call x1, Pallas kernels, run_last(): call(last_body, bf(MEM, ROWS, COLS, CH), mix_scratch(2 * MID) + [pltpu.VM...  7.46 us
    ppermute x2, starting transfers between devices, lat_rims(): lax.ppermute(bottom_row, 'lat', [(i, i + 1) for i in range(count - 1)])  7.33 us
    pallas_call x1, Pallas kernels, run_mix_edges(): call(mix_edges, (bf(2 * WIDTH, MEM, CH),) + (bf(WIDTH, MEM, CH),) * 2, mi...  5.64 us
    ppermute x2, starting transfers between devices, lat_rims(): below = lax.ppermute(top_row, 'lat', [(i + 1, i) for i in range(count - 1)])  5.35 us
    pallas_call x1, Pallas kernels, run_first(): call(first_body, (bf(ROWS, COLS, MEM, CH),) + (bf(ROWS, 2, MEM, CH),) * 2...  5.2 us
  transfers between devices with their start and end apart: 10, of which 2 were waited for; matrix products, arithmetic and copies ran while one was open for 1% of the time, Pallas kernels for 24%

profile of v3, /device:TPU:1, one launch (start us, length us, event | category | flops | bytes accessed | tf_op | source)
XLA Modules:
  0.0 124.5 jit_solution(13204546369399126880)
XLA Ops:
  0.0 5.2 %conv_rows12.1 = (bf16[8,64,16,128]{3,2,1,0:T(8,128)(2,1)}, bf16[8,2,16,128]{3,2,1,0:T(8,128)(2,1)}, bf16[8,2,16,128]{3,2,1,0:T(8,128)(2,1)}, bf16[112,16,128]{2,1,0:T(8,128)(2,1)}, bf16[112,16,128]{2,1,0:T(8,128)(2,1)}) custom-call(bf16[16,8,64,128]{3,2,1,0:T(8,128)(2,1)} %ens_ref.1, bf16[1152,128]{1,0:T(8,128)(2,1)} %bitcast.17, f32[1,128]{1,0:T(1,128)} %bitcast.22, ...), custom_call_target="tpu_custom_call" | custom-call | flops 35000000 | bytes 1024 | tf_op jit(solution)/shard_map/conv_rows12/pallas_call | solution.py:349
  5.2 0.0 copy-start
  5.2 2.5 %collective-permute-start = (bf16[8,2,16,128]{3,2,1,0:T(8,128)(2,1)}, bf16[8,2,16,128]{3,2,1,0:T(8,128)(2,1)S(1)}, u32[]{:S(2)}, u32[]{:S(2)}) collective-permute-start(bf16[8,2,16,128]{3,2,1,0:T(8,128)(2,1)} %get-tuple-element.23), channel_id=1, source_target_pairs={{0,1},{1,2},{2,3},{3,0},{4,5},{5,6},{6,7},{7,4},{8,9},{9,10},{10,1... | collective-permute-start | bytes 196616 | tf_op jit(solution)/shard_map/ppermute | solution.py:489
  7.8 2.8 %collective-permute-start.1 = (bf16[8,2,16,128]{3,2,1,0:T(8,128)(2,1)}, bf16[8,2,16,128]{3,2,1,0:T(8,128)(2,1)S(1)}, u32[]{:S(2)}, u32[]{:S(2)}) collective-permute-start(bf16[8,2,16,128]{3,2,1,0:T(8,128)(2,1)} %get-tuple-element.24), channel_id=1, source_target_pairs={{1,0},{2,1},{3,2},{0,3},{5,4},{6,5},{7,6},{4,7},{9,8},{10,9},{11,1... | collective-permute-start | bytes 196616 | tf_op jit(solution)/shard_map/ppermute | solution.py:490
  10.6 5.7 %collective-permute-start.5 = (bf16[112,16,128]{2,1,0:T(8,128)(2,1)}, bf16[112,16,128]{2,1,0:T(8,128)(2,1)S(1)}, u32[]{:S(2)}, u32[]{:S(2)}) collective-permute-start(bf16[112,16,128]{2,1,0:T(8,128)(2,1)} %get-tuple-element.31.refs_0_), channel_id=1, source_target_pairs={{0,128},{128,0},{1,129},{129,1},{2,130},{130,2},{3,131},{131,3},{4... | collective-permute-start | bytes 1376264 | tf_op jit(solution)/shard_map/ppermute | solution.py:477
  16.3 1.1 slice_bitcast_fusion
  17.5 3.4 %collective-permute-start.3 = (bf16[68,16,128]{2,1,0:T(8,128)(2,1)S(1)}, bf16[68,16,128]{2,1,0:T(8,128)(2,1)S(1)}, u32[]{:S(2)}, u32[]{:S(2)}) collective-permute-start(bf16[68,16,128]{2,1,0:T(8,128)(2,1)S(1)} %pad_maximum_fusion), channel_id=1, source_target_pairs={{4,0},{8,4},{12,8},{16,12},{20,16},{24,20},{28,24},{32,28},{36,32}... | collective-permute-start | bytes 835592 | tf_op jit(solution)/shard_map/ppermute | solution.py:483
  20.9 3.0 %collective-permute-start.2 = (bf16[68,16,128]{2,1,0:T(8,128)(2,1)S(1)}, bf16[68,16,128]{2,1,0:T(8,128)(2,1)S(1)}, u32[]{:S(2)}, u32[]{:S(2)}) collective-permute-start(bf16[68,16,128]{2,1,0:T(8,128)(2,1)S(1)} %pad_maximum_fusion.1), channel_id=1, source_target_pairs={{0,4},{4,8},{8,12},{12,16},{16,20},{20,24},{24,28},{28,32},{32,36}... | collective-permute-start | bytes 835592 | tf_op jit(solution)/shard_map/ppermute | solution.py:482
  24.0 5.1 %conv_rows3456.1 = (bf16[112,16,128]{2,1,0:T(8,128)(2,1)S(1)}, bf16[112,16,128]{2,1,0:T(8,128)(2,1)S(1)}, bf16[112,16,128]{2,1,0:T(8,128)(2,1)S(1)}, bf16[112,16,128]{2,1,0:T(8,128)(2,1)S(1)}) custom-call(bf16[8,64,16,128]{3,2,1,0:T(8,128)(2,1)S(1)} %copy-done, bf16[1152,128]{1,0:T(8,128)(2,1)S(1)} %bitcast.18, f32[1,128]{1,0:T(1,128)S(1)} %bitcast.23, ...), custom_call_target="tpu_custom_call" | custom-call | flops 3500000000 | bytes 1024 | tf_op jit(solution)/shard_map/conv_rows3456/pallas_call | solution.py:384
  29.1 0.0 copy-start.3
  29.2 0.0 copy-start.4
  29.2 4.9 %conv_edges.1 = (bf16[132,16,128]{2,1,0:T(8,128)(2,1)S(1)}, bf16[132,16,128]{2,1,0:T(8,128)(2,1)S(1)}, bf16[172,16,128]{2,1,0:T(8,128)(2,1)S(1)}, bf16[172,16,128]{2,1,0:T(8,128)(2,1)S(1)}) custom-call(bf16[8,64,16,128]{3,2,1,0:T(8,128)(2,1)S(1)} %copy-done, bf16[68,16,128]{2,1,0:T(8,128)(2,1)S(1)} %collective-permute-done.2.above, ...), custom_call_target="tpu_custom_call" | custom-call | flops 35000000 | bytes 1024 | tf_op jit(solution)/shard_map/conv_edges/pallas_call | solution.py:372
  34.1 4.2 %collective-permute-start.4 = (bf16[132,16,128]{2,1,0:T(8,128)(2,1)S(1)}, bf16[132,16,128]{2,1,0:T(8,128)(2,1)S(1)}, u32[]{:S(2)}, u32[]{:S(2)}) collective-permute-start(bf16[132,16,128]{2,1,0:T(8,128)(2,1)S(1)} %get-tuple-element.30._.own_ref), channel_id=1, source_target_pairs={{0,128},{128,0},{1,129},{129,1},{2,130},{130,2},{3,131},{131,3},{4... | collective-permute-start | bytes 1622024 | tf_op jit(solution)/shard_map/ppermute | solution.py:477
  38.3 4.5 %mix112.1.refs_1_._.upd12 = bf16[112,16,128]{2,1,0:T(8,128)(2,1)S(1)} custom-call(bf16[132,16,128]{2,1,0:T(8,128)(2,1)S(1)} %get-tuple-element.30._.own_ref, bf16[112,16,128]{2,1,0:T(8,128)(2,1)S(1)} %copy-done.11, bf16[112,16,128]{2,1,0:T(8,128)(2,1)S(1)} %collective-permute-done.5.refs_1_, bf16[112,16,128]{2,1,0:T(8,128)(2,1)S(1)} %copy-done.10, ...), custom_call_target="tpu_custom_call" | custom-call | flops 4200000000 | bytes 1024 | tf_op jit(solution)/shard_map/mix112/pallas_call | solution.py:398
  42.8 21.0 %collective-permute-done.4.refs_0_.far_ref = bf16[132,16,128]{2,1,0:T(8,128)(2,1)S(1)} collective-permute-done((bf16[132,16,128]{2,1,0:T(8,128)(2,1)S(1)}, bf16[132,16,128]{2,1,0:T(8,128)(2,1)S(1)}, u32[]{:S(2)}, u32[]{:S(2)}) %collective-permute-start.4) | collective-permute-done | bytes 540704 | tf_op jit(solution)/shard_map/ppermute | solution.py:477
  63.9 3.7 %collective-permute-start.7 = (bf16[172,16,128]{2,1,0:T(8,128)(2,1)S(1)}, bf16[172,16,128]{2,1,0:T(8,128)(2,1)S(1)}, u32[]{:S(2)}, u32[]{:S(2)}) collective-permute-start(bf16[172,16,128]{2,1,0:T(8,128)(2,1)S(1)} %pass_on.2.refs_0_), channel_id=1, source_target_pairs={{0,128},{128,0},{1,129},{129,1},{2,130},{130,2},{3,131},{131,3},{4... | collective-permute-start | bytes 2113544 | tf_op jit(solution)/shard_map/ppermute | solution.py:477
  67.7 2.0 %collective-permute-start.6 = (bf16[112,16,128]{2,1,0:T(8,128)(2,1)S(1)}, bf16[112,16,128]{2,1,0:T(8,128)(2,1)S(1)}, u32[]{:S(2)}, u32[]{:S(2)}) collective-permute-start(bf16[112,16,128]{2,1,0:T(8,128)(2,1)S(1)} %pass_on.3), channel_id=1, source_target_pairs={{0,128},{128,0},{1,129},{129,1},{2,130},{130,2},{3,131},{131,3},{4... | collective-permute-start | bytes 1376264 | tf_op jit(solution)/shard_map/ppermute | solution.py:477
  69.7 5.6 %mix_edges.1 = (bf16[132,16,128]{2,1,0:T(8,128)(2,1)S(1)}, bf16[66,16,128]{2,1,0:T(8,128)(2,1)S(1)}, bf16[66,16,128]{2,1,0:T(8,128)(2,1)S(1)}) custom-call(bf16[112,16,128]{2,1,0:T(8,128)(2,1)S(1)} %mix112.1.refs_1_._.upd12, bf16[132,16,128]{2,1,0:T(8,128)(2,1)S(1)} %get-tuple-element.30._.own_ref, ...), custom_call_target="tpu_custom_call" | custom-call | flops 2449999872 | bytes 1024 | tf_op jit(solution)/shard_map/mix_edges/pallas_call | solution.py:418
  75.3 4.3 %collective-permute-start.9 = (bf16[66,16,128]{2,1,0:T(8,128)(2,1)S(1)}, bf16[66,16,128]{2,1,0:T(8,128)(2,1)S(1)}, u32[]{:S(2)}, u32[]{:S(2)}) collective-permute-start(bf16[66,16,128]{2,1,0:T(8,128)(2,1)S(1)} %get-tuple-element.38), channel_id=1, source_target_pairs={{0,4},{4,8},{8,12},{12,16},{16,20},{20,24},{24,28},{28,32},{32,36}... | collective-permute-start | bytes 811016 | tf_op jit(solution)/shard_map/ppermute | solution.py:482
  79.6 1.9 %collective-permute-start.8 = (bf16[66,16,128]{2,1,0:T(8,128)(2,1)S(1)}, bf16[66,16,128]{2,1,0:T(8,128)(2,1)S(1)}, u32[]{:S(2)}, u32[]{:S(2)}) collective-permute-start(bf16[66,16,128]{2,1,0:T(8,128)(2,1)S(1)} %get-tuple-element.37), channel_id=1, source_target_pairs={{4,0},{8,4},{12,8},{16,12},{20,16},{24,20},{28,24},{32,28},{36,32}... | collective-permute-start | bytes 811016 | tf_op jit(solution)/shard_map/ppermute | solution.py:483
  81.6 25.3 %collective-permute-done.7.refs_1_ = bf16[172,16,128]{2,1,0:T(8,128)(2,1)S(1)} collective-permute-done((bf16[172,16,128]{2,1,0:T(8,128)(2,1)S(1)}, bf16[172,16,128]{2,1,0:T(8,128)(2,1)S(1)}, u32[]{:S(2)}, u32[]{:S(2)}) %collective-permute-start.7) | collective-permute-done | bytes 704544 | tf_op jit(solution)/shard_map/ppermute | solution.py:477
  106.9 7.0 %mix172.1.upd34 = bf16[172,16,128]{2,1,0:T(8,128)(2,1)S(1)} custom-call(bf16[132,16,128]{2,1,0:T(8,128)(2,1)S(1)} %get-tuple-element.35._.rows, bf16[172,16,128]{2,1,0:T(8,128)(2,1)S(1)} %get-tuple-element.29.cells_ref.refs_0_, bf16[172,16,128]{2,1,0:T(8,128)(2,1)S(1)} %collective-permute-done.7.refs_1_, ...), custom_call_target="tpu_custom_call" | custom-call | flops 3500000000 | bytes 1024 | tf_op jit(solution)/shard_map/mix172/pallas_call | solution.py:398
  113.9 3.1 %conv2_upper.1._ = bf16[16,8,64,128]{3,2,1,0:T(8,128)(2,1)} custom-call(bf16[132,16,128]{2,1,0:T(8,128)(2,1)S(1)} %get-tuple-element.35._.rows, bf16[112,16,128]{2,1,0:T(8,128)(2,1)S(1)} %mix112.1.refs_1_._.upd12, bf16[172,16,128]{2,1,0:T(8,128)(2,1)S(1)} %mix172.1.upd34, bf16[66,16,128]{2,1,0:T(8,128)(2,1)S(1)} %collective-permute-done.9.above, ...), custom_call_target="tpu_custom_call" | custom-call | flops 35000000 | bytes 1024 | tf_op jit(solution)/shard_map/conv2_upper/pallas_call | solution.py:450
  117.0 7.5 %mix_conv2_lower.1 = bf16[16,8,64,128]{3,2,1,0:T(8,128)(2,1)} custom-call(bf16[112,16,128]{2,1,0:T(8,128)(2,1)S(1)} %get-tuple-element.26.cells_ref.own_ref, bf16[112,16,128]{2,1,0:T(8,128)(2,1)S(1)} %collective-permute-done.6.far_ref, bf16[112,16,128]{2,1,0:T(8,128)(2,1)S(1)} %get-tuple-element.33.hid_ref, ...), custom_call_target="tpu_custom_call", output_to_operand_aliasing={{}: (12, {})} | custom-call | flops 35000000 | bytes 1024 | tf_op jit(solution)/shard_map/mix_conv2_lower/pallas_call | solution.py:463
  (35 shorter events, 0.2 us)
Async XLA Ops:
  0.0 24.0 %copy-start.1 = (bf16[3,3,128,128]{3,2,1,0:T(8,128)(2,1)S(1)}, bf16[3,3,128,128]{3,2,1,0:T(8,128)(2,1)}, u32[]{:S(2)}) copy-start(bf16[3,3,128,128]{3,2,1,0:T(8,128)(2,1)} %param.11) | copy-start | bytes 884740
  0.0 24.0 %copy-start.7 = (f32[128]{0:T(128)S(1)}, f32[128]{0:T(128)}, u32[]{:S(2)}) copy-start(f32[128]{0:T(128)} %param.12) | copy-start | bytes 1540
  0.0 24.0 %copy-start.8 = (f32[128]{0:T(128)S(1)}, f32[128]{0:T(128)}, u32[]{:S(2)}) copy-start(f32[128]{0:T(128)} %param.13) | copy-start | bytes 1540
  5.2 18.8 %copy-start = (bf16[8,64,16,128]{3,2,1,0:T(8,128)(2,1)S(1)}, bf16[8,64,16,128]{3,2,1,0:T(8,128)(2,1)}, u32[]{:S(2)}) copy-start(bf16[8,64,16,128]{3,2,1,0:T(8,128)(2,1)} %get-tuple-element.25.x_ref) | copy-start | bytes 6291460
  5.2 12.2 %collective-permute-start = (bf16[8,2,16,128]{3,2,1,0:T(8,128)(2,1)}, bf16[8,2,16,128]{3,2,1,0:T(8,128)(2,1)S(1)}, u32[]{:S(2)}, u32[]{:S(2)}) collective-permute-start(bf16[8,2,16,128]{3,2,1,0:T(8,128)(2,1)} %get-tuple-element.23), channel_id=1, source_target_pairs={{0,1},{1,2},{2,3},{3,0},{4,5},{5,6},{6,7},{7,4},{8,9},{9,10},{10,1... | collective-permute-start | bytes 196616 | tf_op jit(solution)/shard_map/ppermute | solution.py:489
  7.8 9.6 %collective-permute-start.1 = (bf16[8,2,16,128]{3,2,1,0:T(8,128)(2,1)}, bf16[8,2,16,128]{3,2,1,0:T(8,128)(2,1)S(1)}, u32[]{:S(2)}, u32[]{:S(2)}) collective-permute-start(bf16[8,2,16,128]{3,2,1,0:T(8,128)(2,1)} %get-tuple-element.24), channel_id=1, source_target_pairs={{1,0},{2,1},{3,2},{0,3},{5,4},{6,5},{7,6},{4,7},{9,8},{10,9},{11,1... | collective-permute-start | bytes 196616 | tf_op jit(solution)/shard_map/ppermute | solution.py:490
  10.6 27.7 %collective-permute-start.5 = (bf16[112,16,128]{2,1,0:T(8,128)(2,1)}, bf16[112,16,128]{2,1,0:T(8,128)(2,1)S(1)}, u32[]{:S(2)}, u32[]{:S(2)}) collective-permute-start(bf16[112,16,128]{2,1,0:T(8,128)(2,1)} %get-tuple-element.31.refs_0_), channel_id=1, source_target_pairs={{0,128},{128,0},{1,129},{129,1},{2,130},{130,2},{3,131},{131,3},{4... | collective-permute-start | bytes 1376264 | tf_op jit(solution)/shard_map/ppermute | solution.py:477
  17.5 11.7 %collective-permute-start.3 = (bf16[68,16,128]{2,1,0:T(8,128)(2,1)S(1)}, bf16[68,16,128]{2,1,0:T(8,128)(2,1)S(1)}, u32[]{:S(2)}, u32[]{:S(2)}) collective-permute-start(bf16[68,16,128]{2,1,0:T(8,128)(2,1)S(1)} %pad_maximum_fusion), channel_id=1, source_target_pairs={{4,0},{8,4},{12,8},{16,12},{20,16},{24,20},{28,24},{32,28},{36,32}... | collective-permute-start | bytes 835592 | tf_op jit(solution)/shard_map/ppermute | solution.py:483
  20.9 8.3 %collective-permute-start.2 = (bf16[68,16,128]{2,1,0:T(8,128)(2,1)S(1)}, bf16[68,16,128]{2,1,0:T(8,128)(2,1)S(1)}, u32[]{:S(2)}, u32[]{:S(2)}) collective-permute-start(bf16[68,16,128]{2,1,0:T(8,128)(2,1)S(1)} %pad_maximum_fusion.1), channel_id=1, source_target_pairs={{0,4},{4,8},{8,12},{12,16},{16,20},{20,24},{24,28},{28,32},{32,36}... | collective-permute-start | bytes 835592 | tf_op jit(solution)/shard_map/ppermute | solution.py:482
  29.1 9.2 %copy-start.3 = (bf16[128,128]{1,0:T(8,128)(2,1)S(1)}, bf16[128,128]{1,0:T(8,128)(2,1)}, u32[]{:S(2)}) copy-start(bf16[128,128]{1,0:T(8,128)(2,1)} %wq_ref.3) | copy-start | bytes 98308
  29.2 9.1 %copy-start.4 = (bf16[128,128]{1,0:T(8,128)(2,1)S(1)}, bf16[128,128]{1,0:T(8,128)(2,1)}, u32[]{:S(2)}) copy-start(bf16[128,128]{1,0:T(8,128)(2,1)} %wk_ref.3) | copy-start | bytes 98308
  29.2 9.1 %copy-start.5 = (bf16[128,128]{1,0:T(8,128)(2,1)S(1)}, bf16[128,128]{1,0:T(8,128)(2,1)}, u32[]{:S(2)}) copy-start(bf16[128,128]{1,0:T(8,128)(2,1)} %wv_ref.3) | copy-start | bytes 98308
  29.2 9.1 %copy-start.6 = (bf16[128,128]{1,0:T(8,128)(2,1)S(1)}, bf16[128,128]{1,0:T(8,128)(2,1)}, u32[]{:S(2)}) copy-start(bf16[128,128]{1,0:T(8,128)(2,1)} %wo_ref.3) | copy-start | bytes 98308
  29.2 9.1 %copy-start.10 = (bf16[112,16,128]{2,1,0:T(8,128)(2,1)S(1)}, bf16[112,16,128]{2,1,0:T(8,128)(2,1)}, u32[]{:S(2)}) copy-start(bf16[112,16,128]{2,1,0:T(8,128)(2,1)} %get-tuple-element.32.refs_2_) | copy-start | bytes 1376260
  29.2 9.1 %copy-start.11 = (bf16[112,16,128]{2,1,0:T(8,128)(2,1)S(1)}, bf16[112,16,128]{2,1,0:T(8,128)(2,1)}, u32[]{:S(2)}) copy-start(bf16[112,16,128]{2,1,0:T(8,128)(2,1)} %get-tuple-element.31.refs_0_) | copy-start | bytes 1376260
  34.1 29.8 %collective-permute-start.4 = (bf16[132,16,128]{2,1,0:T(8,128)(2,1)S(1)}, bf16[132,16,128]{2,1,0:T(8,128)(2,1)S(1)}, u32[]{:S(2)}, u32[]{:S(2)}) collective-permute-start(bf16[132,16,128]{2,1,0:T(8,128)(2,1)S(1)} %get-tuple-element.30._.own_ref), channel_id=1, source_target_pairs={{0,128},{128,0},{1,129},{129,1},{2,130},{130,2},{3,131},{131,3},{4... | collective-permute-start | bytes 1622024 | tf_op jit(solution)/shard_map/ppermute | solution.py:477
  63.9 43.0 %collective-permute-start.7 = (bf16[172,16,128]{2,1,0:T(8,128)(2,1)S(1)}, bf16[172,16,128]{2,1,0:T(8,128)(2,1)S(1)}, u32[]{:S(2)}, u32[]{:S(2)}) collective-permute-start(bf16[172,16,128]{2,1,0:T(8,128)(2,1)S(1)} %pass_on.2.refs_0_), channel_id=1, source_target_pairs={{0,128},{128,0},{1,129},{129,1},{2,130},{130,2},{3,131},{131,3},{4... | collective-permute-start | bytes 2113544 | tf_op jit(solution)/shard_map/ppermute | solution.py:477
  67.7 49.3 %collective-permute-start.6 = (bf16[112,16,128]{2,1,0:T(8,128)(2,1)S(1)}, bf16[112,16,128]{2,1,0:T(8,128)(2,1)S(1)}, u32[]{:S(2)}, u32[]{:S(2)}) collective-permute-start(bf16[112,16,128]{2,1,0:T(8,128)(2,1)S(1)} %pass_on.3), channel_id=1, source_target_pairs={{0,128},{128,0},{1,129},{129,1},{2,130},{130,2},{3,131},{131,3},{4... | collective-permute-start | bytes 1376264 | tf_op jit(solution)/shard_map/ppermute | solution.py:477
  75.3 38.6 %collective-permute-start.9 = (bf16[66,16,128]{2,1,0:T(8,128)(2,1)S(1)}, bf16[66,16,128]{2,1,0:T(8,128)(2,1)S(1)}, u32[]{:S(2)}, u32[]{:S(2)}) collective-permute-start(bf16[66,16,128]{2,1,0:T(8,128)(2,1)S(1)} %get-tuple-element.38), channel_id=1, source_target_pairs={{0,4},{4,8},{8,12},{12,16},{16,20},{20,24},{24,28},{28,32},{32,36}... | collective-permute-start | bytes 811016 | tf_op jit(solution)/shard_map/ppermute | solution.py:482
  79.6 37.3 %collective-permute-start.8 = (bf16[66,16,128]{2,1,0:T(8,128)(2,1)S(1)}, bf16[66,16,128]{2,1,0:T(8,128)(2,1)S(1)}, u32[]{:S(2)}, u32[]{:S(2)}) collective-permute-start(bf16[66,16,128]{2,1,0:T(8,128)(2,1)S(1)} %get-tuple-element.37), channel_id=1, source_target_pairs={{4,0},{8,4},{12,8},{16,12},{20,16},{24,20},{28,24},{32,28},{36,32}... | collective-permute-start | bytes 811016 | tf_op jit(solution)/shard_map/ppermute | solution.py:483
  106.9 7.0 %copy-start.2 = (bf16[3,3,128,128]{3,2,1,0:T(8,128)(2,1)S(1)}, bf16[3,3,128,128]{3,2,1,0:T(8,128)(2,1)}, u32[]{:S(2)}) copy-start(bf16[3,3,128,128]{3,2,1,0:T(8,128)(2,1)} %param.18) | copy-start | bytes 884740
  106.9 7.0 %copy-start.9 = (f32[128]{0:T(128)S(1)}, f32[128]{0:T(128)}, u32[]{:S(2)}) copy-start(f32[128]{0:T(128)} %param.19) | copy-start | bytes 1540

commit v4 on v2

--- a/solution.py
+++ b/solution.py
@@ -20,7 +20,7 @@
 BF = jnp.bfloat16
 F32 = jnp.float32
 WEIGHT = 0.35
-COST_SECOND, COST_MIX12, COST_MIX56, COST_OUTER = 10, 10, 1, 10
+COST_SECOND, COST_MIX12, COST_MIX56, COST_OUTER, COST_MIX3 = 10, 10, 1, 5, 5
 VMEM_LIMIT = 24 * 1024 * 1024
 FIRST_VMEM = 59 * 1024 * 1024
 
@@ -127,12 +127,12 @@
         finish(acc, MID, k * CH, bias, gain, hid, norm, start)
 
 
-def second_body(x_ref, w_ref, bias_ref, gain_ref, hid34, norm34, hid56, norm56, wide, acc):
+def second_body(x_ref, w_ref, bias_ref, gain_ref, hid3, norm3, hid4, norm4, hid56, norm56, wide, acc):
     pair_weights(w_ref, wide)
     load = lambda r, c, n: x_ref[r, c : c + n]
     bias, gain = bias_ref[...], gain_ref[...]
-    for top, hid, norm in ((3, hid34, norm34), (5, hid56, norm56)):
-        middle(load, top, ((hid, norm, 0), (hid, norm, MID)), wide, acc, bias, gain)
+    middle(load, 3, ((hid3, norm3, 0), (hid4, norm4, 0)), wide, acc, bias, gain)
+    middle(load, 5, ((hid56, norm56, 0), (hid56, norm56, MID)), wide, acc, bias, gain)
 
 
 def edge_body(
@@ -164,11 +164,11 @@
 
 
 def mix(
-    count, start, own_ref, far_ref, hid_ref, wq_ref, wk_ref, wv_ref, wo_ref, upd_ref,
+    count, own_ref, far_ref, hid_ref, wq_ref, wk_ref, wv_ref, wo_ref, upd_ref,
     q_scr, k_scr, v_scr, ctx, s_scr, p_scr,
 ):
-    own = own_ref[start : start + count].reshape(count * MEM, CH)
-    far = far_ref[start : start + count].reshape(count * MEM, CH)
+    own = own_ref[...].reshape(count * MEM, CH)
+    far = far_ref[...].reshape(count * MEM, CH)
     dot = functools.partial(jnp.dot, preferred_element_type=F32)
     points = lambda cells: cells.astype(BF).reshape(count, MEM, CH)
     both = jnp.concatenate([wk_ref[...], wv_ref[...]], axis=1)
@@ -240,7 +240,7 @@
     gather(steps - 1)
     attended = dot(ctx[...].reshape(count * MEM, CH), wo_ref[...]).astype(BF)
     upd_ref[...] = (
-        hid_ref[start : start + count].astype(F32) + attended.astype(F32).reshape(count, MEM, CH)
+        hid_ref[...].astype(F32) + attended.astype(F32).reshape(count, MEM, CH)
     ).astype(BF)
 
 
@@ -281,13 +281,14 @@
 
 
 def outer_body(
-    edge, upd12, upd56, top, bottom, w_ref, bias_ref, out_ref, wide, pad
+    edge, upd12, upd56, top, bottom, w_ref, bias_ref, out_ref, mark, wide, pad
 ):
     step = pl.program_id(0)
 
     @pl.when(step == 0)
     def _():
         pair_weights(w_ref, wide)
+        mark[...] = jnp.zeros_like(mark)
         pad[0] = top[...]
         pad[ROWS + 1] = bottom[...]
         put_edge(pad, edge)
@@ -303,15 +304,15 @@
 
 def last_body(
     own_ref, far_ref, hid_ref, wq_ref, wk_ref, wv_ref, wo_ref,
-    edge, upd12, upd56, w_ref, bias_ref, _, out_ref,
-    q_scr, k_scr, v_scr, ctx, s_scr, p_scr, upd34, wide, pad,
+    edge, upd12, upd56, upd3, w_ref, bias_ref, _, out_ref,
+    q_scr, k_scr, v_scr, ctx, s_scr, p_scr, upd4, wide, pad,
 ):
     step = pl.program_id(0)
 
     @pl.when(step == 0)
     def _():
         mix(
-            2 * MID, 0, own_ref, far_ref, hid_ref, wq_ref, wk_ref, wv_ref, wo_ref, upd34,
+            MID, own_ref, far_ref, hid_ref, wq_ref, wk_ref, wv_ref, wo_ref, upd4,
             q_scr, k_scr, v_scr, ctx, s_scr, p_scr,
         )
         pair_weights(w_ref, wide)
@@ -319,7 +320,7 @@
         mid = slice(EDGE + 1, EDGE + 1 + MID)
         for k in range(2):
             pad[2 + k, mid] = upd12[k * MID : (k + 1) * MID]
-            pad[4 + k, mid] = upd34[k * MID : (k + 1) * MID]
+            pad[4 + k, mid] = (upd3, upd4)[k][...]
             pad[6 + k, mid] = upd56[k * MID : (k + 1) * MID]
         second_conv(pad, 2, wide[...], bias_ref[...], out_ref)
 
@@ -379,31 +380,33 @@
 def run_second(x, w, bias, gain):
     return call(
         second_body,
-        (bf(2 * MID, MEM, CH),) * 4,
+        (bf(MID, MEM, CH),) * 4 + (bf(2 * MID, MEM, CH),) * 2,
         [WIDE, ACC_MID],
         COST_SECOND,
         "conv_rows3456",
         in_specs=[VM] * 4,
-        out_specs=[VM] * 4,
+        out_specs=[VM] * 6,
     )(x, w, bias, gain)
 
 
-def run_mix(count, start, micros, own, far, hid, mats):
-    return call(
-        functools.partial(mix, count, start),
+def run_mix(count, micros, own, far, hid, mats, mark=None):
+    body = functools.partial(mix, count)
+    marks = () if mark is None else (mark,)
+    return call(
+        body if mark is None else lambda _, *refs: body(*refs),
         bf(count, MEM, CH),
         mix_scratch(count),
         micros,
         f"mix{count}",
-        in_specs=[VM] * 7,
+        in_specs=[pl.BlockSpec(memory_space=pl.ANY)] * len(marks) + [VM] * 7,
         out_specs=VM,
-    )(own, far, hid, *mats)
+    )(*marks, own, far, hid, *mats)
 
 
 def mix_edges(
     own_ref, far_ref, hid_ref, wq_ref, wk_ref, wv_ref, wo_ref, upd_ref, top, bottom, *scratch
 ):
-    mix(EDGES, 0, own_ref, far_ref, hid_ref, wq_ref, wk_ref, wv_ref, wo_ref, upd_ref, *scratch)
+    mix(EDGES, own_ref, far_ref, hid_ref, wq_ref, wk_ref, wv_ref, wo_ref, upd_ref, *scratch)
     top[...] = upd_ref[0:WIDTH]
     bottom[...] = upd_ref[WIDTH : 2 * WIDTH]
 
@@ -427,28 +430,28 @@
 def run_outer(edge, upd12, upd56, rim, w, bias):
     return call(
         outer_body,
-        bf(MEM, ROWS, COLS, CH),
+        (bf(MEM, ROWS, COLS, CH), jax.ShapeDtypeStruct((8, CH), F32)),
         [WIDE, PAD],
         COST_OUTER,
         "conv2_outer",
         in_specs=[VM] * 7,
-        out_specs=row_pair(lambda i: (0, 3 * i, 0, 0)),
+        out_specs=[row_pair(lambda i: (0, 3 * i, 0, 0)), VM],
         grid=(2,),
     )(edge, upd12, upd56, *rim, w, bias)
 
 
-def run_last(own, far, hid, mats, edge, upd12, upd56, w, bias, partial):
+def run_last(own, far, hid, mats, edge, upd12, upd56, upd3, w, bias, partial):
     return call(
         last_body,
         bf(MEM, ROWS, COLS, CH),
-        mix_scratch(2 * MID) + [pltpu.VMEM((2 * MID, MEM, CH), BF), WIDE, PAD],
+        mix_scratch(MID) + [pltpu.VMEM((MID, MEM, CH), BF), WIDE, PAD],
         7.3,
         "mix_conv2_inner",
-        aliases={12: 0},
-        in_specs=[VM] * 12 + [pl.BlockSpec(memory_space=pl.ANY)],
+        aliases={13: 0},
+        in_specs=[VM] * 13 + [pl.BlockSpec(memory_space=pl.ANY)],
         out_specs=row_pair(lambda i: (0, i + 1, 0, 0)),
         grid=(2,),
-    )(own, far, hid, *mats, edge, upd12, upd56, w, bias, partial)
+    )(own, far, hid, *mats, edge, upd12, upd56, upd3, w, bias, partial)
 
 
 def swap(cells):
@@ -484,17 +487,19 @@
     far12 = swap(norm12)
     row = lambda r: jnp.concatenate([left[r], x[r], right[r]], axis=0)
     above, below = lat_rims(row(0), row(ROWS - 1))
-    hid34, norm34, hid56, norm56 = run_second(after(x, row(0)), w1, b1, g1)
+    hid3, norm3, hid4, norm4, hid56, norm56 = run_second(after(x, row(0)), w1, b1, g1)
     hid_e, norm_e = run_edge(after(x, norm56), (above, below, left, right), w1, b1, g1)
     far_e = swap(norm_e)
-    upd12 = run_mix(2 * MID, 0, COST_MIX12, after(norm12, norm_e), far12, hid12, mats)
+    upd12 = run_mix(2 * MID, COST_MIX12, after(norm12, norm_e), far12, hid12, mats)
     far56 = swap(after(norm56, norm_e))
     upd_e, row0, row7 = run_mix_edges(after(norm_e, upd12), far_e, hid_e, mats)
     above2, below2 = lat_rims(row0, row7)
-    upd56 = run_mix(2 * MID, 0, COST_MIX56, after(norm56, upd_e), far56, hid56, mats)
-    far34 = swap(after(norm34, far_e))
-    partial = run_outer(upd_e, upd12, upd56, (above2, below2), w2, b2)
-    return run_last(norm34, far34, hid34, mats, upd_e, upd12, upd56, w2, b2, partial)
+    upd56 = run_mix(2 * MID, COST_MIX56, after(norm56, upd_e), far56, hid56, mats)
+    far3 = swap(after(norm3, far_e))
+    far4 = swap(after(norm4, far56))
+    partial, mark = run_outer(upd_e, upd12, upd56, (above2, below2), w2, b2)
+    upd3 = run_mix(MID, COST_MIX3, norm3, far3, hid3, mats, mark)
+    return run_last(norm4, far4, hid4, mats, upd_e, upd12, upd56, upd3, w2, b2, partial)
 
 
 def solution(mesh):

time: 124 us -> 123 us (level)
  waiting for transfers between devices: 48.9 us -> 43.7 us
  starting transfers between devices: 31.4 us -> 33.8 us
    ppermute x4 -> x5, waiting for transfers between devices: 48.9 us -> 43.7 us  [swap(): return lax.ppermute(cells, 'mem', [(0, 1), (1, 0)])]
    ppermute x4 -> x5, starting transfers between devices: 14.2 us -> 16.7 us  [swap(): return lax.ppermute(cells, 'mem', [(0, 1), (1, 0)])]
    pallas_call x5 -> x6, Pallas kernels: 24.6 us -> 25.5 us  [the longest x3 11.7 us: run_mix(): call(body if mark is None else lambda _, *refs: body(*refs), bf(count, ME...]
  transfers between devices with their start and end apart: 10 -> 11, of which waited for: 2 -> 3; matrix products, arithmetic and copies ran while one was open for 1% -> 1% of each run, Pallas kernels for 24% -> 27%
where the time goes in v4:
time: 123 us; the launch traced here: 122 us
  waiting for transfers between devices  43.7 us (36%)
  Pallas kernels  43.3 us (35%)
  starting transfers between devices  33.8 us (27%)
    ppermute x5, waiting for transfers between devices, swap(): return lax.ppermute(cells, 'mem', [(0, 1), (1, 0)])  43.7 us
    ppermute x5, starting transfers between devices, swap(): return lax.ppermute(cells, 'mem', [(0, 1), (1, 0)])  16.7 us
    pallas_call x3, Pallas kernels, run_mix(): call(body if mark is None else lambda _, *refs: body(*refs), bf(count, ME...  11.7 us
    pallas_call x1, Pallas kernels, run_mix_edges(): call(mix_edges, (bf(EDGES, MEM, CH),) + (bf(WIDTH, MEM, CH),) * 2, mix_sc...  7.71 us
    ppermute x2, starting transfers between devices, lat_rims(): lax.ppermute(bottom_row, 'lat', [(i, i + 1) for i in range(count - 1)])  6.49 us
    pallas_call x1, Pallas kernels, run_last(): call(last_body, bf(MEM, ROWS, COLS, CH), mix_scratch(MID) + [pltpu.VMEM((...  5.59 us
    ppermute x2, starting transfers between devices, lat_rims(): below = lax.ppermute(top_row, 'lat', [(i + 1, i) for i in range(count - 1)])  5.35 us
    pallas_call x1, Pallas kernels, run_first(): call(first_body, (bf(ROWS, COLS, MEM, CH),) + (bf(ROWS, 2, MEM, CH),) * 2...  5.21 us
  transfers between devices with their start and end apart: 11, of which 3 were waited for; matrix products, arithmetic and copies ran while one was open for 1% of the time, Pallas kernels for 27%

profile of v4, /device:TPU:1, one launch (start us, length us, event | category | flops | bytes accessed | tf_op | source)
XLA Modules:
  0.0 122.3 jit_solution(4602172446613433179)
XLA Ops:
  0.0 5.2 %conv_rows12.1 = (bf16[8,64,16,128]{3,2,1,0:T(8,128)(2,1)}, bf16[8,2,16,128]{3,2,1,0:T(8,128)(2,1)}, bf16[8,2,16,128]{3,2,1,0:T(8,128)(2,1)}, bf16[112,16,128]{2,1,0:T(8,128)(2,1)}, bf16[112,16,128]{2,1,0:T(8,128)(2,1)}) custom-call(bf16[16,8,64,128]{3,2,1,0:T(8,128)(2,1)} %ens_ref.1, bf16[1152,128]{1,0:T(8,128)(2,1)} %bitcast.17, f32[1,128]{1,0:T(1,128)} %bitcast.20, ...), custom_call_target="tpu_custom_call" | custom-call | flops 35000000 | bytes 1024 | tf_op jit(solution)/shard_map/conv_rows12/pallas_call | solution.py:346
  5.2 2.5 %collective-permute-start = (bf16[8,2,16,128]{3,2,1,0:T(8,128)(2,1)}, bf16[8,2,16,128]{3,2,1,0:T(8,128)(2,1)S(1)}, u32[]{:S(2)}, u32[]{:S(2)}) collective-permute-start(bf16[8,2,16,128]{3,2,1,0:T(8,128)(2,1)} %get-tuple-element.32), channel_id=1, source_target_pairs={{0,1},{1,2},{2,3},{3,0},{4,5},{5,6},{6,7},{7,4},{8,9},{9,10},{10,1... | collective-permute-start | bytes 196616 | tf_op jit(solution)/shard_map/ppermute | solution.py:470
  7.8 2.8 %collective-permute-start.1 = (bf16[8,2,16,128]{3,2,1,0:T(8,128)(2,1)}, bf16[8,2,16,128]{3,2,1,0:T(8,128)(2,1)S(1)}, u32[]{:S(2)}, u32[]{:S(2)}) collective-permute-start(bf16[8,2,16,128]{3,2,1,0:T(8,128)(2,1)} %get-tuple-element.33), channel_id=1, source_target_pairs={{1,0},{2,1},{3,2},{0,3},{5,4},{6,5},{7,6},{4,7},{9,8},{10,9},{11,1... | collective-permute-start | bytes 196616 | tf_op jit(solution)/shard_map/ppermute | solution.py:471
  10.6 5.7 %collective-permute-start.6 = (bf16[112,16,128]{2,1,0:T(8,128)(2,1)}, bf16[112,16,128]{2,1,0:T(8,128)(2,1)S(1)}, u32[]{:S(2)}, u32[]{:S(2)}) collective-permute-start(bf16[112,16,128]{2,1,0:T(8,128)(2,1)} %get-tuple-element.43.own_ref), channel_id=1, source_target_pairs={{0,128},{128,0},{1,129},{129,1},{2,130},{130,2},{3,131},{131,3},{4... | collective-permute-start | bytes 1376264 | tf_op jit(solution)/shard_map/ppermute | solution.py:458
  16.3 1.1 slice_bitcast_fusion
  17.5 3.4 %collective-permute-start.3 = (bf16[68,16,128]{2,1,0:T(8,128)(2,1)S(1)}, bf16[68,16,128]{2,1,0:T(8,128)(2,1)S(1)}, u32[]{:S(2)}, u32[]{:S(2)}) collective-permute-start(bf16[68,16,128]{2,1,0:T(8,128)(2,1)S(1)} %pad_maximum_fusion), channel_id=1, source_target_pairs={{4,0},{8,4},{12,8},{16,12},{20,16},{24,20},{28,24},{32,28},{36,32}... | collective-permute-start | bytes 835592 | tf_op jit(solution)/shard_map/ppermute | solution.py:464
  21.0 3.0 %collective-permute-start.2 = (bf16[68,16,128]{2,1,0:T(8,128)(2,1)S(1)}, bf16[68,16,128]{2,1,0:T(8,128)(2,1)S(1)}, u32[]{:S(2)}, u32[]{:S(2)}) collective-permute-start(bf16[68,16,128]{2,1,0:T(8,128)(2,1)S(1)} %pad_maximum_fusion.1), channel_id=1, source_target_pairs={{0,4},{4,8},{8,12},{12,16},{16,20},{20,24},{24,28},{28,32},{32,36}... | collective-permute-start | bytes 835592 | tf_op jit(solution)/shard_map/ppermute | solution.py:463
  24.0 5.1 %conv_rows3456.1 = (bf16[56,16,128]{2,1,0:T(8,128)(2,1)S(1)}, bf16[56,16,128]{2,1,0:T(8,128)(2,1)S(1)}, bf16[56,16,128]{2,1,0:T(8,128)(2,1)S(1)}, bf16[56,16,128...) custom-call(bf16[8,64,16,128]{3,2,1,0:T(8,128)(2,1)S(1)} %copy-done, ...), custom_call_target="tpu_custom_call" | custom-call | flops 3500000000 | bytes 1024 | tf_op jit(solution)/shard_map/conv_rows3456/pallas_call | solution.py:381
  29.2 4.9 %conv_edges.1 = (bf16[192,16,128]{2,1,0:T(8,128)(2,1)S(1)}, bf16[192,16,128]{2,1,0:T(8,128)(2,1)S(1)}) custom-call(bf16[8,64,16,128]{3,2,1,0:T(8,128)(2,1)S(1)} %copy-done, bf16[68,16,128]{2,1,0:T(8,128)(2,1)S(1)} %collective-permute-done.2.above, bf16[68,16,128]{2,1,0:T(8,128)(2,1)S(1)} %collective-permute-done.3.below, ...), custom_call_target="tpu_custom_call" | custom-call | flops 35000000 | bytes 1024 | tf_op jit(solution)/shard_map/conv_edges/pallas_call | solution.py:369
  34.1 4.2 %collective-permute-start.7 = (bf16[192,16,128]{2,1,0:T(8,128)(2,1)S(1)}, bf16[192,16,128]{2,1,0:T(8,128)(2,1)S(1)}, u32[]{:S(2)}, u32[]{:S(2)}) collective-permute-start(bf16[192,16,128]{2,1,0:T(8,128)(2,1)S(1)} %get-tuple-element.45.own_ref), channel_id=1, source_target_pairs={{0,128},{128,0},{1,129},{129,1},{2,130},{130,2},{3,131},{131,3},{4... | collective-permute-start | bytes 2359304 | tf_op jit(solution)/shard_map/ppermute | solution.py:458
  38.3 1.3 %collective-permute-start.4 = (bf16[112,16,128]{2,1,0:T(8,128)(2,1)S(1)}, bf16[112,16,128]{2,1,0:T(8,128)(2,1)S(1)}, u32[]{:S(2)}, u32[]{:S(2)}) collective-permute-start(bf16[112,16,128]{2,1,0:T(8,128)(2,1)S(1)} %get-tuple-element.48.own_ref), channel_id=1, source_target_pairs={{0,128},{128,0},{1,129},{129,1},{2,130},{130,2},{3,131},{131,3},{4... | collective-permute-start | bytes 1376264 | tf_op jit(solution)/shard_map/ppermute | solution.py:458
  39.6 4.5 %mix112.2.upd12 = bf16[112,16,128]{2,1,0:T(8,128)(2,1)S(1)} custom-call(bf16[112,16,128]{2,1,0:T(8,128)(2,1)S(1)} %copy-done.9, bf16[112,16,128]{2,1,0:T(8,128)(2,1)S(1)} %collective-permute-done.6.far_ref, bf16[112,16,128]{2,1,0:T(8,128)(2,1)S(1)} %copy-done.8, bf16[128,128]{1,0:T(8,128)(2,1)S(1)} %copy-done.2, bf16[128,128]{1,0:T(8,128)(2,1)S(1)} %copy-done.3, ...), custom_call_target="tpu_custom_call" | custom-call | flops 3500000000 | bytes 1024 | tf_op jit(solution)/shard_map/mix112/pallas_call | solution.py:395
  44.1 40.6 %collective-permute-done.7.far_ref = bf16[192,16,128]{2,1,0:T(8,128)(2,1)S(1)} collective-permute-done((bf16[192,16,128]{2,1,0:T(8,128)(2,1)S(1)}, bf16[192,16,128]{2,1,0:T(8,128)(2,1)S(1)}, u32[]{:S(2)}, u32[]{:S(2)}) %collective-permute-start.7) | collective-permute-done | bytes 786464 | tf_op jit(solution)/shard_map/ppermute | solution.py:458
  84.7 7.7 %mix_edges.1 = (bf16[192,16,128]{2,1,0:T(8,128)(2,1)S(1)}, bf16[66,16,128]{2,1,0:T(8,128)(2,1)S(1)}, bf16[66,16,128]{2,1,0:T(8,128)(2,1)S(1)}) custom-call(bf16[192,16,128]{2,1,0:T(8,128)(2,1)S(1)} %get-tuple-element.45.own_ref, bf16[192,16,128]{2,1,0:T(8,128)(2,1)S(1)} %collective-permute-done.7.far_ref, ...), custom_call_target="tpu_custom_call" | custom-call | flops 35000000 | bytes 1024 | tf_op jit(solution)/shard_map/mix_edges/pallas_call | solution.py:415
  92.5 3.5 %collective-permute-start.8 = (bf16[66,16,128]{2,1,0:T(8,128)(2,1)S(1)}, bf16[66,16,128]{2,1,0:T(8,128)(2,1)S(1)}, u32[]{:S(2)}, u32[]{:S(2)}) collective-permute-start(bf16[66,16,128]{2,1,0:T(8,128)(2,1)S(1)} %get-tuple-element.50), channel_id=1, source_target_pairs={{0,4},{4,8},{8,12},{12,16},{16,20},{20,24},{24,28},{28,32},{32,36}... | collective-permute-start | bytes 811016 | tf_op jit(solution)/shard_map/ppermute | solution.py:463
  95.9 1.9 %collective-permute-start.9 = (bf16[66,16,128]{2,1,0:T(8,128)(2,1)S(1)}, bf16[66,16,128]{2,1,0:T(8,128)(2,1)S(1)}, u32[]{:S(2)}, u32[]{:S(2)}) collective-permute-start(bf16[66,16,128]{2,1,0:T(8,128)(2,1)S(1)} %get-tuple-element.51), channel_id=1, source_target_pairs={{4,0},{8,4},{12,8},{16,12},{20,16},{24,20},{28,24},{32,28},{36,32}... | collective-permute-start | bytes 811016 | tf_op jit(solution)/shard_map/ppermute | solution.py:464
  97.9 3.0 %collective-permute-start.10 = (bf16[56,16,128]{2,1,0:T(8,128)(2,1)S(1)}, bf16[56,16,128]{2,1,0:T(8,128)(2,1)S(1)}, u32[]{:S(2)}, u32[]{:S(2)}) collective-permute-start(bf16[56,16,128]{2,1,0:T(8,128)(2,1)S(1)} %get-tuple-element.54.refs_0_), channel_id=1, source_target_pairs={{0,128},{128,0},{1,129},{129,1},{2,130},{130,2},{3,131},{131,3},{4... | collective-permute-start | bytes 688136 | tf_op jit(solution)/shard_map/ppermute | solution.py:458
  100.9 2.4 %collective-permute-start.5 = (bf16[56,16,128]{2,1,0:T(8,128)(2,1)S(1)}, bf16[56,16,128]{2,1,0:T(8,128)(2,1)S(1)}, u32[]{:S(2)}, u32[]{:S(2)}) collective-permute-start(bf16[56,16,128]{2,1,0:T(8,128)(2,1)S(1)} %get-tuple-element.40.own_ref), channel_id=1, source_target_pairs={{0,128},{128,0},{1,129},{129,1},{2,130},{130,2},{3,131},{131,3},{4... | collective-permute-start | bytes 688136 | tf_op jit(solution)/shard_map/ppermute | solution.py:458
  103.3 4.5 %mix112.3.upd56 = bf16[112,16,128]{2,1,0:T(8,128)(2,1)S(1)} custom-call(bf16[112,16,128]{2,1,0:T(8,128)(2,1)S(1)} %get-tuple-element.48.own_ref, bf16[112,16,128]{2,1,0:T(8,128)(2,1)S(1)} %collective-permute-done.4.far_ref, bf16[112,16,128]{2,1,0:T(8,128)(2,1)S(1)} %get-tuple-element.49.hid_ref, bf16[128,128]{1,0:T(8,128)(2,1)S(1)} %copy-done.2, ...), custom_call_target="tpu_custom_call" | custom-call | flops 350000000 | bytes 1024 | tf_op jit(solution)/shard_map/mix112/pallas_call | solution.py:395
  107.9 3.1 %conv2_outer.1 = (bf16[16,8,64,128]{3,2,1,0:T(8,128)(2,1)}, f32[8,128]{1,0:T(8,128)S(1)}) custom-call(bf16[192,16,128]{2,1,0:T(8,128)(2,1)S(1)} %get-tuple-element.47.edge, bf16[112,16,128]{2,1,0:T(8,128)(2,1)S(1)} %mix112.2.upd12, bf16[112,16,128]{2,1,0:T(8,128)(2,1)S(1)} %mix112.3.upd56, bf16[66,16,128]{2,1,0:T(8,128)(2,1)S(1)} %collective-permute-done.8.top, ...), custom_call_target="tpu_custom_call" | custom-call | flops 1750000000 | bytes 1024 | tf_op jit(solution)/shard_map/conv2_outer/pallas_call | solution.py:431
  111.0 1.1 collective-permute-done.10.refs_1_
  112.0 2.8 %mix56.1.upd3 = bf16[56,16,128]{2,1,0:T(8,128)(2,1)S(1)} custom-call(f32[8,128]{1,0:T(8,128)S(1)} %get-tuple-element.52._, bf16[56,16,128]{2,1,0:T(8,128)(2,1)S(1)} %get-tuple-element.54.refs_0_, bf16[56,16,128]{2,1,0:T(8,128)(2,1)S(1)} %collective-permute-done.10.refs_1_, bf16[56,16,128]{2,1,0:T(8,128)(2,1)S(1)} %get-tuple-element.55.refs_2_, ...), custom_call_target="tpu_custom_call" | custom-call | flops 1750000000 | bytes 1024 | tf_op jit(solution)/shard_map/mix56/pallas_call | solution.py:395
  114.8 2.0 %collective-permute-done.5.far_ref = bf16[56,16,128]{2,1,0:T(8,128)(2,1)S(1)} collective-permute-done((bf16[56,16,128]{2,1,0:T(8,128)(2,1)S(1)}, bf16[56,16,128]{2,1,0:T(8,128)(2,1)S(1)}, u32[]{:S(2)}, u32[]{:S(2)}) %collective-permute-start.5) | collective-permute-done | bytes 229408 | tf_op jit(solution)/shard_map/ppermute | solution.py:458
  116.8 5.6 %mix_conv2_inner.1 = bf16[16,8,64,128]{3,2,1,0:T(8,128)(2,1)} custom-call(bf16[56,16,128]{2,1,0:T(8,128)(2,1)S(1)} %get-tuple-element.40.own_ref, bf16[56,16,128]{2,1,0:T(8,128)(2,1)S(1)} %collective-permute-done.5.far_ref, bf16[56,16,128]{2,1,0:T(8,128)(2,1)S(1)} %get-tuple-element.41.hid_ref, ...), custom_call_target="tpu_custom_call", output_to_operand_aliasing={{}: (13, {})} | custom-call | flops 2555000064 | bytes 1024 | tf_op jit(solution)/shard_map/mix_conv2_inner/pallas_call | solution.py:444
  (36 shorter events, 0.2 us)
Async XLA Ops:
  0.0 24.0 %copy-start.1 = (bf16[3,3,128,128]{3,2,1,0:T(8,128)(2,1)S(1)}, bf16[3,3,128,128]{3,2,1,0:T(8,128)(2,1)}, u32[]{:S(2)}) copy-start(bf16[3,3,128,128]{3,2,1,0:T(8,128)(2,1)} %param.11) | copy-start | bytes 884740
  0.0 24.0 %copy-start.6 = (f32[128]{0:T(128)S(1)}, f32[128]{0:T(128)}, u32[]{:S(2)}) copy-start(f32[128]{0:T(128)} %param.12) | copy-start | bytes 1540
  0.0 24.0 %copy-start.7 = (f32[128]{0:T(128)S(1)}, f32[128]{0:T(128)}, u32[]{:S(2)}) copy-start(f32[128]{0:T(128)} %param.13) | copy-start | bytes 1540
  5.2 18.8 %copy-start = (bf16[8,64,16,128]{3,2,1,0:T(8,128)(2,1)S(1)}, bf16[8,64,16,128]{3,2,1,0:T(8,128)(2,1)}, u32[]{:S(2)}) copy-start(bf16[8,64,16,128]{3,2,1,0:T(8,128)(2,1)} %get-tuple-element.37.x_ref) | copy-start | bytes 6291460
  5.2 12.2 %collective-permute-start = (bf16[8,2,16,128]{3,2,1,0:T(8,128)(2,1)}, bf16[8,2,16,128]{3,2,1,0:T(8,128)(2,1)S(1)}, u32[]{:S(2)}, u32[]{:S(2)}) collective-permute-start(bf16[8,2,16,128]{3,2,1,0:T(8,128)(2,1)} %get-tuple-element.32), channel_id=1, source_target_pairs={{0,1},{1,2},{2,3},{3,0},{4,5},{5,6},{6,7},{7,4},{8,9},{9,10},{10,1... | collective-permute-start | bytes 196616 | tf_op jit(solution)/shard_map/ppermute | solution.py:470
  7.8 9.6 %collective-permute-start.1 = (bf16[8,2,16,128]{3,2,1,0:T(8,128)(2,1)}, bf16[8,2,16,128]{3,2,1,0:T(8,128)(2,1)S(1)}, u32[]{:S(2)}, u32[]{:S(2)}) collective-permute-start(bf16[8,2,16,128]{3,2,1,0:T(8,128)(2,1)} %get-tuple-element.33), channel_id=1, source_target_pairs={{1,0},{2,1},{3,2},{0,3},{5,4},{6,5},{7,6},{4,7},{9,8},{10,9},{11,1... | collective-permute-start | bytes 196616 | tf_op jit(solution)/shard_map/ppermute | solution.py:471
  10.6 29.0 %collective-permute-start.6 = (bf16[112,16,128]{2,1,0:T(8,128)(2,1)}, bf16[112,16,128]{2,1,0:T(8,128)(2,1)S(1)}, u32[]{:S(2)}, u32[]{:S(2)}) collective-permute-start(bf16[112,16,128]{2,1,0:T(8,128)(2,1)} %get-tuple-element.43.own_ref), channel_id=1, source_target_pairs={{0,128},{128,0},{1,129},{129,1},{2,130},{130,2},{3,131},{131,3},{4... | collective-permute-start | bytes 1376264 | tf_op jit(solution)/shard_map/ppermute | solution.py:458
  17.5 11.7 %collective-permute-start.3 = (bf16[68,16,128]{2,1,0:T(8,128)(2,1)S(1)}, bf16[68,16,128]{2,1,0:T(8,128)(2,1)S(1)}, u32[]{:S(2)}, u32[]{:S(2)}) collective-permute-start(bf16[68,16,128]{2,1,0:T(8,128)(2,1)S(1)} %pad_maximum_fusion), channel_id=1, source_target_pairs={{4,0},{8,4},{12,8},{16,12},{20,16},{24,20},{28,24},{32,28},{36,32}... | collective-permute-start | bytes 835592 | tf_op jit(solution)/shard_map/ppermute | solution.py:464
  21.0 8.3 %collective-permute-start.2 = (bf16[68,16,128]{2,1,0:T(8,128)(2,1)S(1)}, bf16[68,16,128]{2,1,0:T(8,128)(2,1)S(1)}, u32[]{:S(2)}, u32[]{:S(2)}) collective-permute-start(bf16[68,16,128]{2,1,0:T(8,128)(2,1)S(1)} %pad_maximum_fusion.1), channel_id=1, source_target_pairs={{0,4},{4,8},{8,12},{12,16},{16,20},{20,24},{24,28},{28,32},{32,36}... | collective-permute-start | bytes 835592 | tf_op jit(solution)/shard_map/ppermute | solution.py:463
  29.1 10.4 %copy-start.2 = (bf16[128,128]{1,0:T(8,128)(2,1)S(1)}, bf16[128,128]{1,0:T(8,128)(2,1)}, u32[]{:S(2)}) copy-start(bf16[128,128]{1,0:T(8,128)(2,1)} %wq_ref.7) | copy-start | bytes 98308
  29.2 10.4 %copy-start.3 = (bf16[128,128]{1,0:T(8,128)(2,1)S(1)}, bf16[128,128]{1,0:T(8,128)(2,1)}, u32[]{:S(2)}) copy-start(bf16[128,128]{1,0:T(8,128)(2,1)} %wk_ref.7) | copy-start | bytes 98308
  29.2 10.4 %copy-start.4 = (bf16[128,128]{1,0:T(8,128)(2,1)S(1)}, bf16[128,128]{1,0:T(8,128)(2,1)}, u32[]{:S(2)}) copy-start(bf16[128,128]{1,0:T(8,128)(2,1)} %wv_ref.7) | copy-start | bytes 98308
  29.2 10.4 %copy-start.5 = (bf16[128,128]{1,0:T(8,128)(2,1)S(1)}, bf16[128,128]{1,0:T(8,128)(2,1)}, u32[]{:S(2)}) copy-start(bf16[128,128]{1,0:T(8,128)(2,1)} %wo_ref.7) | copy-start | bytes 98308
  29.2 10.4 %copy-start.8 = (bf16[112,16,128]{2,1,0:T(8,128)(2,1)S(1)}, bf16[112,16,128]{2,1,0:T(8,128)(2,1)}, u32[]{:S(2)}) copy-start(bf16[112,16,128]{2,1,0:T(8,128)(2,1)} %get-tuple-element.44.hid_ref) | copy-start | bytes 1376260
  29.2 10.4 %copy-start.9 = (bf16[112,16,128]{2,1,0:T(8,128)(2,1)S(1)}, bf16[112,16,128]{2,1,0:T(8,128)(2,1)}, u32[]{:S(2)}) copy-start(bf16[112,16,128]{2,1,0:T(8,128)(2,1)} %get-tuple-element.43.own_ref) | copy-start | bytes 1376260
  34.1 50.6 %collective-permute-start.7 = (bf16[192,16,128]{2,1,0:T(8,128)(2,1)S(1)}, bf16[192,16,128]{2,1,0:T(8,128)(2,1)S(1)}, u32[]{:S(2)}, u32[]{:S(2)}) collective-permute-start(bf16[192,16,128]{2,1,0:T(8,128)(2,1)S(1)} %get-tuple-element.45.own_ref), channel_id=1, source_target_pairs={{0,128},{128,0},{1,129},{129,1},{2,130},{130,2},{3,131},{131,3},{4... | collective-permute-start | bytes 2359304 | tf_op jit(solution)/shard_map/ppermute | solution.py:458
  38.3 62.6 %collective-permute-start.4 = (bf16[112,16,128]{2,1,0:T(8,128)(2,1)S(1)}, bf16[112,16,128]{2,1,0:T(8,128)(2,1)S(1)}, u32[]{:S(2)}, u32[]{:S(2)}) collective-permute-start(bf16[112,16,128]{2,1,0:T(8,128)(2,1)S(1)} %get-tuple-element.48.own_ref), channel_id=1, source_target_pairs={{0,128},{128,0},{1,129},{129,1},{2,130},{130,2},{3,131},{131,3},{4... | collective-permute-start | bytes 1376264 | tf_op jit(solution)/shard_map/ppermute | solution.py:458
  84.7 23.1 %copy-start.10 = (bf16[3,3,128,128]{3,2,1,0:T(8,128)(2,1)S(1)}, bf16[3,3,128,128]{3,2,1,0:T(8,128)(2,1)}, u32[]{:S(2)}) copy-start(bf16[3,3,128,128]{3,2,1,0:T(8,128)(2,1)} %param.18) | copy-start | bytes 884740
  84.7 23.1 %copy-start.11 = (f32[128]{0:T(128)S(1)}, f32[128]{0:T(128)}, u32[]{:S(2)}) copy-start(f32[128]{0:T(128)} %param.19) | copy-start | bytes 1540
  92.5 15.4 %collective-permute-start.8 = (bf16[66,16,128]{2,1,0:T(8,128)(2,1)S(1)}, bf16[66,16,128]{2,1,0:T(8,128)(2,1)S(1)}, u32[]{:S(2)}, u32[]{:S(2)}) collective-permute-start(bf16[66,16,128]{2,1,0:T(8,128)(2,1)S(1)} %get-tuple-element.50), channel_id=1, source_target_pairs={{0,4},{4,8},{8,12},{12,16},{16,20},{20,24},{24,28},{28,32},{32,36}... | collective-permute-start | bytes 811016 | tf_op jit(solution)/shard_map/ppermute | solution.py:463
  95.9 11.9 %collective-permute-start.9 = (bf16[66,16,128]{2,1,0:T(8,128)(2,1)S(1)}, bf16[66,16,128]{2,1,0:T(8,128)(2,1)S(1)}, u32[]{:S(2)}, u32[]{:S(2)}) collective-permute-start(bf16[66,16,128]{2,1,0:T(8,128)(2,1)S(1)} %get-tuple-element.51), channel_id=1, source_target_pairs={{4,0},{8,4},{12,8},{16,12},{20,16},{24,20},{28,24},{32,28},{36,32}... | collective-permute-start | bytes 811016 | tf_op jit(solution)/shard_map/ppermute | solution.py:464
  97.9 14.2 %collective-permute-start.10 = (bf16[56,16,128]{2,1,0:T(8,128)(2,1)S(1)}, bf16[56,16,128]{2,1,0:T(8,128)(2,1)S(1)}, u32[]{:S(2)}, u32[]{:S(2)}) collective-permute-start(bf16[56,16,128]{2,1,0:T(8,128)(2,1)S(1)} %get-tuple-element.54.refs_0_), channel_id=1, source_target_pairs={{0,128},{128,0},{1,129},{129,1},{2,130},{130,2},{3,131},{131,3},{4... | collective-permute-start | bytes 688136 | tf_op jit(solution)/shard_map/ppermute | solution.py:458
  100.9 15.8 %collective-permute-start.5 = (bf16[56,16,128]{2,1,0:T(8,128)(2,1)S(1)}, bf16[56,16,128]{2,1,0:T(8,128)(2,1)S(1)}, u32[]{:S(2)}, u32[]{:S(2)}) collective-permute-start(bf16[56,16,128]{2,1,0:T(8,128)(2,1)S(1)} %get-tuple-element.40.own_ref), channel_id=1, source_target_pairs={{0,128},{128,0},{1,129},{129,1},{2,130},{130,2},{3,131},{131,3},{4... | collective-permute-start | bytes 688136 | tf_op jit(solution)/shard_map/ppermute | solution.py:458

commit v5 on v4

--- a/solution.py
+++ b/solution.py
@@ -245,7 +245,7 @@
 
 
 def group_of(count):
-    return 16 if count % 16 == 0 else 8
+    return 16 if count % 16 == 0 else 28 if count % 28 == 0 else 8
 
 
 def mix_scratch(count):

time: 123 us -> 122 us (level)
  Pallas kernels: 43.3 us -> 41.9 us
  transfers between devices with their start and end apart: 11 -> 11, of which waited for: 3 -> 3; matrix products, arithmetic and copies ran while one was open for 1% -> 1% of each run, Pallas kernels for 27% -> 26%
where the time goes in v5:
time: 122 us
  waiting for transfers between devices  44.3 us (36%)
  Pallas kernels  41.9 us (34%)
  starting transfers between devices  33.8 us (28%)
    ppermute x5, waiting for transfers between devices, swap(): return lax.ppermute(cells, 'mem', [(0, 1), (1, 0)])  44.3 us
    ppermute x5, starting transfers between devices, swap(): return lax.ppermute(cells, 'mem', [(0, 1), (1, 0)])  16.7 us
    pallas_call x3, Pallas kernels, run_mix(): call(body if mark is None else lambda _, *refs: body(*refs), bf(count, ME...  11.1 us
    pallas_call x1, Pallas kernels, run_mix_edges(): call(mix_edges, (bf(EDGES, MEM, CH),) + (bf(WIDTH, MEM, CH),) * 2, mix_sc...  7.71 us
    ppermute x2, starting transfers between devices, lat_rims(): lax.ppermute(bottom_row, 'lat', [(i, i + 1) for i in range(count - 1)])  6.49 us
    ppermute x2, starting transfers between devices, lat_rims(): below = lax.ppermute(top_row, 'lat', [(i + 1, i) for i in range(count - 1)])  5.35 us
    pallas_call x1, Pallas kernels, run_first(): call(first_body, (bf(ROWS, COLS, MEM, CH),) + (bf(ROWS, 2, MEM, CH),) * 2...  5.21 us
    pallas_call x1, Pallas kernels, run_second(): call(second_body, (bf(MID, MEM, CH),) * 4 + (bf(2 * MID, MEM, CH),) * 2,...  5.12 us
  transfers between devices with their start and end apart: 11, of which 3 were waited for; matrix products, arithmetic and copies ran while one was open for 1% of the time, Pallas kernels for 26%

profile of v5, /device:TPU:1, one launch (start us, length us, event | category | flops | bytes accessed | tf_op | source)
XLA Modules:
  0.0 121.5 jit_solution(14911669146291703357)
XLA Ops:
  0.0 5.2 %conv_rows12.1 = (bf16[8,64,16,128]{3,2,1,0:T(8,128)(2,1)}, bf16[8,2,16,128]{3,2,1,0:T(8,128)(2,1)}, bf16[8,2,16,128]{3,2,1,0:T(8,128)(2,1)}, bf16[112,16,128]{2,1,0:T(8,128)(2,1)}, bf16[112,16,128]{2,1,0:T(8,128)(2,1)}) custom-call(bf16[16,8,64,128]{3,2,1,0:T(8,128)(2,1)} %ens_ref.1, bf16[1152,128]{1,0:T(8,128)(2,1)} %bitcast.17, f32[1,128]{1,0:T(1,128)} %bitcast.20, ...), custom_call_target="tpu_custom_call" | custom-call | flops 35000000 | bytes 1024 | tf_op jit(solution)/shard_map/conv_rows12/pallas_call | solution.py:346
  5.2 2.5 %collective-permute-start = (bf16[8,2,16,128]{3,2,1,0:T(8,128)(2,1)}, bf16[8,2,16,128]{3,2,1,0:T(8,128)(2,1)S(1)}, u32[]{:S(2)}, u32[]{:S(2)}) collective-permute-start(bf16[8,2,16,128]{3,2,1,0:T(8,128)(2,1)} %get-tuple-element.32), channel_id=1, source_target_pairs={{0,1},{1,2},{2,3},{3,0},{4,5},{5,6},{6,7},{7,4},{8,9},{9,10},{10,1... | collective-permute-start | bytes 196616 | tf_op jit(solution)/shard_map/ppermute | solution.py:470
  7.8 2.8 %collective-permute-start.1 = (bf16[8,2,16,128]{3,2,1,0:T(8,128)(2,1)}, bf16[8,2,16,128]{3,2,1,0:T(8,128)(2,1)S(1)}, u32[]{:S(2)}, u32[]{:S(2)}) collective-permute-start(bf16[8,2,16,128]{3,2,1,0:T(8,128)(2,1)} %get-tuple-element.33), channel_id=1, source_target_pairs={{1,0},{2,1},{3,2},{0,3},{5,4},{6,5},{7,6},{4,7},{9,8},{10,9},{11,1... | collective-permute-start | bytes 196616 | tf_op jit(solution)/shard_map/ppermute | solution.py:471
  10.6 5.7 %collective-permute-start.6 = (bf16[112,16,128]{2,1,0:T(8,128)(2,1)}, bf16[112,16,128]{2,1,0:T(8,128)(2,1)S(1)}, u32[]{:S(2)}, u32[]{:S(2)}) collective-permute-start(bf16[112,16,128]{2,1,0:T(8,128)(2,1)} %get-tuple-element.43.own_ref), channel_id=1, source_target_pairs={{0,128},{128,0},{1,129},{129,1},{2,130},{130,2},{3,131},{131,3},{4... | collective-permute-start | bytes 1376264 | tf_op jit(solution)/shard_map/ppermute | solution.py:458
  16.3 1.1 slice_bitcast_fusion
  17.5 3.4 %collective-permute-start.3 = (bf16[68,16,128]{2,1,0:T(8,128)(2,1)S(1)}, bf16[68,16,128]{2,1,0:T(8,128)(2,1)S(1)}, u32[]{:S(2)}, u32[]{:S(2)}) collective-permute-start(bf16[68,16,128]{2,1,0:T(8,128)(2,1)S(1)} %pad_maximum_fusion), channel_id=1, source_target_pairs={{4,0},{8,4},{12,8},{16,12},{20,16},{24,20},{28,24},{32,28},{36,32}... | collective-permute-start | bytes 835592 | tf_op jit(solution)/shard_map/ppermute | solution.py:464
  21.0 3.0 %collective-permute-start.2 = (bf16[68,16,128]{2,1,0:T(8,128)(2,1)S(1)}, bf16[68,16,128]{2,1,0:T(8,128)(2,1)S(1)}, u32[]{:S(2)}, u32[]{:S(2)}) collective-permute-start(bf16[68,16,128]{2,1,0:T(8,128)(2,1)S(1)} %pad_maximum_fusion.1), channel_id=1, source_target_pairs={{0,4},{4,8},{8,12},{12,16},{16,20},{20,24},{24,28},{28,32},{32,36}... | collective-permute-start | bytes 835592 | tf_op jit(solution)/shard_map/ppermute | solution.py:463
  24.0 5.1 %conv_rows3456.1 = (bf16[56,16,128]{2,1,0:T(8,128)(2,1)S(1)}, bf16[56,16,128]{2,1,0:T(8,128)(2,1)S(1)}, bf16[56,16,128]{2,1,0:T(8,128)(2,1)S(1)}, bf16[56,16,128...) custom-call(bf16[8,64,16,128]{3,2,1,0:T(8,128)(2,1)S(1)} %copy-done, ...), custom_call_target="tpu_custom_call" | custom-call | flops 3500000000 | bytes 1024 | tf_op jit(solution)/shard_map/conv_rows3456/pallas_call | solution.py:381
  29.2 4.9 %conv_edges.1 = (bf16[192,16,128]{2,1,0:T(8,128)(2,1)S(1)}, bf16[192,16,128]{2,1,0:T(8,128)(2,1)S(1)}) custom-call(bf16[8,64,16,128]{3,2,1,0:T(8,128)(2,1)S(1)} %copy-done, bf16[68,16,128]{2,1,0:T(8,128)(2,1)S(1)} %collective-permute-done.2.above, bf16[68,16,128]{2,1,0:T(8,128)(2,1)S(1)} %collective-permute-done.3.below, ...), custom_call_target="tpu_custom_call" | custom-call | flops 35000000 | bytes 1024 | tf_op jit(solution)/shard_map/conv_edges/pallas_call | solution.py:369
  34.1 4.2 %collective-permute-start.7 = (bf16[192,16,128]{2,1,0:T(8,128)(2,1)S(1)}, bf16[192,16,128]{2,1,0:T(8,128)(2,1)S(1)}, u32[]{:S(2)}, u32[]{:S(2)}) collective-permute-start(bf16[192,16,128]{2,1,0:T(8,128)(2,1)S(1)} %get-tuple-element.45.own_ref), channel_id=1, source_target_pairs={{0,128},{128,0},{1,129},{129,1},{2,130},{130,2},{3,131},{131,3},{4... | collective-permute-start | bytes 2359304 | tf_op jit(solution)/shard_map/ppermute | solution.py:458
  38.3 1.3 %collective-permute-start.4 = (bf16[112,16,128]{2,1,0:T(8,128)(2,1)S(1)}, bf16[112,16,128]{2,1,0:T(8,128)(2,1)S(1)}, u32[]{:S(2)}, u32[]{:S(2)}) collective-permute-start(bf16[112,16,128]{2,1,0:T(8,128)(2,1)S(1)} %get-tuple-element.48.own_ref), channel_id=1, source_target_pairs={{0,128},{128,0},{1,129},{129,1},{2,130},{130,2},{3,131},{131,3},{4... | collective-permute-start | bytes 1376264 | tf_op jit(solution)/shard_map/ppermute | solution.py:458
  39.6 4.5 %mix112.2.upd12 = bf16[112,16,128]{2,1,0:T(8,128)(2,1)S(1)} custom-call(bf16[112,16,128]{2,1,0:T(8,128)(2,1)S(1)} %copy-done.9, bf16[112,16,128]{2,1,0:T(8,128)(2,1)S(1)} %collective-permute-done.6.far_ref, bf16[112,16,128]{2,1,0:T(8,128)(2,1)S(1)} %copy-done.8, bf16[128,128]{1,0:T(8,128)(2,1)S(1)} %copy-done.2, bf16[128,128]{1,0:T(8,128)(2,1)S(1)} %copy-done.3, ...), custom_call_target="tpu_custom_call" | custom-call | flops 3500000000 | bytes 1024 | tf_op jit(solution)/shard_map/mix112/pallas_call | solution.py:395
  44.1 40.6 %collective-permute-done.7.far_ref = bf16[192,16,128]{2,1,0:T(8,128)(2,1)S(1)} collective-permute-done((bf16[192,16,128]{2,1,0:T(8,128)(2,1)S(1)}, bf16[192,16,128]{2,1,0:T(8,128)(2,1)S(1)}, u32[]{:S(2)}, u32[]{:S(2)}) %collective-permute-start.7) | collective-permute-done | bytes 786464 | tf_op jit(solution)/shard_map/ppermute | solution.py:458
  84.7 7.7 %mix_edges.1 = (bf16[192,16,128]{2,1,0:T(8,128)(2,1)S(1)}, bf16[66,16,128]{2,1,0:T(8,128)(2,1)S(1)}, bf16[66,16,128]{2,1,0:T(8,128)(2,1)S(1)}) custom-call(bf16[192,16,128]{2,1,0:T(8,128)(2,1)S(1)} %get-tuple-element.45.own_ref, bf16[192,16,128]{2,1,0:T(8,128)(2,1)S(1)} %collective-permute-done.7.far_ref, ...), custom_call_target="tpu_custom_call" | custom-call | flops 35000000 | bytes 1024 | tf_op jit(solution)/shard_map/mix_edges/pallas_call | solution.py:415
  92.5 3.5 %collective-permute-start.8 = (bf16[66,16,128]{2,1,0:T(8,128)(2,1)S(1)}, bf16[66,16,128]{2,1,0:T(8,128)(2,1)S(1)}, u32[]{:S(2)}, u32[]{:S(2)}) collective-permute-start(bf16[66,16,128]{2,1,0:T(8,128)(2,1)S(1)} %get-tuple-element.50), channel_id=1, source_target_pairs={{0,4},{4,8},{8,12},{12,16},{16,20},{20,24},{24,28},{28,32},{32,36}... | collective-permute-start | bytes 811016 | tf_op jit(solution)/shard_map/ppermute | solution.py:463
  95.9 1.9 %collective-permute-start.9 = (bf16[66,16,128]{2,1,0:T(8,128)(2,1)S(1)}, bf16[66,16,128]{2,1,0:T(8,128)(2,1)S(1)}, u32[]{:S(2)}, u32[]{:S(2)}) collective-permute-start(bf16[66,16,128]{2,1,0:T(8,128)(2,1)S(1)} %get-tuple-element.51), channel_id=1, source_target_pairs={{4,0},{8,4},{12,8},{16,12},{20,16},{24,20},{28,24},{32,28},{36,32}... | collective-permute-start | bytes 811016 | tf_op jit(solution)/shard_map/ppermute | solution.py:464
  97.9 3.0 %collective-permute-start.10 = (bf16[56,16,128]{2,1,0:T(8,128)(2,1)S(1)}, bf16[56,16,128]{2,1,0:T(8,128)(2,1)S(1)}, u32[]{:S(2)}, u32[]{:S(2)}) collective-permute-start(bf16[56,16,128]{2,1,0:T(8,128)(2,1)S(1)} %get-tuple-element.54.refs_0_), channel_id=1, source_target_pairs={{0,128},{128,0},{1,129},{129,1},{2,130},{130,2},{3,131},{131,3},{4... | collective-permute-start | bytes 688136 | tf_op jit(solution)/shard_map/ppermute | solution.py:458
  100.9 2.4 %collective-permute-start.5 = (bf16[56,16,128]{2,1,0:T(8,128)(2,1)S(1)}, bf16[56,16,128]{2,1,0:T(8,128)(2,1)S(1)}, u32[]{:S(2)}, u32[]{:S(2)}) collective-permute-start(bf16[56,16,128]{2,1,0:T(8,128)(2,1)S(1)} %get-tuple-element.40.own_ref), channel_id=1, source_target_pairs={{0,128},{128,0},{1,129},{129,1},{2,130},{130,2},{3,131},{131,3},{4... | collective-permute-start | bytes 688136 | tf_op jit(solution)/shard_map/ppermute | solution.py:458
  103.3 4.5 %mix112.3.upd56 = bf16[112,16,128]{2,1,0:T(8,128)(2,1)S(1)} custom-call(bf16[112,16,128]{2,1,0:T(8,128)(2,1)S(1)} %get-tuple-element.48.own_ref, bf16[112,16,128]{2,1,0:T(8,128)(2,1)S(1)} %collective-permute-done.4.far_ref, bf16[112,16,128]{2,1,0:T(8,128)(2,1)S(1)} %get-tuple-element.49.hid_ref, bf16[128,128]{1,0:T(8,128)(2,1)S(1)} %copy-done.2, ...), custom_call_target="tpu_custom_call" | custom-call | flops 350000000 | bytes 1024 | tf_op jit(solution)/shard_map/mix112/pallas_call | solution.py:395
  107.9 3.1 %conv2_outer.1 = (bf16[16,8,64,128]{3,2,1,0:T(8,128)(2,1)}, f32[8,128]{1,0:T(8,128)S(1)}) custom-call(bf16[192,16,128]{2,1,0:T(8,128)(2,1)S(1)} %get-tuple-element.47.edge, bf16[112,16,128]{2,1,0:T(8,128)(2,1)S(1)} %mix112.2.upd12, bf16[112,16,128]{2,1,0:T(8,128)(2,1)S(1)} %mix112.3.upd56, bf16[66,16,128]{2,1,0:T(8,128)(2,1)S(1)} %collective-permute-done.8.top, ...), custom_call_target="tpu_custom_call" | custom-call | flops 1750000000 | bytes 1024 | tf_op jit(solution)/shard_map/conv2_outer/pallas_call | solution.py:431
  111.0 1.1 collective-permute-done.10.refs_1_
  112.0 2.1 %mix56.1.upd3 = bf16[56,16,128]{2,1,0:T(8,128)(2,1)S(1)} custom-call(f32[8,128]{1,0:T(8,128)S(1)} %get-tuple-element.52._, bf16[56,16,128]{2,1,0:T(8,128)(2,1)S(1)} %get-tuple-element.54.refs_0_, bf16[56,16,128]{2,1,0:T(8,128)(2,1)S(1)} %collective-permute-done.10.refs_1_, bf16[56,16,128]{2,1,0:T(8,128)(2,1)S(1)} %get-tuple-element.55.refs_2_, ...), custom_call_target="tpu_custom_call" | custom-call | flops 1750000000 | bytes 1024 | tf_op jit(solution)/shard_map/mix56/pallas_call | solution.py:395
  114.2 2.6 %collective-permute-done.5.far_ref = bf16[56,16,128]{2,1,0:T(8,128)(2,1)S(1)} collective-permute-done((bf16[56,16,128]{2,1,0:T(8,128)(2,1)S(1)}, bf16[56,16,128]{2,1,0:T(8,128)(2,1)S(1)}, u32[]{:S(2)}, u32[]{:S(2)}) %collective-permute-start.5) | collective-permute-done | bytes 229408 | tf_op jit(solution)/shard_map/ppermute | solution.py:458
  116.8 4.8 %mix_conv2_inner.1 = bf16[16,8,64,128]{3,2,1,0:T(8,128)(2,1)} custom-call(bf16[56,16,128]{2,1,0:T(8,128)(2,1)S(1)} %get-tuple-element.40.own_ref, bf16[56,16,128]{2,1,0:T(8,128)(2,1)S(1)} %collective-permute-done.5.far_ref, bf16[56,16,128]{2,1,0:T(8,128)(2,1)S(1)} %get-tuple-element.41.hid_ref, ...), custom_call_target="tpu_custom_call", output_to_operand_aliasing={{}: (13, {})} | custom-call | flops 2555000064 | bytes 1024 | tf_op jit(solution)/shard_map/mix_conv2_inner/pallas_call | solution.py:444
  (36 shorter events, 0.2 us)
Async XLA Ops:
  0.0 24.0 %copy-start.1 = (bf16[3,3,128,128]{3,2,1,0:T(8,128)(2,1)S(1)}, bf16[3,3,128,128]{3,2,1,0:T(8,128)(2,1)}, u32[]{:S(2)}) copy-start(bf16[3,3,128,128]{3,2,1,0:T(8,128)(2,1)} %param.11) | copy-start | bytes 884740
  0.0 24.0 %copy-start.6 = (f32[128]{0:T(128)S(1)}, f32[128]{0:T(128)}, u32[]{:S(2)}) copy-start(f32[128]{0:T(128)} %param.12) | copy-start | bytes 1540
  0.0 24.0 %copy-start.7 = (f32[128]{0:T(128)S(1)}, f32[128]{0:T(128)}, u32[]{:S(2)}) copy-start(f32[128]{0:T(128)} %param.13) | copy-start | bytes 1540
  5.2 18.8 %copy-start = (bf16[8,64,16,128]{3,2,1,0:T(8,128)(2,1)S(1)}, bf16[8,64,16,128]{3,2,1,0:T(8,128)(2,1)}, u32[]{:S(2)}) copy-start(bf16[8,64,16,128]{3,2,1,0:T(8,128)(2,1)} %get-tuple-element.37.x_ref) | copy-start | bytes 6291460
  5.2 12.2 %collective-permute-start = (bf16[8,2,16,128]{3,2,1,0:T(8,128)(2,1)}, bf16[8,2,16,128]{3,2,1,0:T(8,128)(2,1)S(1)}, u32[]{:S(2)}, u32[]{:S(2)}) collective-permute-start(bf16[8,2,16,128]{3,2,1,0:T(8,128)(2,1)} %get-tuple-element.32), channel_id=1, source_target_pairs={{0,1},{1,2},{2,3},{3,0},{4,5},{5,6},{6,7},{7,4},{8,9},{9,10},{10,1... | collective-permute-start | bytes 196616 | tf_op jit(solution)/shard_map/ppermute | solution.py:470
  7.8 9.6 %collective-permute-start.1 = (bf16[8,2,16,128]{3,2,1,0:T(8,128)(2,1)}, bf16[8,2,16,128]{3,2,1,0:T(8,128)(2,1)S(1)}, u32[]{:S(2)}, u32[]{:S(2)}) collective-permute-start(bf16[8,2,16,128]{3,2,1,0:T(8,128)(2,1)} %get-tuple-element.33), channel_id=1, source_target_pairs={{1,0},{2,1},{3,2},{0,3},{5,4},{6,5},{7,6},{4,7},{9,8},{10,9},{11,1... | collective-permute-start | bytes 196616 | tf_op jit(solution)/shard_map/ppermute | solution.py:471
  10.6 29.0 %collective-permute-start.6 = (bf16[112,16,128]{2,1,0:T(8,128)(2,1)}, bf16[112,16,128]{2,1,0:T(8,128)(2,1)S(1)}, u32[]{:S(2)}, u32[]{:S(2)}) collective-permute-start(bf16[112,16,128]{2,1,0:T(8,128)(2,1)} %get-tuple-element.43.own_ref), channel_id=1, source_target_pairs={{0,128},{128,0},{1,129},{129,1},{2,130},{130,2},{3,131},{131,3},{4... | collective-permute-start | bytes 1376264 | tf_op jit(solution)/shard_map/ppermute | solution.py:458
  17.5 11.7 %collective-permute-start.3 = (bf16[68,16,128]{2,1,0:T(8,128)(2,1)S(1)}, bf16[68,16,128]{2,1,0:T(8,128)(2,1)S(1)}, u32[]{:S(2)}, u32[]{:S(2)}) collective-permute-start(bf16[68,16,128]{2,1,0:T(8,128)(2,1)S(1)} %pad_maximum_fusion), channel_id=1, source_target_pairs={{4,0},{8,4},{12,8},{16,12},{20,16},{24,20},{28,24},{32,28},{36,32}... | collective-permute-start | bytes 835592 | tf_op jit(solution)/shard_map/ppermute | solution.py:464
  21.0 8.3 %collective-permute-start.2 = (bf16[68,16,128]{2,1,0:T(8,128)(2,1)S(1)}, bf16[68,16,128]{2,1,0:T(8,128)(2,1)S(1)}, u32[]{:S(2)}, u32[]{:S(2)}) collective-permute-start(bf16[68,16,128]{2,1,0:T(8,128)(2,1)S(1)} %pad_maximum_fusion.1), channel_id=1, source_target_pairs={{0,4},{4,8},{8,12},{12,16},{16,20},{20,24},{24,28},{28,32},{32,36}... | collective-permute-start | bytes 835592 | tf_op jit(solution)/shard_map/ppermute | solution.py:463
  29.1 10.4 %copy-start.2 = (bf16[128,128]{1,0:T(8,128)(2,1)S(1)}, bf16[128,128]{1,0:T(8,128)(2,1)}, u32[]{:S(2)}) copy-start(bf16[128,128]{1,0:T(8,128)(2,1)} %wq_ref.7) | copy-start | bytes 98308
  29.2 10.4 %copy-start.3 = (bf16[128,128]{1,0:T(8,128)(2,1)S(1)}, bf16[128,128]{1,0:T(8,128)(2,1)}, u32[]{:S(2)}) copy-start(bf16[128,128]{1,0:T(8,128)(2,1)} %wk_ref.7) | copy-start | bytes 98308
  29.2 10.4 %copy-start.4 = (bf16[128,128]{1,0:T(8,128)(2,1)S(1)}, bf16[128,128]{1,0:T(8,128)(2,1)}, u32[]{:S(2)}) copy-start(bf16[128,128]{1,0:T(8,128)(2,1)} %wv_ref.7) | copy-start | bytes 98308
  29.2 10.4 %copy-start.5 = (bf16[128,128]{1,0:T(8,128)(2,1)S(1)}, bf16[128,128]{1,0:T(8,128)(2,1)}, u32[]{:S(2)}) copy-start(bf16[128,128]{1,0:T(8,128)(2,1)} %wo_ref.7) | copy-start | bytes 98308
  29.2 10.4 %copy-start.8 = (bf16[112,16,128]{2,1,0:T(8,128)(2,1)S(1)}, bf16[112,16,128]{2,1,0:T(8,128)(2,1)}, u32[]{:S(2)}) copy-start(bf16[112,16,128]{2,1,0:T(8,128)(2,1)} %get-tuple-element.44.hid_ref) | copy-start | bytes 1376260
  29.2 10.4 %copy-start.9 = (bf16[112,16,128]{2,1,0:T(8,128)(2,1)S(1)}, bf16[112,16,128]{2,1,0:T(8,128)(2,1)}, u32[]{:S(2)}) copy-start(bf16[112,16,128]{2,1,0:T(8,128)(2,1)} %get-tuple-element.43.own_ref) | copy-start | bytes 1376260
  34.1 50.6 %collective-permute-start.7 = (bf16[192,16,128]{2,1,0:T(8,128)(2,1)S(1)}, bf16[192,16,128]{2,1,0:T(8,128)(2,1)S(1)}, u32[]{:S(2)}, u32[]{:S(2)}) collective-permute-start(bf16[192,16,128]{2,1,0:T(8,128)(2,1)S(1)} %get-tuple-element.45.own_ref), channel_id=1, source_target_pairs={{0,128},{128,0},{1,129},{129,1},{2,130},{130,2},{3,131},{131,3},{4... | collective-permute-start | bytes 2359304 | tf_op jit(solution)/shard_map/ppermute | solution.py:458
  38.3 62.6 %collective-permute-start.4 = (bf16[112,16,128]{2,1,0:T(8,128)(2,1)S(1)}, bf16[112,16,128]{2,1,0:T(8,128)(2,1)S(1)}, u32[]{:S(2)}, u32[]{:S(2)}) collective-permute-start(bf16[112,16,128]{2,1,0:T(8,128)(2,1)S(1)} %get-tuple-element.48.own_ref), channel_id=1, source_target_pairs={{0,128},{128,0},{1,129},{129,1},{2,130},{130,2},{3,131},{131,3},{4... | collective-permute-start | bytes 1376264 | tf_op jit(solution)/shard_map/ppermute | solution.py:458
  84.7 23.1 %copy-start.10 = (bf16[3,3,128,128]{3,2,1,0:T(8,128)(2,1)S(1)}, bf16[3,3,128,128]{3,2,1,0:T(8,128)(2,1)}, u32[]{:S(2)}) copy-start(bf16[3,3,128,128]{3,2,1,0:T(8,128)(2,1)} %param.18) | copy-start | bytes 884740
  84.7 23.1 %copy-start.11 = (f32[128]{0:T(128)S(1)}, f32[128]{0:T(128)}, u32[]{:S(2)}) copy-start(f32[128]{0:T(128)} %param.19) | copy-start | bytes 1540
  92.5 15.4 %collective-permute-start.8 = (bf16[66,16,128]{2,1,0:T(8,128)(2,1)S(1)}, bf16[66,16,128]{2,1,0:T(8,128)(2,1)S(1)}, u32[]{:S(2)}, u32[]{:S(2)}) collective-permute-start(bf16[66,16,128]{2,1,0:T(8,128)(2,1)S(1)} %get-tuple-element.50), channel_id=1, source_target_pairs={{0,4},{4,8},{8,12},{12,16},{16,20},{20,24},{24,28},{28,32},{32,36}... | collective-permute-start | bytes 811016 | tf_op jit(solution)/shard_map/ppermute | solution.py:463
  95.9 11.9 %collective-permute-start.9 = (bf16[66,16,128]{2,1,0:T(8,128)(2,1)S(1)}, bf16[66,16,128]{2,1,0:T(8,128)(2,1)S(1)}, u32[]{:S(2)}, u32[]{:S(2)}) collective-permute-start(bf16[66,16,128]{2,1,0:T(8,128)(2,1)S(1)} %get-tuple-element.51), channel_id=1, source_target_pairs={{4,0},{8,4},{12,8},{16,12},{20,16},{24,20},{28,24},{32,28},{36,32}... | collective-permute-start | bytes 811016 | tf_op jit(solution)/shard_map/ppermute | solution.py:464
  97.9 14.2 %collective-permute-start.10 = (bf16[56,16,128]{2,1,0:T(8,128)(2,1)S(1)}, bf16[56,16,128]{2,1,0:T(8,128)(2,1)S(1)}, u32[]{:S(2)}, u32[]{:S(2)}) collective-permute-start(bf16[56,16,128]{2,1,0:T(8,128)(2,1)S(1)} %get-tuple-element.54.refs_0_), channel_id=1, source_target_pairs={{0,128},{128,0},{1,129},{129,1},{2,130},{130,2},{3,131},{131,3},{4... | collective-permute-start | bytes 688136 | tf_op jit(solution)/shard_map/ppermute | solution.py:458
  100.9 15.8 %collective-permute-start.5 = (bf16[56,16,128]{2,1,0:T(8,128)(2,1)S(1)}, bf16[56,16,128]{2,1,0:T(8,128)(2,1)S(1)}, u32[]{:S(2)}, u32[]{:S(2)}) collective-permute-start(bf16[56,16,128]{2,1,0:T(8,128)(2,1)S(1)} %get-tuple-element.40.own_ref), channel_id=1, source_target_pairs={{0,128},{128,0},{1,129},{129,1},{2,130},{130,2},{3,131},{131,3},{4... | collective-permute-start | bytes 688136 | tf_op jit(solution)/shard_map/ppermute | solution.py:458
